TPU v7x, 32 devices: a whole 2x2x4 slice. The times are simulated.
32 devices in a mesh: row: 8 (over z, x), col: 4 (over y, core).
Axes of the slice: x: 2, y: 2, z: 4, core: 2. Of those that a mesh axis runs over, the one named last changes fastest.
Arguments:
- interaction: bfloat16 [5, 8192, 8192], P(None, 'row', 'col'), may hold values from -0.0390625 to 0.0390625
- history_currents: bfloat16 [4, 8192, 512], P(None, ('col', 'row')), may hold values from -5 to 5
- incident: float32 [2, 8192, 512], P(None, ('row', 'col')), may hold values from -4 to 4
- load_gain: float32 [8192], P('row'), may hold values from 0.5 to 1.5
- load_cubic: float32 [8192], P('row'), may hold values from 0.005 to 0.04
- delays: int32 [8, 4, 5], P('row', 'col'), may hold values from 1 to 4
- tile_map: int32 [8, 4], P('row', 'col'), may hold values 0 or 1
Outputs:
- currents: bfloat16 [2, 8192, 512], P(None, ('row', 'col'))
Inputs may be any that keep to these rules, and one draw needn't show every extreme that they name: Slot k of tile (r, c) reads the current of delays[r, c, k] steps before the marched step.
All inputs are finite; a program needn't handle non-finite values. No bound on the sum of `tile_map` on one device may be relied on, other than what follows from the above.
Results may differ from a plain program's by a relative error of at most 0.0024.
Values may be sent and summed in bfloat16 or wider, within the bound.
No kernel may reach another device: no remote copies, remote signals or barrier semaphores. Data moves between devices by JAX's collectives and lax.ppermute only.
A program may use at most 128 MiB of HBM per device.

v0:
```python
import functools

import jax
import jax.numpy as jnp
from jax import lax
from jax.experimental import pallas as pl
from jax.experimental.pallas import tpu as pltpu
from jax.sharding import PartitionSpec as P

BOTH = ("row", "col")
VMEM_BYTES = 8 * 1024 * 1024
TILE = 16
ROWS = 256
SHORT = pl.CostEstimate(flops=0, bytes_accessed=0, transcendentals=0)
LANES = 128
LEVELS = 32000.0
IN_VMEM = pl.BlockSpec(memory_space=pltpu.VMEM)
IN_SMEM = pl.BlockSpec(memory_space=pltpu.SMEM)


def split_waves(waves):
    unit = 128
    if waves % unit or waves < 2 * unit:
        return [(0, waves)]
    half = (waves // unit + 1) // 2 * unit
    return [(0, half), (half, waves)]


def whereabouts(fanout):
    row = lax.axis_index("row")
    return lax.div(row, fanout), lax.rem(row, fanout), lax.axis_index("col")


def cycle_row(layers, fanout, place):
    lane, along = lax.div(place, layers), lax.rem(place, layers)
    return jnp.where(lax.rem(lane, 2) == 0, along, layers - 1 - along) * fanout + lane


def cycle_place(layers, layer, lane):
    return lane * layers + jnp.where(lax.rem(lane, 2) == 0, layer, layers - 1 - layer)


def first_kernel(matrix, gain, cubic, mark, own_gain, own_cubic, held):
    mark[...] = matrix[0, :8, :128].astype(jnp.float32)
    share = own_gain.shape[0]
    own = pl.ds(pl.multiple_of(lax.axis_index("col") * share, share), share)
    for source, out in ((gain, own_gain), (cubic, own_cubic)):
        for number in range(source.shape[0]):
            line = jnp.broadcast_to(source[number : number + 1, :], (LANES, LANES))
            held[number * LANES : (number + 1) * LANES, :] = jnp.transpose(line)
        out[...] = held[own, :]


def first_call(matrix, gain, cubic, share):
    rows = matrix.shape[1]
    lines = (rows // LANES, LANES)
    return pl.pallas_call(
        first_kernel,
        out_shape=[jax.ShapeDtypeStruct((8, LANES), jnp.float32)]
        + [jax.ShapeDtypeStruct((share, LANES), jnp.float32)] * 2,
        in_specs=[IN_VMEM] * 3,
        out_specs=[IN_VMEM] * 3,
        scratch_shapes=[pltpu.VMEM((rows, LANES), jnp.float32)],
        compiler_params=pltpu.CompilerParams(vmem_limit_bytes=VMEM_BYTES),
        cost_estimate=SHORT,
    )(matrix, gain.reshape(lines), cubic.reshape(lines))


def past_kernel(number, opening, steps, layers, fanout, delays, tile, matrix, front, back, mark, *refs):
    refs = list(refs)
    carried = None if opening else refs.pop(0)
    incident = refs.pop(0) if len(steps) == 1 else None
    slots = matrix.shape[0]
    depth, half, waves = front.shape
    layer, lane, col = whereabouts(fanout)
    count = matrix.shape[2] // (2 * half)
    here = cycle_place(layers, layer, lane)
    right, columns = [], []
    for side, piece in enumerate((front, back)):
        if count == 1:
            place = side
        else:
            walked = lax.rem(here + (number if side else count - number), count)
            place = 2 * cycle_row(layers, fanout, walked) + side
        columns.append(pl.ds(pl.multiple_of(place * half, half), half))
        for slot in range(slots):
            delay = delays[slot]
            parts = []
            if 0 in steps:
                parts.append(piece[depth - delay])
            if 1 in steps:
                later = piece[jnp.minimum(depth + 1 - delay, depth - 1)]
                parts.append(jnp.where(delay >= 2, later, jnp.zeros_like(later)))
            right.append(jnp.concatenate(parts, axis=1))
    right = jnp.concatenate(right, axis=0)
    span = slice(None) if len(steps) == 2 else slice(steps[0] * waves, (steps[0] + 1) * waves)
    total = refs[-1] if steps == (0,) else refs[0]
    weight = 1.0 if len(steps) == 2 else -tile[0].astype(jnp.float32)

    def some_rows(turn, _):
        rows = pl.ds(pl.multiple_of(turn * ROWS, ROWS), ROWS)
        left = jnp.concatenate([matrix[slot, rows, line] for line in columns for slot in range(slots)], axis=1)
        added = jnp.dot(left, right, preferred_element_type=jnp.float32)
        if not opening:
            added = added + carried[rows, span]
        total[rows, :] = added if len(steps) == 2 else weight * added
        return 0

    lax.fori_loop(0, matrix.shape[1] // ROWS, some_rows, 0)
    if len(steps) == 2:
        refs[1][...] = jnp.zeros_like(refs[1])
        return
    share = incident.shape[1]
    if steps[0]:
        total[pl.ds(pl.multiple_of(col * share, share), share), :] += incident[1]
        return
    kept, sent, held = refs
    bit = lax.rem(col, 2)
    for pair in range(kept.shape[0]):
        for out, which in ((kept, bit), (sent, 1 - bit)):
            rows = pl.ds(pl.multiple_of((2 * pair + which) * share, share), share)
            out[pair] = held[rows, :]
    kept[lax.div(col, 2)] += incident[0]


def past_call(delays, tile, matrix, pieces, mark, carried, incident, number, steps, layers, fanout):
    slots, rows, _ = matrix.shape
    _, half, waves = pieces[0].shape
    totals = jax.ShapeDtypeStruct((rows, 2 * waves), jnp.float32)
    operands = [delays, tile, matrix, *pieces, mark]
    aliases, scratch = {}, []
    if carried is not None:
        operands.append(carried)
    if len(steps) == 2:
        ends = [totals, jax.ShapeDtypeStruct((8, LANES), jnp.float32)]
        aliases = {} if carried is None else {6: 0}
    else:
        operands.append(incident)
        share = incident.shape[1]
        if steps[0]:
            ends = [jax.ShapeDtypeStruct((rows, waves), jnp.float32)]
        else:
            ends = [jax.ShapeDtypeStruct((rows // share // 2, share, waves), jnp.float32)] * 2
            scratch = [pltpu.VMEM((rows, waves), jnp.float32)]
    return pl.pallas_call(
        functools.partial(past_kernel, number, carried is None, steps, layers, fanout),
        out_shape=ends,
        in_specs=[IN_SMEM] * 2 + [IN_VMEM] * (len(operands) - 2),
        out_specs=[IN_VMEM] * len(ends),
        scratch_shapes=scratch,
        input_output_aliases=aliases,
        compiler_params=pltpu.CompilerParams(vmem_limit_bytes=VMEM_BYTES),
        cost_estimate=pl.CostEstimate(
            flops=4 * slots * rows * half * waves * len(steps),
            bytes_accessed=4 * slots * rows * half,
            transcendentals=0,
        ),
    )(*operands)


def small_call(kernel, shapes, matrix, *operands):
    return pl.pallas_call(
        kernel,
        out_shape=shapes,
        in_specs=[IN_VMEM] * (1 + len(operands)),
        out_specs=[IN_VMEM] * len(shapes),
        compiler_params=pltpu.CompilerParams(vmem_limit_bytes=VMEM_BYTES),
        cost_estimate=SHORT,
    )(matrix, *operands)


def fold_kernel(bit, last, matrix, kept, got, kept_out, sent_out):
    own = lax.rem(lax.div(lax.axis_index("col"), bit), 2)
    for pair in range(kept_out.shape[0]):
        kept_out[pair] = kept[2 * pair + own] + got[2 * pair + own]
        sent = kept[2 * pair + 1 - own] + got[2 * pair + 1 - own]
        if not last:
            sent_out[pair] = sent
            continue
        rows = sent.shape[0]
        peak = jnp.maximum(jnp.max(jnp.abs(sent), axis=0, keepdims=True), 1e-30)
        power = jnp.ceil(jnp.log2(peak))
        coded = jnp.round(sent * (jnp.exp2(-power) * LEVELS))
        sent_out[:rows] = coded.astype(jnp.int32).astype(jnp.int16)
        sent_out[rows:] = jnp.broadcast_to(power, (TILE, sent.shape[1])).astype(jnp.int32).astype(jnp.int16)


def fold_call(matrix, kept, got, bit, last):
    pairs, (share, waves) = kept.shape[0] // 2, kept.shape[1:]
    shapes = [jax.ShapeDtypeStruct((pairs, share, waves), jnp.float32)]
    if last:
        shapes.append(jax.ShapeDtypeStruct((share + TILE, waves), jnp.int16))
    else:
        shapes.append(shapes[0])
    return small_call(functools.partial(fold_kernel, bit, last), shapes, matrix, kept, got)


def load_kernel(matrix, kept, got, gain, cubic, out):
    share, waves = out.shape
    gain, cubic = (jnp.concatenate([ref[...]] * (waves // LANES), axis=1) for ref in (gain, cubic))
    power = got[share:].astype(jnp.int32).astype(jnp.float32)[:1]
    field = kept[0] + got[:share].astype(jnp.int32).astype(jnp.float32) * (jnp.exp2(power) * (1.0 / LEVELS))
    out[...] = (gain * field - cubic * field * field * field).astype(jnp.bfloat16)


def load_call(matrix, kept, got, gain, cubic):
    shapes = [jax.ShapeDtypeStruct(kept.shape[1:], jnp.bfloat16)]
    return small_call(load_kernel, shapes, matrix, kept, got, gain, cubic)[0]


def arrange_kernel(layers, fanout, matrix, *refs):
    layer, _, col = whereabouts(fanout)
    apart = layer ^ col
    for place in range(layers):
        @pl.when(apart == place)
        def _():
            for other in range(layers):
                refs[layers + other][...] = refs[place ^ other][...]


def arrange_call(matrix, values, fanout):
    shapes = [jax.ShapeDtypeStruct(value.shape, value.dtype) for value in values]
    return small_call(functools.partial(arrange_kernel, len(values), fanout), shapes, matrix, *values)


def recent_kernel(fanout, beside, ending, pieces, delays, tile, matrix, *refs):
    sources, base, refs = refs[:pieces], refs[pieces], list(refs[pieces + 1 :])
    outs = [refs.pop(0) for _ in range(2 if ending else 1)]
    total, held = refs
    slots = matrix.shape[0]
    _, lane, col = whereabouts(fanout)
    depth, share = held.shape[0], sources[0].shape[0]
    for other, source in enumerate(sources):
        held[pl.ds(pl.multiple_of((col ^ other) * share, share), share), :] = source[...]
    lane = lax.rem(lane + beside, fanout)
    columns = pl.ds(pl.multiple_of(lane * depth, depth), depth)
    total[...] = jnp.zeros_like(total)

    def some_slot(slot, _):
        @pl.when(delays[slot] == 1)
        def _():
            total[...] += jnp.dot(matrix[slot, :, columns], held[...], preferred_element_type=jnp.float32)

        return 0

    lax.fori_loop(0, slots, some_slot, 0)
    weight = -tile[0].astype(jnp.float32)
    if not ending:
        outs[0][...] = base[...] + weight * total[...]
        return
    bit = lax.rem(col, 2)
    for pair in range(outs[0].shape[0]):
        for out, own in ((outs[0], bit), (outs[1], 1 - bit)):
            rows = pl.ds(pl.multiple_of((2 * pair + own) * share, share), share)
            out[pair] = base[rows, :] + weight * total[rows, :]


def recent_call(delays, tile, matrix, sources, base, beside, fanout, cols_count):
    slots, rows, depth = matrix.shape
    waves = base.shape[1]
    depth = depth // fanout
    ending = beside == fanout - 1
    if ending:
        ends = [jax.ShapeDtypeStruct((cols_count // 2, rows // cols_count, waves), jnp.float32)] * 2
    else:
        ends = [jax.ShapeDtypeStruct(base.shape, jnp.float32)]
    return pl.pallas_call(
        functools.partial(recent_kernel, fanout, beside, ending, len(sources)),
        out_shape=ends,
        in_specs=[IN_SMEM] * 2 + [IN_VMEM] * (len(sources) + 2),
        out_specs=[IN_VMEM] * len(ends),
        scratch_shapes=[pltpu.VMEM((rows, waves), jnp.float32), pltpu.VMEM((depth, waves), jnp.bfloat16)],
        compiler_params=pltpu.CompilerParams(vmem_limit_bytes=VMEM_BYTES),
        cost_estimate=SHORT,
    )(delays, tile, matrix, *sources, base)


def per_device(rows_count, cols_count, interaction, history, incident, load_gain, load_cubic, delays, tile_map):
    fanout = rows_count // cols_count
    layers = cols_count
    share = incident.shape[1]
    delay, tile = delays.reshape(-1), tile_map.reshape(-1)
    bits = [1 << bit for bit in range((cols_count - 1).bit_length())]

    def send(value, target):
        pairs = []
        for row in range(rows_count):
            for col in range(cols_count):
                goal = target(row // fanout, row % fanout, col)
                if goal is not None:
                    pairs.append((row * cols_count + col, (goal[0] * fanout + goal[1]) * cols_count + goal[2]))
        return lax.ppermute(value, BOTH, pairs)

    cycle = [
        (layer if lane % 2 == 0 else layers - 1 - layer) * fanout + lane
        for lane in range(fanout)
        for layer in range(layers)
    ]
    spot = {row: place for place, row in enumerate(cycle)}

    def around(value, steps):
        pairs = [(row, cycle[(spot[row] + steps) % rows_count]) for row in range(rows_count)]
        return lax.ppermute(value, "row", pairs)

    aligned = history.shape[1] % 256 == 0

    def in_row_order(values, sense):
        row = lax.axis_index("row")
        here = jnp.asarray([spot[row] for row in range(rows_count)], jnp.int32)[row]
        rows = jnp.asarray(cycle, jnp.int32)[(here - sense * jnp.arange(rows_count)) % rows_count]
        return jnp.take(jnp.stack(values), jnp.argsort(rows), axis=0)

    mark, gain, cubic = first_call(interaction, load_gain, load_cubic, share)

    def folded(kept, sent):
        for bit in bits[:-1]:
            got = send(sent, lambda layer, lane, col: (layer, lane, col ^ bit))
            kept, sent = fold_call(interaction, kept, got, 2 * bit, 2 * bit == bits[-1])
        return kept, sent

    def last_hop(sent):
        return send(sent, lambda layer, lane, col: (layer, lane, col ^ bits[-1]))

    def to_layers(current):
        by_layer = {0: current}
        for bit in reversed(bits):
            for apart in list(by_layer):
                value = by_layer[apart]
                if apart and bit in by_layer:
                    value, by_layer[bit] = lax.optimization_barrier((value, by_layer[bit]))
                by_layer[apart ^ bit] = send(value, lambda layer, lane, col: (layer ^ bit, lane, col))
        return by_layer

    def to_sources(ordered):
        lanes = [None] * fanout
        for beside in reversed(range(fanout)):
            lanes[beside] = [
                send(ordered[other], lambda layer, lane, col: (layer, (lane - beside) % fanout, col ^ other))
                if beside or other
                else ordered[0]
                for other in range(cols_count)
            ]
        return lanes

    chunks = split_waves(history.shape[2])
    half = history.shape[1] // 2
    moving = [(history[:, :half, start:stop], history[:, half:, start:stop]) for start, stop in chunks]
    carried, marks = [None] * len(chunks), [None] * len(chunks)
    arrived = [[moving[number]] for number in range(len(chunks))]

    def add_piece(number, step):
        start, stop = chunks[number]
        outs = past_call(
            delay,
            tile,
            interaction,
            arrived[number][step],
            marks[number],
            carried[number],
            None,
            step,
            (0, 1),
            layers,
            fanout,
        )
        carried[number], marks[number] = outs

    marks = [mark] * len(chunks)
    added = [0] * len(chunks)
    for step in range(1, rows_count):
        for number in range(len(chunks)):
            front, back = arrived[number][-1]
            if step >= 2 and aligned:
                wanted = 0 if step == 2 else 1 if step == 3 else step - 1
                while added[number] < wanted:
                    add_piece(number, added[number])
                    added[number] += 1
                front, back, marks[number] = lax.optimization_barrier((front, back, marks[number]))
            arrived[number].append((around(front, 1), around(back, -1)))
    last = rows_count - 1
    for number, (start, stop) in enumerate(chunks):
        if aligned:
            for step in range(added[number], last):
                add_piece(number, step)
            arrived[number] = arrived[number][last]
        else:
            fronts, backs = zip(*arrived[number])
            ordered = jnp.stack([in_row_order(fronts, 1), in_row_order(backs, -1)], axis=1)
            ordered = jnp.moveaxis(ordered, 2, 0).reshape(history.shape[0], 2, rows_count * half, stop - start)
            arrived[number] = ordered[:, 0], ordered[:, 1]

    def end_past(number, step):
        start, stop = chunks[number]
        return past_call(
            delay,
            tile,
            interaction,
            arrived[number],
            marks[number],
            carried[number],
            incident[:, :, start:stop],
            last,
            (step,),
            layers,
            fanout,
        )

    numbers = range(len(chunks))
    kepts, sents = [None] * len(chunks), [None] * len(chunks)
    for number in numbers:
        kepts[number], sents[number] = folded(*end_past(number, 0))
    gots, laters = [], []
    for number in numbers:
        gots.append(last_hop(sents[number]))
        sents[number], marks[number] = lax.optimization_barrier((sents[number], marks[number]))
        laters.append(end_past(number, 1)[0])
    by_layers = [to_layers(load_call(interaction, kepts[number], gots[number], gain, cubic)) for number in numbers]
    every, ends = [], []
    for number in numbers:
        ordered = arrange_call(interaction, [by_layers[number][apart] for apart in range(layers)], fanout)
        if number:
            ordered, ends[-1] = lax.optimization_barrier((ordered, ends[-1]))
        every.append(to_sources(ordered))
        ends.append(
            recent_call(delay, tile, interaction, every[number][0], laters[number], 0, fanout, cols_count)
        )
    for number in numbers:
        for beside in range(1, fanout):
            ends[number] = recent_call(
                delay, tile, interaction, every[number][beside], ends[number][0], beside, fanout, cols_count
            )
        kepts[number], sents[number] = folded(*ends[number])
    gots = [last_hop(sents[number]) for number in numbers]
    lasts = [load_call(interaction, kepts[number], gots[number], gain, cubic) for number in numbers]
    results = [jnp.stack([by_layer[0], last]) for by_layer, last in zip(by_layers, lasts)]
    return jnp.concatenate(results, axis=2)


def solution(mesh):
    placed = (
        P(None, "row", "col"),
        P(None, ("col", "row"), None),
        P(None, ("row", "col"), None),
        P("row"),
        P("row"),
        P("row", "col", None),
        P("row", "col"),
    )
    return jax.shard_map(
        functools.partial(per_device, mesh.shape["row"], mesh.shape["col"]),
        mesh=mesh,
        in_specs=placed,
        out_specs=P(None, ("row", "col"), None),
        check_vma=False,
    )
```

profile of v0, /device:TPU:0, one launch (start us, length us, event | category | flops | bytes accessed | tf_op | source)
XLA Modules:
  0.0 158.3 jit_solution(11640173432345817850)
XLA Ops:
  0.0 1.3 fusion.1
  1.3 3.1 %collective-permute-start = (bf16[4,128,256]{2,1,0:T(8,128)(2,1)S(1)}, bf16[4,128,256]{2,1,0:T(8,128)(2,1)S(1)}, u32[]{:S(2)}, u32[]{:S(2)}) collective-permute-start(bf16[4,128,256]{2,1,0:T(8,128)(2,1)S(1)} %get-tuple-element.212.front), channel_id=1, source_target_pairs={{0,8},{4,0},{8,16},{12,4},{16,24},{20,12},{24,28},{28,20},{1,9},{5... | collective-permute-start | bytes 786440 | tf_op jit(solution)/shard_map/ppermute | solution.py:303
  4.4 2.0 %collective-permute-start.23 = (bf16[4,128,256]{2,1,0:T(8,128)(2,1)S(1)}, bf16[4,128,256]{2,1,0:T(8,128)(2,1)S(1)}, u32[]{:S(2)}, u32[]{:S(2)}) collective-permute-start(bf16[4,128,256]{2,1,0:T(8,128)(2,1)S(1)} %get-tuple-element.214.front), channel_id=1, source_target_pairs={{0,8},{4,0},{8,16},{12,4},{16,24},{20,12},{24,28},{28,20},{1,9},{5... | collective-permute-start | bytes 786440 | tf_op jit(solution)/shard_map/ppermute | solution.py:303
  6.4 7.0 %copy-done = bf16[5,1024,2048]{2,1,0:T(8,128)(2,1)S(1)} copy-done((bf16[5,1024,2048]{2,1,0:T(8,128)(2,1)S(1)}, bf16[5,1024,2048]{2,1,0:T(8,128)(2,1)}, u32[]{:S(2)}) %copy-start) | copy-done | bytes 20971544
  13.8 2.1 %collective-permute-start.2 = (bf16[4,128,256]{2,1,0:T(8,128)(2,1)S(1)}, bf16[4,128,256]{2,1,0:T(8,128)(2,1)S(1)}, u32[]{:S(2)}, u32[]{:S(2)}) collective-permute-start(bf16[4,128,256]{2,1,0:T(8,128)(2,1)S(1)} %collective-permute-done.front), channel_id=1, source_target_pairs={{0,8},{4,0},{8,16},{12,4},{16,24},{20,12},{24,28},{28,20},{1,9},{5... | collective-permute-start | bytes 786440 | tf_op jit(solution)/shard_map/ppermute | solution.py:303
  15.9 1.1 collective-permute-done.23.front
  16.9 1.6 %collective-permute-done.24.back = bf16[4,128,256]{2,1,0:T(8,128)(2,1)S(1)} collective-permute-done((bf16[4,128,256]{2,1,0:T(8,128)(2,1)S(1)}, bf16[4,128,256]{2,1,0:T(8,128)(2,1)S(1)}, u32[]{:S(2)}, u32[]{:S(2)}) %collective-permute-start.24) | collective-permute-done | bytes 262176 | tf_op jit(solution)/shard_map/ppermute | solution.py:303
  18.6 1.6 collective-permute-start.25
  21.3 2.7 %shard_map.74 = (f32[1024,512]{1,0:T(8,128)S(1)}, f32[8,128]{1,0:T(8,128)S(1)}) custom-call(s32[5]{0:T(128)S(1)} %bitcast.34, s32[1]{0:T(128)} %bitcast.8.tile, bf16[5,1024,2048]{2,1,0:T(8,128)(2,1)S(1)} %copy-done.1, bf16[4,128,256]{2,1,0:T(8,128)(2,1)S(1)} %get-tuple-element.212.front, bf16[4,128,256]{2,1,0:T(8,128)(2,1)S(1)} %get-tuple-element.211.back, ...), custom_call_target="tpu_custom_call" | custom-call | flops 1342177280 | bytes 2621440 | tf_op jit(solution)/shard_map/pallas_call | solution.py:145
  24.0 1.1 collective-permute-done.3.back
  25.1 1.6 collective-permute-start.4
  27.1 2.7 %shard_map.85 = (f32[1024,512]{1,0:T(8,128)S(1)}, f32[8,128]{1,0:T(8,128)S(1)}) custom-call(s32[5]{0:T(128)S(1)} %bitcast.35, s32[1]{0:T(128)} %bitcast.16.tile, bf16[5,1024,2048]{2,1,0:T(8,128)(2,1)S(1)} %copy-done.1, bf16[4,128,256]{2,1,0:T(8,128)(2,1)S(1)} %get-tuple-element.214.front, bf16[4,128,256]{2,1,0:T(8,128)(2,1)S(1)} %get-tuple-element.213.back, ...), custom_call_target="tpu_custom_call" | custom-call | flops 1342177280 | bytes 2621440 | tf_op jit(solution)/shard_map/pallas_call | solution.py:145
  30.7 1.6 collective-permute-start.27
  32.8 2.7 %shard_map.75 = (f32[1024,512]{1,0:T(8,128)S(1)}, f32[8,128]{1,0:T(8,128)S(1)}) custom-call(s32[5]{0:T(128)S(1)} %bitcast.36, s32[1]{0:T(128)} %bitcast.9.tile, bf16[5,1024,2048]{2,1,0:T(8,128)(2,1)S(1)} %copy-done.1, bf16[4,128,256]{2,1,0:T(8,128)(2,1)S(1)} %collective-permute-done.front, ...), custom_call_target="tpu_custom_call", output_to_operand_aliasing={{0}: (6, {})} | custom-call | flops 1342177280 | bytes 2621440 | tf_op jit(solution)/shard_map/pallas_call | solution.py:145
  35.5 2.8 %shard_map.76 = (f32[1024,512]{1,0:T(8,128)S(1)}, f32[8,128]{1,0:T(8,128)S(1)}) custom-call(s32[5]{0:T(128)S(1)} %bitcast.37, s32[1]{0:T(128)} %bitcast.10.tile, bf16[5,1024,2048]{2,1,0:T(8,128)(2,1)S(1)} %copy-done.1, bf16[4,128,256]{2,1,0:T(8,128)(2,1)S(1)} %collective-permute-done.2.front, ...), custom_call_target="tpu_custom_call", output_to_operand_aliasing={{0}: (6, {})} | custom-call | flops 1342177280 | bytes 2621440 | tf_op jit(solution)/shard_map/pallas_call | solution.py:145
  38.3 1.7 %collective-permute-start.6 = (bf16[4,128,256]{2,1,0:T(8,128)(2,1)S(1)}, bf16[4,128,256]{2,1,0:T(8,128)(2,1)S(1)}, u32[]{:S(2)}, u32[]{:S(2)}) collective-permute-start(bf16[4,128,256]{2,1,0:T(8,128)(2,1)S(1)} %collective-permute-done.4.front), channel_id=1, source_target_pairs={{0,8},{4,0},{8,16},{12,4},{16,24},{20,12},{24,28},{28,20},{1,9},{5... | collective-permute-start | bytes 786440 | tf_op jit(solution)/shard_map/ppermute | solution.py:303
  40.4 2.7 %shard_map.86 = (f32[1024,512]{1,0:T(8,128)S(1)}, f32[8,128]{1,0:T(8,128)S(1)}) custom-call(s32[5]{0:T(128)S(1)} %bitcast.38, s32[1]{0:T(128)} %bitcast.17.tile, bf16[5,1024,2048]{2,1,0:T(8,128)(2,1)S(1)} %copy-done.1, bf16[4,128,256]{2,1,0:T(8,128)(2,1)S(1)} %collective-permute-done.23.front, ...), custom_call_target="tpu_custom_call", output_to_operand_aliasing={{0}: (6, {})} | custom-call | flops 1342177280 | bytes 2621440 | tf_op jit(solution)/shard_map/pallas_call | solution.py:145
  43.1 2.8 %shard_map.87 = (f32[1024,512]{1,0:T(8,128)S(1)}, f32[8,128]{1,0:T(8,128)S(1)}) custom-call(s32[5]{0:T(128)S(1)} %bitcast.39, s32[1]{0:T(128)} %bitcast.18.tile, bf16[5,1024,2048]{2,1,0:T(8,128)(2,1)S(1)} %copy-done.1, bf16[4,128,256]{2,1,0:T(8,128)(2,1)S(1)} %collective-permute-done.25.front, ...), custom_call_target="tpu_custom_call", output_to_operand_aliasing={{0}: (6, {})} | custom-call | flops 1342177280 | bytes 2621440 | tf_op jit(solution)/shard_map/pallas_call | solution.py:145
  45.9 1.7 %collective-permute-start.29 = (bf16[4,128,256]{2,1,0:T(8,128)(2,1)S(1)}, bf16[4,128,256]{2,1,0:T(8,128)(2,1)S(1)}, u32[]{:S(2)}, u32[]{:S(2)}) collective-permute-start(bf16[4,128,256]{2,1,0:T(8,128)(2,1)S(1)} %collective-permute-done.27.front), channel_id=1, source_target_pairs={{0,8},{4,0},{8,16},{12,4},{16,24},{20,12},{24,28},{28,20},{1,9},{5... | collective-permute-start | bytes 786440 | tf_op jit(solution)/shard_map/ppermute | solution.py:303
  48.0 2.7 %shard_map.77 = (f32[1024,512]{1,0:T(8,128)S(1)}, f32[8,128]{1,0:T(8,128)S(1)}) custom-call(s32[5]{0:T(128)S(1)} %bitcast.40, s32[1]{0:T(128)} %bitcast.11.tile, bf16[5,1024,2048]{2,1,0:T(8,128)(2,1)S(1)} %copy-done.1, bf16[4,128,256]{2,1,0:T(8,128)(2,1)S(1)} %collective-permute-done.4.front, ...), custom_call_target="tpu_custom_call", output_to_operand_aliasing={{0}: (6, {})} | custom-call | flops 1342177280 | bytes 2621440 | tf_op jit(solution)/shard_map/pallas_call | solution.py:145
  50.8 1.7 %collective-permute-start.8 = (bf16[4,128,256]{2,1,0:T(8,128)(2,1)S(1)}, bf16[4,128,256]{2,1,0:T(8,128)(2,1)S(1)}, u32[]{:S(2)}, u32[]{:S(2)}) collective-permute-start(bf16[4,128,256]{2,1,0:T(8,128)(2,1)S(1)} %collective-permute-done.6.front), channel_id=1, source_target_pairs={{0,8},{4,0},{8,16},{12,4},{16,24},{20,12},{24,28},{28,20},{1,9},{5... | collective-permute-start | bytes 786440 | tf_op jit(solution)/shard_map/ppermute | solution.py:303
  52.9 2.7 %shard_map.88 = (f32[1024,512]{1,0:T(8,128)S(1)}, f32[8,128]{1,0:T(8,128)S(1)}) custom-call(s32[5]{0:T(128)S(1)} %bitcast.41, s32[1]{0:T(128)} %bitcast.19.tile, bf16[5,1024,2048]{2,1,0:T(8,128)(2,1)S(1)} %copy-done.1, bf16[4,128,256]{2,1,0:T(8,128)(2,1)S(1)} %collective-permute-done.27.front, ...), custom_call_target="tpu_custom_call", output_to_operand_aliasing={{0}: (6, {})} | custom-call | flops 1342177280 | bytes 2621440 | tf_op jit(solution)/shard_map/pallas_call | solution.py:145
  55.6 1.0 collective-permute-done.30.back
  56.7 1.4 collective-permute-start.31
  58.7 2.8 %shard_map.78 = (f32[1024,512]{1,0:T(8,128)S(1)}, f32[8,128]{1,0:T(8,128)S(1)}) custom-call(s32[5]{0:T(128)S(1)} %bitcast.42, s32[1]{0:T(128)} %bitcast.12.tile, bf16[5,1024,2048]{2,1,0:T(8,128)(2,1)S(1)} %copy-done.1, bf16[4,128,256]{2,1,0:T(8,128)(2,1)S(1)} %collective-permute-done.6.front, ...), custom_call_target="tpu_custom_call", output_to_operand_aliasing={{0}: (6, {})} | custom-call | flops 1342177280 | bytes 2621440 | tf_op jit(solution)/shard_map/pallas_call | solution.py:145
  62.3 1.4 collective-permute-start.10
  64.3 2.8 %shard_map.89 = (f32[1024,512]{1,0:T(8,128)S(1)}, f32[8,128]{1,0:T(8,128)S(1)}) custom-call(s32[5]{0:T(128)S(1)} %bitcast.43, s32[1]{0:T(128)} %bitcast.20.tile, bf16[5,1024,2048]{2,1,0:T(8,128)(2,1)S(1)} %copy-done.1, bf16[4,128,256]{2,1,0:T(8,128)(2,1)S(1)} %collective-permute-done.29.front, ...), custom_call_target="tpu_custom_call", output_to_operand_aliasing={{0}: (6, {})} | custom-call | flops 1342177280 | bytes 2621440 | tf_op jit(solution)/shard_map/pallas_call | solution.py:145
  67.9 1.4 collective-permute-start.33
  69.9 2.7 %shard_map.79 = (f32[1024,512]{1,0:T(8,128)S(1)}, f32[8,128]{1,0:T(8,128)S(1)}) custom-call(s32[5]{0:T(128)S(1)} %bitcast.44, s32[1]{0:T(128)} %bitcast.13.tile, bf16[5,1024,2048]{2,1,0:T(8,128)(2,1)S(1)} %copy-done.1, bf16[4,128,256]{2,1,0:T(8,128)(2,1)S(1)} %collective-permute-done.8.front, ...), custom_call_target="tpu_custom_call", output_to_operand_aliasing={{0}: (6, {})} | custom-call | flops 1342177280 | bytes 2621440 | tf_op jit(solution)/shard_map/pallas_call | solution.py:145
  73.5 1.4 collective-permute-start.12
  75.6 2.7 %shard_map.90 = (f32[1024,512]{1,0:T(8,128)S(1)}, f32[8,128]{1,0:T(8,128)S(1)}) custom-call(s32[5]{0:T(128)S(1)} %bitcast.45, s32[1]{0:T(128)} %bitcast.21.tile, bf16[5,1024,2048]{2,1,0:T(8,128)(2,1)S(1)} %copy-done.1, bf16[4,128,256]{2,1,0:T(8,128)(2,1)S(1)} %collective-permute-done.31.front, ...), custom_call_target="tpu_custom_call", output_to_operand_aliasing={{0}: (6, {})} | custom-call | flops 1342177280 | bytes 2621440 | tf_op jit(solution)/shard_map/pallas_call | solution.py:145
  79.1 1.4 collective-permute-start.35
  81.2 2.8 %shard_map.80 = (f32[1024,512]{1,0:T(8,128)S(1)}, f32[8,128]{1,0:T(8,128)S(1)}) custom-call(s32[5]{0:T(128)S(1)} %bitcast.46, s32[1]{0:T(128)} %bitcast.14.tile, bf16[5,1024,2048]{2,1,0:T(8,128)(2,1)S(1)} %copy-done.1, bf16[4,128,256]{2,1,0:T(8,128)(2,1)S(1)} %collective-permute-done.10.front, ...), custom_call_target="tpu_custom_call", output_to_operand_aliasing={{0}: (6, {})} | custom-call | flops 1342177280 | bytes 2621440 | tf_op jit(solution)/shard_map/pallas_call | solution.py:145
  84.0 2.1 %shard_map.81 = (f32[2,256,256]{2,1,0:T(8,128)S(1)}, f32[2,256,256]{2,1,0:T(8,128)S(1)}) custom-call(s32[5]{0:T(128)S(1)} %bitcast.47, s32[1]{0:T(128)} %bitcast.15.tile, bf16[5,1024,2048]{2,1,0:T(8,128)(2,1)S(1)} %copy-done.1, bf16[4,128,256]{2,1,0:T(8,128)(2,1)S(1)} %collective-permute-done.12.front, ...), custom_call_target="tpu_custom_call" | custom-call | flops 671088640 | bytes 2621440 | tf_op jit(solution)/shard_map/pallas_call | solution.py:145
  86.2 2.8 %shard_map.91 = (f32[1024,512]{1,0:T(8,128)S(1)}, f32[8,128]{1,0:T(8,128)S(1)}) custom-call(s32[5]{0:T(128)S(1)} %bitcast.48, s32[1]{0:T(128)} %bitcast.22.tile, bf16[5,1024,2048]{2,1,0:T(8,128)(2,1)S(1)} %copy-done.1, bf16[4,128,256]{2,1,0:T(8,128)(2,1)S(1)} %collective-permute-done.33.front, ...), custom_call_target="tpu_custom_call", output_to_operand_aliasing={{0}: (6, {})} | custom-call | flops 1342177280 | bytes 2621440 | tf_op jit(solution)/shard_map/pallas_call | solution.py:145
  89.0 2.1 %shard_map.92 = (f32[2,256,256]{2,1,0:T(8,128)S(1)}, f32[2,256,256]{2,1,0:T(8,128)S(1)}) custom-call(s32[5]{0:T(128)S(1)} %bitcast.49, s32[1]{0:T(128)} %bitcast.23.tile, bf16[5,1024,2048]{2,1,0:T(8,128)(2,1)S(1)} %copy-done.1, bf16[4,128,256]{2,1,0:T(8,128)(2,1)S(1)} %collective-permute-done.35.front, ...), custom_call_target="tpu_custom_call" | custom-call | flops 671088640 | bytes 2621440 | tf_op jit(solution)/shard_map/pallas_call | solution.py:145
  91.7 1.6 collective-permute-start.15
  93.4 1.4 collective-permute-start.38
  94.8 3.5 %collective-permute-done.15.got = s16[272,256]{1,0:T(8,128)(2,1)S(1)} collective-permute-done((s16[272,256]{1,0:T(8,128)(2,1)S(1)}, s16[272,256]{1,0:T(8,128)(2,1)S(1)}, u32[]{:S(2)}, u32[]{:S(2)}) %collective-permute-start.15) | collective-permute-done | bytes 139296 | tf_op jit(solution)/shard_map/ppermute | solution.py:292
  98.4 2.5 %collective-permute-start.16 = (bf16[256,256]{1,0:T(8,128)(2,1)S(1)}, bf16[256,256]{1,0:T(8,128)(2,1)S(1)}, u32[]{:S(2)}, u32[]{:S(2)}) collective-permute-start(bf16[256,256]{1,0:T(8,128)(2,1)S(1)} %shard_map.83.refs_0_), channel_id=1, source_target_pairs={{0,16},{1,17},{2,18},{3,19},{4,20},{5,21},{6,22},{7,23},{8,24},{9,... | collective-permute-start | bytes 393224 | tf_op jit(solution)/shard_map/ppermute | solution.py:292
  101.6 1.3 collective-permute-start.39
  103.6 5.0 %collective-permute-done.16.refs_2_ = bf16[256,256]{1,0:T(8,128)(2,1)S(1)} collective-permute-done((bf16[256,256]{1,0:T(8,128)(2,1)S(1)}, bf16[256,256]{1,0:T(8,128)(2,1)S(1)}, u32[]{:S(2)}, u32[]{:S(2)}) %collective-permute-start.16) | collective-permute-done | bytes 131104 | tf_op jit(solution)/shard_map/ppermute | solution.py:292
  108.6 1.6 collective-permute-done.17.refs_1_
  110.9 2.5 %collective-permute-done.40.refs_1_ = bf16[256,256]{1,0:T(8,128)(2,1)S(1)} collective-permute-done((bf16[256,256]{1,0:T(8,128)(2,1)S(1)}, bf16[256,256]{1,0:T(8,128)(2,1)S(1)}, u32[]{:S(2)}, u32[]{:S(2)}) %collective-permute-start.40) | collective-permute-done | bytes 131104 | tf_op jit(solution)/shard_map/ppermute | solution.py:292
  113.4 2.3 %collective-permute-start.41 = (bf16[256,256]{1,0:T(8,128)(2,1)S(1)}, bf16[256,256]{1,0:T(8,128)(2,1)S(1)}, u32[]{:S(2)}, u32[]{:S(2)}) collective-permute-start(bf16[256,256]{1,0:T(8,128)(2,1)S(1)} %collective-permute-done.39.refs_2_), channel_id=1, source_target_pairs={{0,8},{1,9},{2,10},{3,11},{4,12},{5,13},{6,14},{7,15},{8,0},{9,1},... | collective-permute-start | bytes 393224 | tf_op jit(solution)/shard_map/ppermute | solution.py:292
  116.3 1.6 collective-permute-start.43
  118.7 2.1 %shard_map.96.refs_4_ = f32[1024,256]{1,0:T(8,128)S(1)} custom-call(s32[5]{0:T(128)S(1)} %bitcast.50, s32[1]{0:T(128)} %bitcast.24.tile, bf16[5,1024,2048]{2,1,0:T(8,128)(2,1)S(1)} %copy-done.1, bf16[4,128,256]{2,1,0:T(8,128)(2,1)S(1)} %collective-permute-done.12.front, bf16[4,128,256]{2,1,0:T(8,128)(2,1)S(1)} %collective-permute-done.13.back, ...), custom_call_target="tpu_custom_call" | custom-call | flops 671088640 | bytes 2621440 | tf_op jit(solution)/shard_map/pallas_call | solution.py:145
  120.8 1.2 collective-permute-start.20
  122.1 1.5 collective-permute-start.21
  123.6 1.3 collective-permute-start.22
  125.7 1.9 %collective-permute-start.51 = (bf16[256,256]{1,0:T(8,128)(2,1)S(1)}, bf16[256,256]{1,0:T(8,128)(2,1)S(1)}, u32[]{:S(2)}, u32[]{:S(2)}) collective-permute-start(bf16[256,256]{1,0:T(8,128)(2,1)S(1)} %get-tuple-element.201), channel_id=1, source_target_pairs={{0,1},{1,0},{2,3},{3,2},{4,5},{5,4},{6,7},{7,6},{8,9},{9,8},{10,11... | collective-permute-start | bytes 393224 | tf_op jit(solution)/shard_map/ppermute | solution.py:292
  127.6 2.0 %collective-permute-start.52 = (bf16[256,256]{1,0:T(8,128)(2,1)S(1)}, bf16[256,256]{1,0:T(8,128)(2,1)S(1)}, u32[]{:S(2)}, u32[]{:S(2)}) collective-permute-start(bf16[256,256]{1,0:T(8,128)(2,1)S(1)} %get-tuple-element.202), channel_id=1, source_target_pairs={{0,2},{1,3},{2,0},{3,1},{4,6},{5,7},{6,4},{7,5},{8,10},{9,11},{10,... | collective-permute-start | bytes 393224 | tf_op jit(solution)/shard_map/ppermute | solution.py:292
  129.6 1.0 collective-permute-done.21.refs_2_
  131.4 1.9 %collective-permute-done.22.refs_3_ = bf16[256,256]{1,0:T(8,128)(2,1)S(1)} collective-permute-done((bf16[256,256]{1,0:T(8,128)(2,1)S(1)}, bf16[256,256]{1,0:T(8,128)(2,1)S(1)}, u32[]{:S(2)}, u32[]{:S(2)}) %collective-permute-start.22) | collective-permute-done | bytes 131104 | tf_op jit(solution)/shard_map/ppermute | solution.py:292
  133.2 1.3 collective-permute-start.47
  136.1 1.0 collective-permute-start.50
  137.1 2.1 %shard_map.101.refs_4_ = f32[1024,256]{1,0:T(8,128)S(1)} custom-call(s32[5]{0:T(128)S(1)} %bitcast.52, s32[1]{0:T(128)} %bitcast.27.tile, bf16[5,1024,2048]{2,1,0:T(8,128)(2,1)S(1)} %copy-done.1, bf16[4,128,256]{2,1,0:T(8,128)(2,1)S(1)} %collective-permute-done.35.front, bf16[4,128,256]{2,1,0:T(8,128)(2,1)S(1)} %collective-permute-done.36.back, ...), custom_call_target="tpu_custom_call" | custom-call | flops 671088640 | bytes 2621440 | tf_op jit(solution)/shard_map/pallas_call | solution.py:145
  140.1 2.0 %collective-permute-start.45 = (f32[2,256,256]{2,1,0:T(8,128)S(1)}, f32[2,256,256]{2,1,0:T(8,128)S(1)}, u32[]{:S(2)}, u32[]{:S(2)}) collective-permute-start(f32[2,256,256]{2,1,0:T(8,128)S(1)} %get-tuple-element.197), channel_id=1, source_target_pairs={{0,1},{1,0},{2,3},{3,2},{4,5},{5,4},{6,7},{7,6},{8,9},{9,8},{10,11... | collective-permute-start | bytes 1572872 | tf_op jit(solution)/shard_map/ppermute | solution.py:292
  142.9 1.6 %collective-permute-done.50.refs_3_ = bf16[256,256]{1,0:T(8,128)(2,1)S(1)} collective-permute-done((bf16[256,256]{1,0:T(8,128)(2,1)S(1)}, bf16[256,256]{1,0:T(8,128)(2,1)S(1)}, u32[]{:S(2)}, u32[]{:S(2)}) %collective-permute-start.50) | collective-permute-done | bytes 131104 | tf_op jit(solution)/shard_map/ppermute | solution.py:292
  145.3 1.8 %collective-permute-start.54 = (f32[2,256,256]{2,1,0:T(8,128)S(1)}, f32[2,256,256]{2,1,0:T(8,128)S(1)}, u32[]{:S(2)}, u32[]{:S(2)}) collective-permute-start(f32[2,256,256]{2,1,0:T(8,128)S(1)} %get-tuple-element.206), channel_id=1, source_target_pairs={{0,1},{1,0},{2,3},{3,2},{4,5},{5,4},{6,7},{7,6},{8,9},{9,8},{10,11... | collective-permute-start | bytes 1572872 | tf_op jit(solution)/shard_map/ppermute | solution.py:292
  147.2 2.9 %collective-permute-start.46 = (s16[272,256]{1,0:T(8,128)(2,1)S(1)}, s16[272,256]{1,0:T(8,128)(2,1)S(1)}, u32[]{:S(2)}, u32[]{:S(2)}) collective-permute-start(s16[272,256]{1,0:T(8,128)(2,1)S(1)} %get-tuple-element.199), channel_id=1, source_target_pairs={{0,2},{1,3},{2,0},{3,1},{4,6},{5,7},{6,4},{7,5},{8,10},{9,11},{10,... | collective-permute-start | bytes 417800 | tf_op jit(solution)/shard_map/ppermute | solution.py:292
  150.2 1.8 %collective-permute-start.55 = (s16[272,256]{1,0:T(8,128)(2,1)S(1)}, s16[272,256]{1,0:T(8,128)(2,1)S(1)}, u32[]{:S(2)}, u32[]{:S(2)}) collective-permute-start(s16[272,256]{1,0:T(8,128)(2,1)S(1)} %get-tuple-element.208), channel_id=1, source_target_pairs={{0,2},{1,3},{2,0},{3,1},{4,6},{5,7},{6,4},{7,5},{8,10},{9,11},{10,... | collective-permute-start | bytes 417800 | tf_op jit(solution)/shard_map/ppermute | solution.py:292
  152.0 2.7 %collective-permute-done.46.got = s16[272,256]{1,0:T(8,128)(2,1)S(1)} collective-permute-done((s16[272,256]{1,0:T(8,128)(2,1)S(1)}, s16[272,256]{1,0:T(8,128)(2,1)S(1)}, u32[]{:S(2)}, u32[]{:S(2)}) %collective-permute-start.46) | collective-permute-done | bytes 139296 | tf_op jit(solution)/shard_map/ppermute | solution.py:292
  154.7 2.7 %collective-permute-done.55.got = s16[272,256]{1,0:T(8,128)(2,1)S(1)} collective-permute-done((s16[272,256]{1,0:T(8,128)(2,1)S(1)}, s16[272,256]{1,0:T(8,128)(2,1)S(1)}, u32[]{:S(2)}, u32[]{:S(2)}) %collective-permute-start.55) | collective-permute-done | bytes 139296 | tf_op jit(solution)/shard_map/ppermute | solution.py:292
  (96 shorter events, 21.8 us)
Async XLA Ops:
  0.0 6.4 %copy-start.3 = (f32[1024]{0:T(1024)S(1)}, f32[1024]{0:T(1024)}, u32[]{:S(2)}) copy-start(f32[1024]{0:T(1024)} %param.10) | copy-start | bytes 12292
  0.0 6.4 %copy-start.4 = (f32[1024]{0:T(1024)S(1)}, f32[1024]{0:T(1024)}, u32[]{:S(2)}) copy-start(f32[1024]{0:T(1024)} %param.11) | copy-start | bytes 12292
  1.3 12.5 %collective-permute-start = (bf16[4,128,256]{2,1,0:T(8,128)(2,1)S(1)}, bf16[4,128,256]{2,1,0:T(8,128)(2,1)S(1)}, u32[]{:S(2)}, u32[]{:S(2)}) collective-permute-start(bf16[4,128,256]{2,1,0:T(8,128)(2,1)S(1)} %get-tuple-element.212.front), channel_id=1, source_target_pairs={{0,8},{4,0},{8,16},{12,4},{16,24},{20,12},{24,28},{28,20},{1,9},{5... | collective-permute-start | bytes 786440 | tf_op jit(solution)/shard_map/ppermute | solution.py:303
  4.4 9.4 %collective-permute-start.1 = (bf16[4,128,256]{2,1,0:T(8,128)(2,1)S(1)}, bf16[4,128,256]{2,1,0:T(8,128)(2,1)S(1)}, u32[]{:S(2)}, u32[]{:S(2)}) collective-permute-start(bf16[4,128,256]{2,1,0:T(8,128)(2,1)S(1)} %get-tuple-element.211.back), channel_id=1, source_target_pairs={{0,4},{4,12},{8,0},{12,20},{16,8},{20,28},{24,16},{28,24},{1,5},{5... | collective-permute-start | bytes 786440 | tf_op jit(solution)/shard_map/ppermute | solution.py:303
  4.4 12.6 %collective-permute-start.23 = (bf16[4,128,256]{2,1,0:T(8,128)(2,1)S(1)}, bf16[4,128,256]{2,1,0:T(8,128)(2,1)S(1)}, u32[]{:S(2)}, u32[]{:S(2)}) collective-permute-start(bf16[4,128,256]{2,1,0:T(8,128)(2,1)S(1)} %get-tuple-element.214.front), channel_id=1, source_target_pairs={{0,8},{4,0},{8,16},{12,4},{16,24},{20,12},{24,28},{28,20},{1,9},{5... | collective-permute-start | bytes 786440 | tf_op jit(solution)/shard_map/ppermute | solution.py:303
  6.4 12.2 %collective-permute-start.24 = (bf16[4,128,256]{2,1,0:T(8,128)(2,1)S(1)}, bf16[4,128,256]{2,1,0:T(8,128)(2,1)S(1)}, u32[]{:S(2)}, u32[]{:S(2)}) collective-permute-start(bf16[4,128,256]{2,1,0:T(8,128)(2,1)S(1)} %get-tuple-element.213.back), channel_id=1, source_target_pairs={{0,4},{4,12},{8,0},{12,20},{16,8},{20,28},{24,16},{28,24},{1,5},{5... | collective-permute-start | bytes 786440 | tf_op jit(solution)/shard_map/ppermute | solution.py:303
  6.4 7.0 %copy-start = (bf16[5,1024,2048]{2,1,0:T(8,128)(2,1)S(1)}, bf16[5,1024,2048]{2,1,0:T(8,128)(2,1)}, u32[]{:S(2)}) copy-start(bf16[5,1024,2048]{2,1,0:T(8,128)(2,1)} %matrix.65) | copy-start | bytes 62914564
  13.4 7.9 %copy-start.1 = (bf16[5,1024,2048]{2,1,0:T(8,128)(2,1)S(1)}, bf16[5,1024,2048]{2,1,0:T(8,128)(2,1)}, u32[]{:S(2)}) copy-start(bf16[5,1024,2048]{2,1,0:T(8,128)(2,1)} %matrix.65) | copy-start | bytes 62914564
  13.4 7.9 %copy-start.2 = (s32[1,1,5]{2,1,0:T(1,128)S(1)}, s32[1,1,5]{2,1,0:T(1,128)}, u32[]{:S(2)}) copy-start(s32[1,1,5]{2,1,0:T(1,128)} %param.12) | copy-start | bytes 64
  13.8 10.2 %collective-permute-start.2 = (bf16[4,128,256]{2,1,0:T(8,128)(2,1)S(1)}, bf16[4,128,256]{2,1,0:T(8,128)(2,1)S(1)}, u32[]{:S(2)}, u32[]{:S(2)}) collective-permute-start(bf16[4,128,256]{2,1,0:T(8,128)(2,1)S(1)} %collective-permute-done.front), channel_id=1, source_target_pairs={{0,8},{4,0},{8,16},{12,4},{16,24},{20,12},{24,28},{28,20},{1,9},{5... | collective-permute-start | bytes 786440 | tf_op jit(solution)/shard_map/ppermute | solution.py:303
  15.9 9.2 %collective-permute-start.3 = (bf16[4,128,256]{2,1,0:T(8,128)(2,1)S(1)}, bf16[4,128,256]{2,1,0:T(8,128)(2,1)S(1)}, u32[]{:S(2)}, u32[]{:S(2)}) collective-permute-start(bf16[4,128,256]{2,1,0:T(8,128)(2,1)S(1)} %collective-permute-done.1.back), channel_id=1, source_target_pairs={{0,4},{4,12},{8,0},{12,20},{16,8},{20,28},{24,16},{28,24},{1,5},{5... | collective-permute-start | bytes 786440 | tf_op jit(solution)/shard_map/ppermute | solution.py:303
  18.6 11.3 %collective-permute-start.25 = (bf16[4,128,256]{2,1,0:T(8,128)(2,1)S(1)}, bf16[4,128,256]{2,1,0:T(8,128)(2,1)S(1)}, u32[]{:S(2)}, u32[]{:S(2)}) collective-permute-start(bf16[4,128,256]{2,1,0:T(8,128)(2,1)S(1)} %collective-permute-done.23.front), channel_id=1, source_target_pairs={{0,8},{4,0},{8,16},{12,4},{16,24},{20,12},{24,28},{28,20},{1,9},{5... | collective-permute-start | bytes 786440 | tf_op jit(solution)/shard_map/ppermute | solution.py:303
  20.2 10.6 %collective-permute-start.26 = (bf16[4,128,256]{2,1,0:T(8,128)(2,1)S(1)}, bf16[4,128,256]{2,1,0:T(8,128)(2,1)S(1)}, u32[]{:S(2)}, u32[]{:S(2)}) collective-permute-start(bf16[4,128,256]{2,1,0:T(8,128)(2,1)S(1)} %collective-permute-done.24.back), channel_id=1, source_target_pairs={{0,4},{4,12},{8,0},{12,20},{16,8},{20,28},{24,16},{28,24},{1,5},{5... | collective-permute-start | bytes 786440 | tf_op jit(solution)/shard_map/ppermute | solution.py:303
  25.1 13.2 %collective-permute-start.4 = (bf16[4,128,256]{2,1,0:T(8,128)(2,1)S(1)}, bf16[4,128,256]{2,1,0:T(8,128)(2,1)S(1)}, u32[]{:S(2)}, u32[]{:S(2)}) collective-permute-start(bf16[4,128,256]{2,1,0:T(8,128)(2,1)S(1)} %collective-permute-done.2.front), channel_id=1, source_target_pairs={{0,8},{4,0},{8,16},{12,4},{16,24},{20,12},{24,28},{28,20},{1,9},{5... | collective-permute-start | bytes 786440 | tf_op jit(solution)/shard_map/ppermute | solution.py:303
  26.7 11.6 %collective-permute-start.5 = (bf16[4,128,256]{2,1,0:T(8,128)(2,1)S(1)}, bf16[4,128,256]{2,1,0:T(8,128)(2,1)S(1)}, u32[]{:S(2)}, u32[]{:S(2)}) collective-permute-start(bf16[4,128,256]{2,1,0:T(8,128)(2,1)S(1)} %collective-permute-done.3.back), channel_id=1, source_target_pairs={{0,4},{4,12},{8,0},{12,20},{16,8},{20,28},{24,16},{28,24},{1,5},{5... | collective-permute-start | bytes 786440 | tf_op jit(solution)/shard_map/ppermute | solution.py:303
  30.7 15.2 %collective-permute-start.27 = (bf16[4,128,256]{2,1,0:T(8,128)(2,1)S(1)}, bf16[4,128,256]{2,1,0:T(8,128)(2,1)S(1)}, u32[]{:S(2)}, u32[]{:S(2)}) collective-permute-start(bf16[4,128,256]{2,1,0:T(8,128)(2,1)S(1)} %collective-permute-done.25.front), channel_id=1, source_target_pairs={{0,8},{4,0},{8,16},{12,4},{16,24},{20,12},{24,28},{28,20},{1,9},{5... | collective-permute-start | bytes 786440 | tf_op jit(solution)/shard_map/ppermute | solution.py:303
  32.3 13.6 %collective-permute-start.28 = (bf16[4,128,256]{2,1,0:T(8,128)(2,1)S(1)}, bf16[4,128,256]{2,1,0:T(8,128)(2,1)S(1)}, u32[]{:S(2)}, u32[]{:S(2)}) collective-permute-start(bf16[4,128,256]{2,1,0:T(8,128)(2,1)S(1)} %collective-permute-done.26.back), channel_id=1, source_target_pairs={{0,4},{4,12},{8,0},{12,20},{16,8},{20,28},{24,16},{28,24},{1,5},{5... | collective-permute-start | bytes 786440 | tf_op jit(solution)/shard_map/ppermute | solution.py:303
  38.3 12.5 %collective-permute-start.6 = (bf16[4,128,256]{2,1,0:T(8,128)(2,1)S(1)}, bf16[4,128,256]{2,1,0:T(8,128)(2,1)S(1)}, u32[]{:S(2)}, u32[]{:S(2)}) collective-permute-start(bf16[4,128,256]{2,1,0:T(8,128)(2,1)S(1)} %collective-permute-done.4.front), channel_id=1, source_target_pairs={{0,8},{4,0},{8,16},{12,4},{16,24},{20,12},{24,28},{28,20},{1,9},{5... | collective-permute-start | bytes 786440 | tf_op jit(solution)/shard_map/ppermute | solution.py:303
  40.0 10.8 %collective-permute-start.7 = (bf16[4,128,256]{2,1,0:T(8,128)(2,1)S(1)}, bf16[4,128,256]{2,1,0:T(8,128)(2,1)S(1)}, u32[]{:S(2)}, u32[]{:S(2)}) collective-permute-start(bf16[4,128,256]{2,1,0:T(8,128)(2,1)S(1)} %collective-permute-done.5.back), channel_id=1, source_target_pairs={{0,4},{4,12},{8,0},{12,20},{16,8},{20,28},{24,16},{28,24},{1,5},{5... | collective-permute-start | bytes 786440 | tf_op jit(solution)/shard_map/ppermute | solution.py:303
  45.9 9.7 %collective-permute-start.29 = (bf16[4,128,256]{2,1,0:T(8,128)(2,1)S(1)}, bf16[4,128,256]{2,1,0:T(8,128)(2,1)S(1)}, u32[]{:S(2)}, u32[]{:S(2)}) collective-permute-start(bf16[4,128,256]{2,1,0:T(8,128)(2,1)S(1)} %collective-permute-done.27.front), channel_id=1, source_target_pairs={{0,8},{4,0},{8,16},{12,4},{16,24},{20,12},{24,28},{28,20},{1,9},{5... | collective-permute-start | bytes 786440 | tf_op jit(solution)/shard_map/ppermute | solution.py:303
  47.6 9.0 %collective-permute-start.30 = (bf16[4,128,256]{2,1,0:T(8,128)(2,1)S(1)}, bf16[4,128,256]{2,1,0:T(8,128)(2,1)S(1)}, u32[]{:S(2)}, u32[]{:S(2)}) collective-permute-start(bf16[4,128,256]{2,1,0:T(8,128)(2,1)S(1)} %collective-permute-done.28.back), channel_id=1, source_target_pairs={{0,4},{4,12},{8,0},{12,20},{16,8},{20,28},{24,16},{28,24},{1,5},{5... | collective-permute-start | bytes 786440 | tf_op jit(solution)/shard_map/ppermute | solution.py:303
  50.8 10.7 %collective-permute-start.8 = (bf16[4,128,256]{2,1,0:T(8,128)(2,1)S(1)}, bf16[4,128,256]{2,1,0:T(8,128)(2,1)S(1)}, u32[]{:S(2)}, u32[]{:S(2)}) collective-permute-start(bf16[4,128,256]{2,1,0:T(8,128)(2,1)S(1)} %collective-permute-done.6.front), channel_id=1, source_target_pairs={{0,8},{4,0},{8,16},{12,4},{16,24},{20,12},{24,28},{28,20},{1,9},{5... | collective-permute-start | bytes 786440 | tf_op jit(solution)/shard_map/ppermute | solution.py:303
  52.5 9.8 %collective-permute-start.9 = (bf16[4,128,256]{2,1,0:T(8,128)(2,1)S(1)}, bf16[4,128,256]{2,1,0:T(8,128)(2,1)S(1)}, u32[]{:S(2)}, u32[]{:S(2)}) collective-permute-start(bf16[4,128,256]{2,1,0:T(8,128)(2,1)S(1)} %collective-permute-done.7.back), channel_id=1, source_target_pairs={{0,4},{4,12},{8,0},{12,20},{16,8},{20,28},{24,16},{28,24},{1,5},{5... | collective-permute-start | bytes 786440 | tf_op jit(solution)/shard_map/ppermute | solution.py:303
  56.7 10.4 %collective-permute-start.31 = (bf16[4,128,256]{2,1,0:T(8,128)(2,1)S(1)}, bf16[4,128,256]{2,1,0:T(8,128)(2,1)S(1)}, u32[]{:S(2)}, u32[]{:S(2)}) collective-permute-start(bf16[4,128,256]{2,1,0:T(8,128)(2,1)S(1)} %collective-permute-done.29.front), channel_id=1, source_target_pairs={{0,8},{4,0},{8,16},{12,4},{16,24},{20,12},{24,28},{28,20},{1,9},{5... | collective-permute-start | bytes 786440 | tf_op jit(solution)/shard_map/ppermute | solution.py:303
  58.0 9.9 %collective-permute-start.32 = (bf16[4,128,256]{2,1,0:T(8,128)(2,1)S(1)}, bf16[4,128,256]{2,1,0:T(8,128)(2,1)S(1)}, u32[]{:S(2)}, u32[]{:S(2)}) collective-permute-start(bf16[4,128,256]{2,1,0:T(8,128)(2,1)S(1)} %collective-permute-done.30.back), channel_id=1, source_target_pairs={{0,4},{4,12},{8,0},{12,20},{16,8},{20,28},{24,16},{28,24},{1,5},{5... | collective-permute-start | bytes 786440 | tf_op jit(solution)/shard_map/ppermute | solution.py:303
  62.3 10.4 %collective-permute-start.10 = (bf16[4,128,256]{2,1,0:T(8,128)(2,1)S(1)}, bf16[4,128,256]{2,1,0:T(8,128)(2,1)S(1)}, u32[]{:S(2)}, u32[]{:S(2)}) collective-permute-start(bf16[4,128,256]{2,1,0:T(8,128)(2,1)S(1)} %collective-permute-done.8.front), channel_id=1, source_target_pairs={{0,8},{4,0},{8,16},{12,4},{16,24},{20,12},{24,28},{28,20},{1,9},{5... | collective-permute-start | bytes 786440 | tf_op jit(solution)/shard_map/ppermute | solution.py:303
  63.7 9.9 %collective-permute-start.11 = (bf16[4,128,256]{2,1,0:T(8,128)(2,1)S(1)}, bf16[4,128,256]{2,1,0:T(8,128)(2,1)S(1)}, u32[]{:S(2)}, u32[]{:S(2)}) collective-permute-start(bf16[4,128,256]{2,1,0:T(8,128)(2,1)S(1)} %collective-permute-done.9.back), channel_id=1, source_target_pairs={{0,4},{4,12},{8,0},{12,20},{16,8},{20,28},{24,16},{28,24},{1,5},{5... | collective-permute-start | bytes 786440 | tf_op jit(solution)/shard_map/ppermute | solution.py:303
  67.9 10.5 %collective-permute-start.33 = (bf16[4,128,256]{2,1,0:T(8,128)(2,1)S(1)}, bf16[4,128,256]{2,1,0:T(8,128)(2,1)S(1)}, u32[]{:S(2)}, u32[]{:S(2)}) collective-permute-start(bf16[4,128,256]{2,1,0:T(8,128)(2,1)S(1)} %collective-permute-done.31.front), channel_id=1, source_target_pairs={{0,8},{4,0},{8,16},{12,4},{16,24},{20,12},{24,28},{28,20},{1,9},{5... | collective-permute-start | bytes 786440 | tf_op jit(solution)/shard_map/ppermute | solution.py:303
  69.3 9.9 %collective-permute-start.34 = (bf16[4,128,256]{2,1,0:T(8,128)(2,1)S(1)}, bf16[4,128,256]{2,1,0:T(8,128)(2,1)S(1)}, u32[]{:S(2)}, u32[]{:S(2)}) collective-permute-start(bf16[4,128,256]{2,1,0:T(8,128)(2,1)S(1)} %collective-permute-done.32.back), channel_id=1, source_target_pairs={{0,4},{4,12},{8,0},{12,20},{16,8},{20,28},{24,16},{28,24},{1,5},{5... | collective-permute-start | bytes 786440 | tf_op jit(solution)/shard_map/ppermute | solution.py:303
  69.9 5.6 %copy-start.5 = (f32[2,256,512]{2,1,0:T(8,128)S(1)}, f32[2,256,512]{2,1,0:T(8,128)}, u32[]{:S(2)}) copy-start(f32[2,256,512]{2,1,0:T(8,128)} %param.9) | copy-start | bytes 3145732
  73.5 10.4 %collective-permute-start.12 = (bf16[4,128,256]{2,1,0:T(8,128)(2,1)S(1)}, bf16[4,128,256]{2,1,0:T(8,128)(2,1)S(1)}, u32[]{:S(2)}, u32[]{:S(2)}) collective-permute-start(bf16[4,128,256]{2,1,0:T(8,128)(2,1)S(1)} %collective-permute-done.10.front), channel_id=1, source_target_pairs={{0,8},{4,0},{8,16},{12,4},{16,24},{20,12},{24,28},{28,20},{1,9},{5... | collective-permute-start | bytes 786440 | tf_op jit(solution)/shard_map/ppermute | solution.py:303
  74.9 9.1 %collective-permute-start.13 = (bf16[4,128,256]{2,1,0:T(8,128)(2,1)S(1)}, bf16[4,128,256]{2,1,0:T(8,128)(2,1)S(1)}, u32[]{:S(2)}, u32[]{:S(2)}) collective-permute-start(bf16[4,128,256]{2,1,0:T(8,128)(2,1)S(1)} %collective-permute-done.11.back), channel_id=1, source_target_pairs={{0,4},{4,12},{8,0},{12,20},{16,8},{20,28},{24,16},{28,24},{1,5},{5... | collective-permute-start | bytes 786440 | tf_op jit(solution)/shard_map/ppermute | solution.py:303
  79.1 9.8 %collective-permute-start.35 = (bf16[4,128,256]{2,1,0:T(8,128)(2,1)S(1)}, bf16[4,128,256]{2,1,0:T(8,128)(2,1)S(1)}, u32[]{:S(2)}, u32[]{:S(2)}) collective-permute-start(bf16[4,128,256]{2,1,0:T(8,128)(2,1)S(1)} %collective-permute-done.33.front), channel_id=1, source_target_pairs={{0,8},{4,0},{8,16},{12,4},{16,24},{20,12},{24,28},{28,20},{1,9},{5... | collective-permute-start | bytes 786440 | tf_op jit(solution)/shard_map/ppermute | solution.py:303
  80.5 8.4 %collective-permute-start.36 = (bf16[4,128,256]{2,1,0:T(8,128)(2,1)S(1)}, bf16[4,128,256]{2,1,0:T(8,128)(2,1)S(1)}, u32[]{:S(2)}, u32[]{:S(2)}) collective-permute-start(bf16[4,128,256]{2,1,0:T(8,128)(2,1)S(1)} %collective-permute-done.34.back), channel_id=1, source_target_pairs={{0,4},{4,12},{8,0},{12,20},{16,8},{20,28},{24,16},{28,24},{1,5},{5... | collective-permute-start | bytes 786440 | tf_op jit(solution)/shard_map/ppermute | solution.py:303
  86.1 5.5 %collective-permute-start.14 = (f32[2,256,256]{2,1,0:T(8,128)S(1)}, f32[2,256,256]{2,1,0:T(8,128)S(1)}, u32[]{:S(2)}, u32[]{:S(2)}) collective-permute-start(f32[2,256,256]{2,1,0:T(8,128)S(1)} %get-tuple-element.141), channel_id=1, source_target_pairs={{0,1},{1,0},{2,3},{3,2},{4,5},{5,4},{6,7},{7,6},{8,9},{9,8},{10,11... | collective-permute-start | bytes 1572872 | tf_op jit(solution)/shard_map/ppermute | solution.py:292
  91.1 2.2 %collective-permute-start.37 = (f32[2,256,256]{2,1,0:T(8,128)S(1)}, f32[2,256,256]{2,1,0:T(8,128)S(1)}, u32[]{:S(2)}, u32[]{:S(2)}) collective-permute-start(f32[2,256,256]{2,1,0:T(8,128)S(1)} %get-tuple-element.185), channel_id=1, source_target_pairs={{0,1},{1,0},{2,3},{3,2},{4,5},{5,4},{6,7},{7,6},{8,9},{9,8},{10,11... | collective-permute-start | bytes 1572872 | tf_op jit(solution)/shard_map/ppermute | solution.py:292
  91.7 6.6 %collective-permute-start.15 = (s16[272,256]{1,0:T(8,128)(2,1)S(1)}, s16[272,256]{1,0:T(8,128)(2,1)S(1)}, u32[]{:S(2)}, u32[]{:S(2)}) collective-permute-start(s16[272,256]{1,0:T(8,128)(2,1)S(1)} %get-tuple-element.143), channel_id=1, source_target_pairs={{0,2},{1,3},{2,0},{3,1},{4,6},{5,7},{6,4},{7,5},{8,10},{9,11},{10,... | collective-permute-start | bytes 417800 | tf_op jit(solution)/shard_map/ppermute | solution.py:292
  93.4 8.1 %collective-permute-start.38 = (s16[272,256]{1,0:T(8,128)(2,1)S(1)}, s16[272,256]{1,0:T(8,128)(2,1)S(1)}, u32[]{:S(2)}, u32[]{:S(2)}) collective-permute-start(s16[272,256]{1,0:T(8,128)(2,1)S(1)} %get-tuple-element.187), channel_id=1, source_target_pairs={{0,2},{1,3},{2,0},{3,1},{4,6},{5,7},{6,4},{7,5},{8,10},{9,11},{10,... | collective-permute-start | bytes 417800 | tf_op jit(solution)/shard_map/ppermute | solution.py:292
  98.4 10.2 %collective-permute-start.16 = (bf16[256,256]{1,0:T(8,128)(2,1)S(1)}, bf16[256,256]{1,0:T(8,128)(2,1)S(1)}, u32[]{:S(2)}, u32[]{:S(2)}) collective-permute-start(bf16[256,256]{1,0:T(8,128)(2,1)S(1)} %shard_map.83.refs_0_), channel_id=1, source_target_pairs={{0,16},{1,17},{2,18},{3,19},{4,20},{5,21},{6,22},{7,23},{8,24},{9,... | collective-permute-start | bytes 393224 | tf_op jit(solution)/shard_map/ppermute | solution.py:292
  100.9 9.3 %collective-permute-start.17 = (bf16[256,256]{1,0:T(8,128)(2,1)S(1)}, bf16[256,256]{1,0:T(8,128)(2,1)S(1)}, u32[]{:S(2)}, u32[]{:S(2)}) collective-permute-start(bf16[256,256]{1,0:T(8,128)(2,1)S(1)} %shard_map.83.refs_0_), channel_id=1, source_target_pairs={{0,8},{1,9},{2,10},{3,11},{4,12},{5,13},{6,14},{7,15},{8,0},{9,1},... | collective-permute-start | bytes 393224 | tf_op jit(solution)/shard_map/ppermute | solution.py:292
  101.6 9.3 %collective-permute-start.39 = (bf16[256,256]{1,0:T(8,128)(2,1)S(1)}, bf16[256,256]{1,0:T(8,128)(2,1)S(1)}, u32[]{:S(2)}, u32[]{:S(2)}) collective-permute-start(bf16[256,256]{1,0:T(8,128)(2,1)S(1)} %shard_map.94.refs_0_), channel_id=1, source_target_pairs={{0,16},{1,17},{2,18},{3,19},{4,20},{5,21},{6,22},{7,23},{8,24},{9,... | collective-permute-start | bytes 393224 | tf_op jit(solution)/shard_map/ppermute | solution.py:292
  102.9 10.4 %collective-permute-start.40 = (bf16[256,256]{1,0:T(8,128)(2,1)S(1)}, bf16[256,256]{1,0:T(8,128)(2,1)S(1)}, u32[]{:S(2)}, u32[]{:S(2)}) collective-permute-start(bf16[256,256]{1,0:T(8,128)(2,1)S(1)} %shard_map.94.refs_0_), channel_id=1, source_target_pairs={{0,8},{1,9},{2,10},{3,11},{4,12},{5,13},{6,14},{7,15},{8,0},{9,1},... | collective-permute-start | bytes 393224 | tf_op jit(solution)/shard_map/ppermute | solution.py:292
  110.2 6.0 %collective-permute-start.18 = (bf16[256,256]{1,0:T(8,128)(2,1)S(1)}, bf16[256,256]{1,0:T(8,128)(2,1)S(1)}, u32[]{:S(2)}, u32[]{:S(2)}) collective-permute-start(bf16[256,256]{1,0:T(8,128)(2,1)S(1)} %collective-permute-done.16.refs_2_), channel_id=1, source_target_pairs={{0,8},{1,9},{2,10},{3,11},{4,12},{5,13},{6,14},{7,15},{8,0},{9,1},... | collective-permute-start | bytes 393224 | tf_op jit(solution)/shard_map/ppermute | solution.py:292
  113.4 7.4 %collective-permute-start.41 = (bf16[256,256]{1,0:T(8,128)(2,1)S(1)}, bf16[256,256]{1,0:T(8,128)(2,1)S(1)}, u32[]{:S(2)}, u32[]{:S(2)}) collective-permute-start(bf16[256,256]{1,0:T(8,128)(2,1)S(1)} %collective-permute-done.39.refs_2_), channel_id=1, source_target_pairs={{0,8},{1,9},{2,10},{3,11},{4,12},{5,13},{6,14},{7,15},{8,0},{9,1},... | collective-permute-start | bytes 393224 | tf_op jit(solution)/shard_map/ppermute | solution.py:292
  116.2 5.8 %collective-permute-start.42 = (bf16[256,256]{1,0:T(8,128)(2,1)S(1)}, bf16[256,256]{1,0:T(8,128)(2,1)S(1)}, u32[]{:S(2)}, u32[]{:S(2)}) collective-permute-start(bf16[256,256]{1,0:T(8,128)(2,1)S(1)} %get-tuple-element.149), channel_id=1, source_target_pairs={{0,1},{1,0},{2,3},{3,2},{4,5},{5,4},{6,7},{7,6},{8,9},{9,8},{10,11... | collective-permute-start | bytes 393224 | tf_op jit(solution)/shard_map/ppermute | solution.py:292
  116.3 7.3 %collective-permute-start.43 = (bf16[256,256]{1,0:T(8,128)(2,1)S(1)}, bf16[256,256]{1,0:T(8,128)(2,1)S(1)}, u32[]{:S(2)}, u32[]{:S(2)}) collective-permute-start(bf16[256,256]{1,0:T(8,128)(2,1)S(1)} %get-tuple-element.150), channel_id=1, source_target_pairs={{0,2},{1,3},{2,0},{3,1},{4,6},{5,7},{6,4},{7,5},{8,10},{9,11},{10,... | collective-permute-start | bytes 393224 | tf_op jit(solution)/shard_map/ppermute | solution.py:292
  117.9 7.0 %collective-permute-start.44 = (bf16[256,256]{1,0:T(8,128)(2,1)S(1)}, bf16[256,256]{1,0:T(8,128)(2,1)S(1)}, u32[]{:S(2)}, u32[]{:S(2)}) collective-permute-start(bf16[256,256]{1,0:T(8,128)(2,1)S(1)} %get-tuple-element.151), channel_id=1, source_target_pairs={{0,3},{1,2},{2,1},{3,0},{4,7},{5,6},{6,5},{7,4},{8,11},{9,10},{10,... | collective-permute-start | bytes 393224 | tf_op jit(solution)/shard_map/ppermute | solution.py:292
  118.2 9.4 %collective-permute-start.19 = (bf16[256,256]{1,0:T(8,128)(2,1)S(1)}, bf16[256,256]{1,0:T(8,128)(2,1)S(1)}, u32[]{:S(2)}, u32[]{:S(2)}) collective-permute-start(bf16[256,256]{1,0:T(8,128)(2,1)S(1)} %get-tuple-element.148.refs_0_), channel_id=1, source_target_pairs={{0,4},{1,5},{2,6},{3,7},{4,0},{5,1},{6,2},{7,3},{8,12},{9,13},{10,... | collective-permute-start | bytes 393224 | tf_op jit(solution)/shard_map/ppermute | solution.py:292
  120.8 8.7 %collective-permute-start.20 = (bf16[256,256]{1,0:T(8,128)(2,1)S(1)}, bf16[256,256]{1,0:T(8,128)(2,1)S(1)}, u32[]{:S(2)}, u32[]{:S(2)}) collective-permute-start(bf16[256,256]{1,0:T(8,128)(2,1)S(1)} %get-tuple-element.149), channel_id=1, source_target_pairs={{0,5},{1,4},{2,7},{3,6},{4,1},{5,0},{6,3},{7,2},{8,13},{9,12},{10,... | collective-permute-start | bytes 393224 | tf_op jit(solution)/shard_map/ppermute | solution.py:292
  122.1 8.5 %collective-permute-start.21 = (bf16[256,256]{1,0:T(8,128)(2,1)S(1)}, bf16[256,256]{1,0:T(8,128)(2,1)S(1)}, u32[]{:S(2)}, u32[]{:S(2)}) collective-permute-start(bf16[256,256]{1,0:T(8,128)(2,1)S(1)} %get-tuple-element.150), channel_id=1, source_target_pairs={{0,6},{1,7},{2,4},{3,5},{4,2},{5,3},{6,0},{7,1},{8,14},{9,15},{10,... | collective-permute-start | bytes 393224 | tf_op jit(solution)/shard_map/ppermute | solution.py:292
  123.6 9.7 %collective-permute-start.22 = (bf16[256,256]{1,0:T(8,128)(2,1)S(1)}, bf16[256,256]{1,0:T(8,128)(2,1)S(1)}, u32[]{:S(2)}, u32[]{:S(2)}) collective-permute-start(bf16[256,256]{1,0:T(8,128)(2,1)S(1)} %get-tuple-element.151), channel_id=1, source_target_pairs={{0,7},{1,6},{2,5},{3,4},{4,3},{5,2},{6,1},{7,0},{8,15},{9,14},{10,... | collective-permute-start | bytes 393224 | tf_op jit(solution)/shard_map/ppermute | solution.py:292
  125.7 8.9 %collective-permute-start.51 = (bf16[256,256]{1,0:T(8,128)(2,1)S(1)}, bf16[256,256]{1,0:T(8,128)(2,1)S(1)}, u32[]{:S(2)}, u32[]{:S(2)}) collective-permute-start(bf16[256,256]{1,0:T(8,128)(2,1)S(1)} %get-tuple-element.201), channel_id=1, source_target_pairs={{0,1},{1,0},{2,3},{3,2},{4,5},{5,4},{6,7},{7,6},{8,9},{9,8},{10,11... | collective-permute-start | bytes 393224 | tf_op jit(solution)/shard_map/ppermute | solution.py:292
  127.6 8.5 %collective-permute-start.52 = (bf16[256,256]{1,0:T(8,128)(2,1)S(1)}, bf16[256,256]{1,0:T(8,128)(2,1)S(1)}, u32[]{:S(2)}, u32[]{:S(2)}) collective-permute-start(bf16[256,256]{1,0:T(8,128)(2,1)S(1)} %get-tuple-element.202), channel_id=1, source_target_pairs={{0,2},{1,3},{2,0},{3,1},{4,6},{5,7},{6,4},{7,5},{8,10},{9,11},{10,... | collective-permute-start | bytes 393224 | tf_op jit(solution)/shard_map/ppermute | solution.py:292
  129.5 10.5 %collective-permute-start.53 = (bf16[256,256]{1,0:T(8,128)(2,1)S(1)}, bf16[256,256]{1,0:T(8,128)(2,1)S(1)}, u32[]{:S(2)}, u32[]{:S(2)}) collective-permute-start(bf16[256,256]{1,0:T(8,128)(2,1)S(1)} %get-tuple-element.203), channel_id=1, source_target_pairs={{0,3},{1,2},{2,1},{3,0},{4,7},{5,6},{6,5},{7,4},{8,11},{9,10},{10,... | collective-permute-start | bytes 393224 | tf_op jit(solution)/shard_map/ppermute | solution.py:292
  130.6 12.3 %collective-permute-start.48 = (bf16[256,256]{1,0:T(8,128)(2,1)S(1)}, bf16[256,256]{1,0:T(8,128)(2,1)S(1)}, u32[]{:S(2)}, u32[]{:S(2)}) collective-permute-start(bf16[256,256]{1,0:T(8,128)(2,1)S(1)} %get-tuple-element.201), channel_id=1, source_target_pairs={{0,5},{1,4},{2,7},{3,6},{4,1},{5,0},{6,3},{7,2},{8,13},{9,12},{10,... | collective-permute-start | bytes 393224 | tf_op jit(solution)/shard_map/ppermute | solution.py:292
  133.2 9.6 %collective-permute-start.47 = (bf16[256,256]{1,0:T(8,128)(2,1)S(1)}, bf16[256,256]{1,0:T(8,128)(2,1)S(1)}, u32[]{:S(2)}, u32[]{:S(2)}) collective-permute-start(bf16[256,256]{1,0:T(8,128)(2,1)S(1)} %get-tuple-element.200.refs_0_), channel_id=1, source_target_pairs={{0,4},{1,5},{2,6},{3,7},{4,0},{5,1},{6,2},{7,3},{8,12},{9,13},{10,... | collective-permute-start | bytes 393224 | tf_op jit(solution)/shard_map/ppermute | solution.py:292
  134.6 8.4 %collective-permute-start.49 = (bf16[256,256]{1,0:T(8,128)(2,1)S(1)}, bf16[256,256]{1,0:T(8,128)(2,1)S(1)}, u32[]{:S(2)}, u32[]{:S(2)}) collective-permute-start(bf16[256,256]{1,0:T(8,128)(2,1)S(1)} %get-tuple-element.202), channel_id=1, source_target_pairs={{0,6},{1,7},{2,4},{3,5},{4,2},{5,3},{6,0},{7,1},{8,14},{9,15},{10,... | collective-permute-start | bytes 393224 | tf_op jit(solution)/shard_map/ppermute | solution.py:292
  136.1 8.4 %collective-permute-start.50 = (bf16[256,256]{1,0:T(8,128)(2,1)S(1)}, bf16[256,256]{1,0:T(8,128)(2,1)S(1)}, u32[]{:S(2)}, u32[]{:S(2)}) collective-permute-start(bf16[256,256]{1,0:T(8,128)(2,1)S(1)} %get-tuple-element.203), channel_id=1, source_target_pairs={{0,7},{1,6},{2,5},{3,4},{4,3},{5,2},{6,1},{7,0},{8,15},{9,14},{10,... | collective-permute-start | bytes 393224 | tf_op jit(solution)/shard_map/ppermute | solution.py:292
  140.1 7.1 %collective-permute-start.45 = (f32[2,256,256]{2,1,0:T(8,128)S(1)}, f32[2,256,256]{2,1,0:T(8,128)S(1)}, u32[]{:S(2)}, u32[]{:S(2)}) collective-permute-start(f32[2,256,256]{2,1,0:T(8,128)S(1)} %get-tuple-element.197), channel_id=1, source_target_pairs={{0,1},{1,0},{2,3},{3,2},{4,5},{5,4},{6,7},{7,6},{8,9},{9,8},{10,11... | collective-permute-start | bytes 1572872 | tf_op jit(solution)/shard_map/ppermute | solution.py:292
  145.3 4.8 %collective-permute-start.54 = (f32[2,256,256]{2,1,0:T(8,128)S(1)}, f32[2,256,256]{2,1,0:T(8,128)S(1)}, u32[]{:S(2)}, u32[]{:S(2)}) collective-permute-start(f32[2,256,256]{2,1,0:T(8,128)S(1)} %get-tuple-element.206), channel_id=1, source_target_pairs={{0,1},{1,0},{2,3},{3,2},{4,5},{5,4},{6,7},{7,6},{8,9},{9,8},{10,11... | collective-permute-start | bytes 1572872 | tf_op jit(solution)/shard_map/ppermute | solution.py:292
  147.2 7.4 %collective-permute-start.46 = (s16[272,256]{1,0:T(8,128)(2,1)S(1)}, s16[272,256]{1,0:T(8,128)(2,1)S(1)}, u32[]{:S(2)}, u32[]{:S(2)}) collective-permute-start(s16[272,256]{1,0:T(8,128)(2,1)S(1)} %get-tuple-element.199), channel_id=1, source_target_pairs={{0,2},{1,3},{2,0},{3,1},{4,6},{5,7},{6,4},{7,5},{8,10},{9,11},{10,... | collective-permute-start | bytes 417800 | tf_op jit(solution)/shard_map/ppermute | solution.py:292
  150.2 7.2 %collective-permute-start.55 = (s16[272,256]{1,0:T(8,128)(2,1)S(1)}, s16[272,256]{1,0:T(8,128)(2,1)S(1)}, u32[]{:S(2)}, u32[]{:S(2)}) collective-permute-start(s16[272,256]{1,0:T(8,128)(2,1)S(1)} %get-tuple-element.208), channel_id=1, source_target_pairs={{0,2},{1,3},{2,0},{3,1},{4,6},{5,7},{6,4},{7,5},{8,10},{9,11},{10,... | collective-permute-start | bytes 417800 | tf_op jit(solution)/shard_map/ppermute | solution.py:292
where the time goes:
time: 160 us; the launch traced here: 158 us
  starting transfers between devices  63.2 us (40%)
  Pallas kernels  51.5 us (32%)
  waiting for transfers between devices  33.3 us (21%)
  local copies, waits for them, and re-layouts  8.36 us (5%)
    pallas_call x18, Pallas kernels, past_call(): pl.pallas_call(functools.partial(past_kernel, number, carried is None, st...  46.9 us
    ppermute x28, starting transfers between devices, send(): return lax.ppermute(value, BOTH, pairs)  33.6 us
    ppermute x28, starting transfers between devices, around(): return lax.ppermute(value, 'row', pairs)  29.6 us
    ppermute x28, waiting for transfers between devices, send(): return lax.ppermute(value, BOTH, pairs)  24.5 us
    ppermute x28, waiting for transfers between devices, around(): return lax.ppermute(value, 'row', pairs)  8.84 us
    unnamed x12, local copies, waits for them, and re-layouts  6.98 us
    pallas_call x4, Pallas kernels, recent_call(): pl.pallas_call(functools.partial(recent_kernel, fanout, beside, ending, l...  3.3 us
  transfers between devices with their start and end apart: 56, of which 21 were waited for; matrix products, arithmetic and copies ran while one was open for 0% of the time, Pallas kernels for 32%

commit v1 on v0

--- a/solution.py
+++ b/solution.py
@@ -10,7 +10,7 @@
 BOTH = ("row", "col")
 VMEM_BYTES = 8 * 1024 * 1024
 TILE = 16
-ROWS = 256
+ROWS = 512
 SHORT = pl.CostEstimate(flops=0, bytes_accessed=0, transcendentals=0)
 LANES = 128
 LEVELS = 32000.0

time: 160 us -> 154 us (0.963); the launches traced: 158 us -> 155 us
  starting transfers between devices: 63.2 us -> 54.9 us
  waiting for transfers between devices: 33.3 us -> 38.5 us
    ppermute x28, starting transfers between devices: 33.6 us -> 25.3 us  [send(): return lax.ppermute(value, BOTH, pairs)]
    pallas_call x18, Pallas kernels: 46.9 us -> 40.5 us  [past_call(): pl.pallas_call(functools.partial(past_kernel, number, carried is None, st...]
    pallas_call x4, Pallas kernels: 3.3 us -> 9.1 us  [recent_call(): pl.pallas_call(functools.partial(recent_kernel, fanout, beside, ending, l...]
    ppermute x28, waiting for transfers between devices: 8.84 us -> 12 us  [around(): return lax.ppermute(value, 'row', pairs)]
    ppermute x28, waiting for transfers between devices: 24.5 us -> 26.5 us  [send(): return lax.ppermute(value, BOTH, pairs)]
  transfers between devices with their start and end apart: 56 -> 56, of which waited for: 21 -> 24; matrix products, arithmetic and copies ran while one was open for 0% -> 0% of each run, Pallas kernels for 32% -> 33%
where the time goes in v1:
time: 154 us; the launch traced here: 155 us
  starting transfers between devices  54.9 us (36%)
  Pallas kernels  51 us (33%)
  waiting for transfers between devices  38.5 us (25%)
  local copies, waits for them, and re-layouts  8.36 us (5%)
    pallas_call x18, Pallas kernels, past_call(): pl.pallas_call(functools.partial(past_kernel, number, carried is None, st...  40.5 us
    ppermute x28, starting transfers between devices, around(): return lax.ppermute(value, 'row', pairs)  29.6 us
    ppermute x28, waiting for transfers between devices, send(): return lax.ppermute(value, BOTH, pairs)  26.5 us
    ppermute x28, starting transfers between devices, send(): return lax.ppermute(value, BOTH, pairs)  25.3 us
    ppermute x28, waiting for transfers between devices, around(): return lax.ppermute(value, 'row', pairs)  12 us
    pallas_call x4, Pallas kernels, recent_call(): pl.pallas_call(functools.partial(recent_kernel, fanout, beside, ending, l...  9.1 us
    unnamed x12, local copies, waits for them, and re-layouts  6.98 us
  transfers between devices with their start and end apart: 56, of which 24 were waited for; matrix products, arithmetic and copies ran while one was open for 0% of the time, Pallas kernels for 33%

profile of v1, /device:TPU:0, one launch (start us, length us, event | category | flops | bytes accessed | tf_op | source)
XLA Modules:
  0.0 154.9 jit_solution(1564481873260112969)
XLA Ops:
  0.0 1.3 fusion.1
  1.3 3.1 %collective-permute-start = (bf16[4,128,256]{2,1,0:T(8,128)(2,1)S(1)}, bf16[4,128,256]{2,1,0:T(8,128)(2,1)S(1)}, u32[]{:S(2)}, u32[]{:S(2)}) collective-permute-start(bf16[4,128,256]{2,1,0:T(8,128)(2,1)S(1)} %get-tuple-element.212.front), channel_id=1, source_target_pairs={{0,8},{4,0},{8,16},{12,4},{16,24},{20,12},{24,28},{28,20},{1,9},{5... | collective-permute-start | bytes 786440 | tf_op jit(solution)/shard_map/ppermute | solution.py:303
  4.4 2.0 %collective-permute-start.23 = (bf16[4,128,256]{2,1,0:T(8,128)(2,1)S(1)}, bf16[4,128,256]{2,1,0:T(8,128)(2,1)S(1)}, u32[]{:S(2)}, u32[]{:S(2)}) collective-permute-start(bf16[4,128,256]{2,1,0:T(8,128)(2,1)S(1)} %get-tuple-element.214.front), channel_id=1, source_target_pairs={{0,8},{4,0},{8,16},{12,4},{16,24},{20,12},{24,28},{28,20},{1,9},{5... | collective-permute-start | bytes 786440 | tf_op jit(solution)/shard_map/ppermute | solution.py:303
  6.4 7.0 %copy-done = bf16[5,1024,2048]{2,1,0:T(8,128)(2,1)S(1)} copy-done((bf16[5,1024,2048]{2,1,0:T(8,128)(2,1)S(1)}, bf16[5,1024,2048]{2,1,0:T(8,128)(2,1)}, u32[]{:S(2)}) %copy-start) | copy-done | bytes 20971544
  13.8 2.1 %collective-permute-start.2 = (bf16[4,128,256]{2,1,0:T(8,128)(2,1)S(1)}, bf16[4,128,256]{2,1,0:T(8,128)(2,1)S(1)}, u32[]{:S(2)}, u32[]{:S(2)}) collective-permute-start(bf16[4,128,256]{2,1,0:T(8,128)(2,1)S(1)} %collective-permute-done.front), channel_id=1, source_target_pairs={{0,8},{4,0},{8,16},{12,4},{16,24},{20,12},{24,28},{28,20},{1,9},{5... | collective-permute-start | bytes 786440 | tf_op jit(solution)/shard_map/ppermute | solution.py:303
  16.9 1.6 %collective-permute-done.24.back = bf16[4,128,256]{2,1,0:T(8,128)(2,1)S(1)} collective-permute-done((bf16[4,128,256]{2,1,0:T(8,128)(2,1)S(1)}, bf16[4,128,256]{2,1,0:T(8,128)(2,1)S(1)}, u32[]{:S(2)}, u32[]{:S(2)}) %collective-permute-start.24) | collective-permute-done | bytes 262176 | tf_op jit(solution)/shard_map/ppermute | solution.py:303
  18.6 1.6 %collective-permute-start.25 = (bf16[4,128,256]{2,1,0:T(8,128)(2,1)S(1)}, bf16[4,128,256]{2,1,0:T(8,128)(2,1)S(1)}, u32[]{:S(2)}, u32[]{:S(2)}) collective-permute-start(bf16[4,128,256]{2,1,0:T(8,128)(2,1)S(1)} %collective-permute-done.23.front), channel_id=1, source_target_pairs={{0,8},{4,0},{8,16},{12,4},{16,24},{20,12},{24,28},{28,20},{1,9},{5... | collective-permute-start | bytes 786440 | tf_op jit(solution)/shard_map/ppermute | solution.py:303
  21.3 2.4 %shard_map.74 = (f32[1024,512]{1,0:T(8,128)S(1)}, f32[8,128]{1,0:T(8,128)S(1)}) custom-call(s32[5]{0:T(128)S(1)} %bitcast.34, s32[1]{0:T(128)} %bitcast.8.tile, bf16[5,1024,2048]{2,1,0:T(8,128)(2,1)S(1)} %copy-done.1, bf16[4,128,256]{2,1,0:T(8,128)(2,1)S(1)} %get-tuple-element.212.front, bf16[4,128,256]{2,1,0:T(8,128)(2,1)S(1)} %get-tuple-element.211.back, ...), custom_call_target="tpu_custom_call" | custom-call | flops 1342177280 | bytes 2621440 | tf_op jit(solution)/shard_map/pallas_call | solution.py:145
  23.7 1.4 collective-permute-done.3.back
  25.1 1.6 %collective-permute-start.4 = (bf16[4,128,256]{2,1,0:T(8,128)(2,1)S(1)}, bf16[4,128,256]{2,1,0:T(8,128)(2,1)S(1)}, u32[]{:S(2)}, u32[]{:S(2)}) collective-permute-start(bf16[4,128,256]{2,1,0:T(8,128)(2,1)S(1)} %collective-permute-done.2.front), channel_id=1, source_target_pairs={{0,8},{4,0},{8,16},{12,4},{16,24},{20,12},{24,28},{28,20},{1,9},{5... | collective-permute-start | bytes 786440 | tf_op jit(solution)/shard_map/ppermute | solution.py:303
  27.1 2.4 %shard_map.85 = (f32[1024,512]{1,0:T(8,128)S(1)}, f32[8,128]{1,0:T(8,128)S(1)}) custom-call(s32[5]{0:T(128)S(1)} %bitcast.35, s32[1]{0:T(128)} %bitcast.16.tile, bf16[5,1024,2048]{2,1,0:T(8,128)(2,1)S(1)} %copy-done.1, bf16[4,128,256]{2,1,0:T(8,128)(2,1)S(1)} %get-tuple-element.214.front, bf16[4,128,256]{2,1,0:T(8,128)(2,1)S(1)} %get-tuple-element.213.back, ...), custom_call_target="tpu_custom_call" | custom-call | flops 1342177280 | bytes 2621440 | tf_op jit(solution)/shard_map/pallas_call | solution.py:145
  29.5 1.2 collective-permute-done.26.back
  30.7 1.6 %collective-permute-start.27 = (bf16[4,128,256]{2,1,0:T(8,128)(2,1)S(1)}, bf16[4,128,256]{2,1,0:T(8,128)(2,1)S(1)}, u32[]{:S(2)}, u32[]{:S(2)}) collective-permute-start(bf16[4,128,256]{2,1,0:T(8,128)(2,1)S(1)} %collective-permute-done.25.front), channel_id=1, source_target_pairs={{0,8},{4,0},{8,16},{12,4},{16,24},{20,12},{24,28},{28,20},{1,9},{5... | collective-permute-start | bytes 786440 | tf_op jit(solution)/shard_map/ppermute | solution.py:303
  32.8 2.4 %shard_map.75 = (f32[1024,512]{1,0:T(8,128)S(1)}, f32[8,128]{1,0:T(8,128)S(1)}) custom-call(s32[5]{0:T(128)S(1)} %bitcast.36, s32[1]{0:T(128)} %bitcast.9.tile, bf16[5,1024,2048]{2,1,0:T(8,128)(2,1)S(1)} %copy-done.1, bf16[4,128,256]{2,1,0:T(8,128)(2,1)S(1)} %collective-permute-done.front, ...), custom_call_target="tpu_custom_call", output_to_operand_aliasing={{0}: (6, {})} | custom-call | flops 1342177280 | bytes 2621440 | tf_op jit(solution)/shard_map/pallas_call | solution.py:145
  35.1 2.4 %shard_map.76 = (f32[1024,512]{1,0:T(8,128)S(1)}, f32[8,128]{1,0:T(8,128)S(1)}) custom-call(s32[5]{0:T(128)S(1)} %bitcast.37, s32[1]{0:T(128)} %bitcast.10.tile, bf16[5,1024,2048]{2,1,0:T(8,128)(2,1)S(1)} %copy-done.1, bf16[4,128,256]{2,1,0:T(8,128)(2,1)S(1)} %collective-permute-done.2.front, ...), custom_call_target="tpu_custom_call", output_to_operand_aliasing={{0}: (6, {})} | custom-call | flops 1342177280 | bytes 2621440 | tf_op jit(solution)/shard_map/pallas_call | solution.py:145
  37.6 1.6 %collective-permute-start.6 = (bf16[4,128,256]{2,1,0:T(8,128)(2,1)S(1)}, bf16[4,128,256]{2,1,0:T(8,128)(2,1)S(1)}, u32[]{:S(2)}, u32[]{:S(2)}) collective-permute-start(bf16[4,128,256]{2,1,0:T(8,128)(2,1)S(1)} %collective-permute-done.4.front), channel_id=1, source_target_pairs={{0,8},{4,0},{8,16},{12,4},{16,24},{20,12},{24,28},{28,20},{1,9},{5... | collective-permute-start | bytes 786440 | tf_op jit(solution)/shard_map/ppermute | solution.py:303
  39.7 2.4 %shard_map.86 = (f32[1024,512]{1,0:T(8,128)S(1)}, f32[8,128]{1,0:T(8,128)S(1)}) custom-call(s32[5]{0:T(128)S(1)} %bitcast.38, s32[1]{0:T(128)} %bitcast.17.tile, bf16[5,1024,2048]{2,1,0:T(8,128)(2,1)S(1)} %copy-done.1, bf16[4,128,256]{2,1,0:T(8,128)(2,1)S(1)} %collective-permute-done.23.front, ...), custom_call_target="tpu_custom_call", output_to_operand_aliasing={{0}: (6, {})} | custom-call | flops 1342177280 | bytes 2621440 | tf_op jit(solution)/shard_map/pallas_call | solution.py:145
  42.1 2.4 %shard_map.87 = (f32[1024,512]{1,0:T(8,128)S(1)}, f32[8,128]{1,0:T(8,128)S(1)}) custom-call(s32[5]{0:T(128)S(1)} %bitcast.39, s32[1]{0:T(128)} %bitcast.18.tile, bf16[5,1024,2048]{2,1,0:T(8,128)(2,1)S(1)} %copy-done.1, bf16[4,128,256]{2,1,0:T(8,128)(2,1)S(1)} %collective-permute-done.25.front, ...), custom_call_target="tpu_custom_call", output_to_operand_aliasing={{0}: (6, {})} | custom-call | flops 1342177280 | bytes 2621440 | tf_op jit(solution)/shard_map/pallas_call | solution.py:145
  44.5 1.6 %collective-permute-start.29 = (bf16[4,128,256]{2,1,0:T(8,128)(2,1)S(1)}, bf16[4,128,256]{2,1,0:T(8,128)(2,1)S(1)}, u32[]{:S(2)}, u32[]{:S(2)}) collective-permute-start(bf16[4,128,256]{2,1,0:T(8,128)(2,1)S(1)} %collective-permute-done.27.front), channel_id=1, source_target_pairs={{0,8},{4,0},{8,16},{12,4},{16,24},{20,12},{24,28},{28,20},{1,9},{5... | collective-permute-start | bytes 786440 | tf_op jit(solution)/shard_map/ppermute | solution.py:303
  46.6 2.4 %shard_map.77 = (f32[1024,512]{1,0:T(8,128)S(1)}, f32[8,128]{1,0:T(8,128)S(1)}) custom-call(s32[5]{0:T(128)S(1)} %bitcast.40, s32[1]{0:T(128)} %bitcast.11.tile, bf16[5,1024,2048]{2,1,0:T(8,128)(2,1)S(1)} %copy-done.1, bf16[4,128,256]{2,1,0:T(8,128)(2,1)S(1)} %collective-permute-done.4.front, ...), custom_call_target="tpu_custom_call", output_to_operand_aliasing={{0}: (6, {})} | custom-call | flops 1342177280 | bytes 2621440 | tf_op jit(solution)/shard_map/pallas_call | solution.py:145
  49.0 1.7 %collective-permute-start.8 = (bf16[4,128,256]{2,1,0:T(8,128)(2,1)S(1)}, bf16[4,128,256]{2,1,0:T(8,128)(2,1)S(1)}, u32[]{:S(2)}, u32[]{:S(2)}) collective-permute-start(bf16[4,128,256]{2,1,0:T(8,128)(2,1)S(1)} %collective-permute-done.6.front), channel_id=1, source_target_pairs={{0,8},{4,0},{8,16},{12,4},{16,24},{20,12},{24,28},{28,20},{1,9},{5... | collective-permute-start | bytes 786440 | tf_op jit(solution)/shard_map/ppermute | solution.py:303
  51.1 2.4 %shard_map.88 = (f32[1024,512]{1,0:T(8,128)S(1)}, f32[8,128]{1,0:T(8,128)S(1)}) custom-call(s32[5]{0:T(128)S(1)} %bitcast.41, s32[1]{0:T(128)} %bitcast.19.tile, bf16[5,1024,2048]{2,1,0:T(8,128)(2,1)S(1)} %copy-done.1, bf16[4,128,256]{2,1,0:T(8,128)(2,1)S(1)} %collective-permute-done.27.front, ...), custom_call_target="tpu_custom_call", output_to_operand_aliasing={{0}: (6, {})} | custom-call | flops 1342177280 | bytes 2621440 | tf_op jit(solution)/shard_map/pallas_call | solution.py:145
  53.8 1.6 %collective-permute-done.30.back = bf16[4,128,256]{2,1,0:T(8,128)(2,1)S(1)} collective-permute-done((bf16[4,128,256]{2,1,0:T(8,128)(2,1)S(1)}, bf16[4,128,256]{2,1,0:T(8,128)(2,1)S(1)}, u32[]{:S(2)}, u32[]{:S(2)}) %collective-permute-start.30) | collective-permute-done | bytes 262176 | tf_op jit(solution)/shard_map/ppermute | solution.py:303
  55.4 1.5 collective-permute-start.31
  57.4 2.4 %shard_map.78 = (f32[1024,512]{1,0:T(8,128)S(1)}, f32[8,128]{1,0:T(8,128)S(1)}) custom-call(s32[5]{0:T(128)S(1)} %bitcast.42, s32[1]{0:T(128)} %bitcast.12.tile, bf16[5,1024,2048]{2,1,0:T(8,128)(2,1)S(1)} %copy-done.1, bf16[4,128,256]{2,1,0:T(8,128)(2,1)S(1)} %collective-permute-done.6.front, ...), custom_call_target="tpu_custom_call", output_to_operand_aliasing={{0}: (6, {})} | custom-call | flops 1342177280 | bytes 2621440 | tf_op jit(solution)/shard_map/pallas_call | solution.py:145
  61.0 1.5 collective-permute-start.10
  63.0 2.4 %shard_map.89 = (f32[1024,512]{1,0:T(8,128)S(1)}, f32[8,128]{1,0:T(8,128)S(1)}) custom-call(s32[5]{0:T(128)S(1)} %bitcast.43, s32[1]{0:T(128)} %bitcast.20.tile, bf16[5,1024,2048]{2,1,0:T(8,128)(2,1)S(1)} %copy-done.1, bf16[4,128,256]{2,1,0:T(8,128)(2,1)S(1)} %collective-permute-done.29.front, ...), custom_call_target="tpu_custom_call", output_to_operand_aliasing={{0}: (6, {})} | custom-call | flops 1342177280 | bytes 2621440 | tf_op jit(solution)/shard_map/pallas_call | solution.py:145
  66.6 1.5 collective-permute-start.33
  68.7 2.4 %shard_map.79 = (f32[1024,512]{1,0:T(8,128)S(1)}, f32[8,128]{1,0:T(8,128)S(1)}) custom-call(s32[5]{0:T(128)S(1)} %bitcast.44, s32[1]{0:T(128)} %bitcast.13.tile, bf16[5,1024,2048]{2,1,0:T(8,128)(2,1)S(1)} %copy-done.1, bf16[4,128,256]{2,1,0:T(8,128)(2,1)S(1)} %collective-permute-done.8.front, ...), custom_call_target="tpu_custom_call", output_to_operand_aliasing={{0}: (6, {})} | custom-call | flops 1342177280 | bytes 2621440 | tf_op jit(solution)/shard_map/pallas_call | solution.py:145
  71.1 1.2 collective-permute-done.11.back
  72.2 1.5 collective-permute-start.12
  74.4 2.4 %shard_map.90 = (f32[1024,512]{1,0:T(8,128)S(1)}, f32[8,128]{1,0:T(8,128)S(1)}) custom-call(s32[5]{0:T(128)S(1)} %bitcast.45, s32[1]{0:T(128)} %bitcast.21.tile, bf16[5,1024,2048]{2,1,0:T(8,128)(2,1)S(1)} %copy-done.1, bf16[4,128,256]{2,1,0:T(8,128)(2,1)S(1)} %collective-permute-done.31.front, ...), custom_call_target="tpu_custom_call", output_to_operand_aliasing={{0}: (6, {})} | custom-call | flops 1342177280 | bytes 2621440 | tf_op jit(solution)/shard_map/pallas_call | solution.py:145
  77.9 1.5 collective-permute-start.35
  79.9 2.4 %shard_map.80 = (f32[1024,512]{1,0:T(8,128)S(1)}, f32[8,128]{1,0:T(8,128)S(1)}) custom-call(s32[5]{0:T(128)S(1)} %bitcast.46, s32[1]{0:T(128)} %bitcast.14.tile, bf16[5,1024,2048]{2,1,0:T(8,128)(2,1)S(1)} %copy-done.1, bf16[4,128,256]{2,1,0:T(8,128)(2,1)S(1)} %collective-permute-done.10.front, ...), custom_call_target="tpu_custom_call", output_to_operand_aliasing={{0}: (6, {})} | custom-call | flops 1342177280 | bytes 2621440 | tf_op jit(solution)/shard_map/pallas_call | solution.py:145
  82.4 1.8 %shard_map.81 = (f32[2,256,256]{2,1,0:T(8,128)S(1)}, f32[2,256,256]{2,1,0:T(8,128)S(1)}) custom-call(s32[5]{0:T(128)S(1)} %bitcast.47, s32[1]{0:T(128)} %bitcast.15.tile, bf16[5,1024,2048]{2,1,0:T(8,128)(2,1)S(1)} %copy-done.1, bf16[4,128,256]{2,1,0:T(8,128)(2,1)S(1)} %collective-permute-done.12.front, ...), custom_call_target="tpu_custom_call" | custom-call | flops 671088640 | bytes 2621440 | tf_op jit(solution)/shard_map/pallas_call | solution.py:145
  84.2 2.4 %shard_map.91 = (f32[1024,512]{1,0:T(8,128)S(1)}, f32[8,128]{1,0:T(8,128)S(1)}) custom-call(s32[5]{0:T(128)S(1)} %bitcast.48, s32[1]{0:T(128)} %bitcast.22.tile, bf16[5,1024,2048]{2,1,0:T(8,128)(2,1)S(1)} %copy-done.1, bf16[4,128,256]{2,1,0:T(8,128)(2,1)S(1)} %collective-permute-done.33.front, ...), custom_call_target="tpu_custom_call", output_to_operand_aliasing={{0}: (6, {})} | custom-call | flops 1342177280 | bytes 2621440 | tf_op jit(solution)/shard_map/pallas_call | solution.py:145
  86.7 1.8 %shard_map.92 = (f32[2,256,256]{2,1,0:T(8,128)S(1)}, f32[2,256,256]{2,1,0:T(8,128)S(1)}) custom-call(s32[5]{0:T(128)S(1)} %bitcast.49, s32[1]{0:T(128)} %bitcast.23.tile, bf16[5,1024,2048]{2,1,0:T(8,128)(2,1)S(1)} %copy-done.1, bf16[4,128,256]{2,1,0:T(8,128)(2,1)S(1)} %collective-permute-done.35.front, ...), custom_call_target="tpu_custom_call" | custom-call | flops 671088640 | bytes 2621440 | tf_op jit(solution)/shard_map/pallas_call | solution.py:145
  89.1 1.6 %collective-permute-start.15 = (s16[272,256]{1,0:T(8,128)(2,1)S(1)}, s16[272,256]{1,0:T(8,128)(2,1)S(1)}, u32[]{:S(2)}, u32[]{:S(2)}) collective-permute-start(s16[272,256]{1,0:T(8,128)(2,1)S(1)} %get-tuple-element.143), channel_id=1, source_target_pairs={{0,2},{1,3},{2,0},{3,1},{4,6},{5,7},{6,4},{7,5},{8,10},{9,11},{10,... | collective-permute-start | bytes 417800 | tf_op jit(solution)/shard_map/ppermute | solution.py:292
  90.8 1.4 collective-permute-start.38
  92.2 3.5 %collective-permute-done.15.got = s16[272,256]{1,0:T(8,128)(2,1)S(1)} collective-permute-done((s16[272,256]{1,0:T(8,128)(2,1)S(1)}, s16[272,256]{1,0:T(8,128)(2,1)S(1)}, u32[]{:S(2)}, u32[]{:S(2)}) %collective-permute-start.15) | collective-permute-done | bytes 139296 | tf_op jit(solution)/shard_map/ppermute | solution.py:292
  95.8 2.6 %collective-permute-start.16 = (bf16[256,256]{1,0:T(8,128)(2,1)S(1)}, bf16[256,256]{1,0:T(8,128)(2,1)S(1)}, u32[]{:S(2)}, u32[]{:S(2)}) collective-permute-start(bf16[256,256]{1,0:T(8,128)(2,1)S(1)} %shard_map.83.refs_0_), channel_id=1, source_target_pairs={{0,16},{1,17},{2,18},{3,19},{4,20},{5,21},{6,22},{7,23},{8,24},{9,... | collective-permute-start | bytes 393224 | tf_op jit(solution)/shard_map/ppermute | solution.py:292
  98.4 1.5 collective-permute-start.17
  100.5 1.5 collective-permute-start.40
  102.0 3.5 %collective-permute-done.16.refs_2_ = bf16[256,256]{1,0:T(8,128)(2,1)S(1)} collective-permute-done((bf16[256,256]{1,0:T(8,128)(2,1)S(1)}, bf16[256,256]{1,0:T(8,128)(2,1)S(1)}, u32[]{:S(2)}, u32[]{:S(2)}) %collective-permute-start.16) | collective-permute-done | bytes 131104 | tf_op jit(solution)/shard_map/ppermute | solution.py:292
  105.4 2.3 %collective-permute-done.17.refs_1_ = bf16[256,256]{1,0:T(8,128)(2,1)S(1)} collective-permute-done((bf16[256,256]{1,0:T(8,128)(2,1)S(1)}, bf16[256,256]{1,0:T(8,128)(2,1)S(1)}, u32[]{:S(2)}, u32[]{:S(2)}) %collective-permute-start.17) | collective-permute-done | bytes 131104 | tf_op jit(solution)/shard_map/ppermute | solution.py:292
  108.1 2.7 %collective-permute-done.40.refs_1_ = bf16[256,256]{1,0:T(8,128)(2,1)S(1)} collective-permute-done((bf16[256,256]{1,0:T(8,128)(2,1)S(1)}, bf16[256,256]{1,0:T(8,128)(2,1)S(1)}, u32[]{:S(2)}, u32[]{:S(2)}) %collective-permute-start.40) | collective-permute-done | bytes 131104 | tf_op jit(solution)/shard_map/ppermute | solution.py:292
  110.7 2.5 %collective-permute-start.41 = (bf16[256,256]{1,0:T(8,128)(2,1)S(1)}, bf16[256,256]{1,0:T(8,128)(2,1)S(1)}, u32[]{:S(2)}, u32[]{:S(2)}) collective-permute-start(bf16[256,256]{1,0:T(8,128)(2,1)S(1)} %collective-permute-done.39.refs_2_), channel_id=1, source_target_pairs={{0,8},{1,9},{2,10},{3,11},{4,12},{5,13},{6,14},{7,15},{8,0},{9,1},... | collective-permute-start | bytes 393224 | tf_op jit(solution)/shard_map/ppermute | solution.py:292
  113.7 1.6 %collective-permute-start.43 = (bf16[256,256]{1,0:T(8,128)(2,1)S(1)}, bf16[256,256]{1,0:T(8,128)(2,1)S(1)}, u32[]{:S(2)}, u32[]{:S(2)}) collective-permute-start(bf16[256,256]{1,0:T(8,128)(2,1)S(1)} %get-tuple-element.150), channel_id=1, source_target_pairs={{0,2},{1,3},{2,0},{3,1},{4,6},{5,7},{6,4},{7,5},{8,10},{9,11},{10,... | collective-permute-start | bytes 393224 | tf_op jit(solution)/shard_map/ppermute | solution.py:292
  116.0 1.7 %shard_map.96.refs_4_ = f32[1024,256]{1,0:T(8,128)S(1)} custom-call(s32[5]{0:T(128)S(1)} %bitcast.50, s32[1]{0:T(128)} %bitcast.24.tile, bf16[5,1024,2048]{2,1,0:T(8,128)(2,1)S(1)} %copy-done.1, bf16[4,128,256]{2,1,0:T(8,128)(2,1)S(1)} %collective-permute-done.12.front, bf16[4,128,256]{2,1,0:T(8,128)(2,1)S(1)} %collective-permute-done.13.back, ...), custom_call_target="tpu_custom_call" | custom-call | flops 671088640 | bytes 2621440 | tf_op jit(solution)/shard_map/pallas_call | solution.py:145
  117.8 1.2 collective-permute-start.20
  119.3 1.5 collective-permute-start.21
  120.8 1.3 collective-permute-start.22
  122.1 2.3 %shard_map.97.refs_4_ = f32[1024,256]{1,0:T(8,128)S(1)} custom-call(s32[5]{0:T(128)S(1)} %bitcast.51, s32[1]{0:T(128)} %bitcast.25.tile, bf16[5,1024,2048]{2,1,0:T(8,128)(2,1)S(1)} %copy-done.1, bf16[256,256]{1,0:T(8,128)(2,1)S(1)} %get-tuple-element.148.refs_0_, bf16[256,256]{1,0:T(8,128)(2,1)S(1)} %collective-permute-done.42.refs_1_, ...), custom_call_target="tpu_custom_call" | custom-call | tf_op jit(solution)/shard_map/pallas_call | solution.py:267
  124.5 1.9 %collective-permute-start.52 = (bf16[256,256]{1,0:T(8,128)(2,1)S(1)}, bf16[256,256]{1,0:T(8,128)(2,1)S(1)}, u32[]{:S(2)}, u32[]{:S(2)}) collective-permute-start(bf16[256,256]{1,0:T(8,128)(2,1)S(1)} %get-tuple-element.202), channel_id=1, source_target_pairs={{0,2},{1,3},{2,0},{3,1},{4,6},{5,7},{6,4},{7,5},{8,10},{9,11},{10,... | collective-permute-start | bytes 393224 | tf_op jit(solution)/shard_map/ppermute | solution.py:292
  126.4 2.0 %collective-permute-done.21.refs_2_ = bf16[256,256]{1,0:T(8,128)(2,1)S(1)} collective-permute-done((bf16[256,256]{1,0:T(8,128)(2,1)S(1)}, bf16[256,256]{1,0:T(8,128)(2,1)S(1)}, u32[]{:S(2)}, u32[]{:S(2)}) %collective-permute-start.21) | collective-permute-done | bytes 131104 | tf_op jit(solution)/shard_map/ppermute | solution.py:292
  128.4 1.9 %collective-permute-done.22.refs_3_ = bf16[256,256]{1,0:T(8,128)(2,1)S(1)} collective-permute-done((bf16[256,256]{1,0:T(8,128)(2,1)S(1)}, bf16[256,256]{1,0:T(8,128)(2,1)S(1)}, u32[]{:S(2)}, u32[]{:S(2)}) %collective-permute-start.22) | collective-permute-done | bytes 131104 | tf_op jit(solution)/shard_map/ppermute | solution.py:292
  130.3 1.3 collective-permute-start.47
  134.1 1.7 %shard_map.101.refs_4_ = f32[1024,256]{1,0:T(8,128)S(1)} custom-call(s32[5]{0:T(128)S(1)} %bitcast.52, s32[1]{0:T(128)} %bitcast.27.tile, bf16[5,1024,2048]{2,1,0:T(8,128)(2,1)S(1)} %copy-done.1, bf16[4,128,256]{2,1,0:T(8,128)(2,1)S(1)} %collective-permute-done.35.front, bf16[4,128,256]{2,1,0:T(8,128)(2,1)S(1)} %collective-permute-done.36.back, ...), custom_call_target="tpu_custom_call" | custom-call | flops 671088640 | bytes 2621440 | tf_op jit(solution)/shard_map/pallas_call | solution.py:145
  135.9 2.3 %shard_map.98 = (f32[2,256,256]{2,1,0:T(8,128)S(1)}, f32[2,256,256]{2,1,0:T(8,128)S(1)}) custom-call(s32[5]{0:T(128)S(1)} %bitcast.53, s32[1]{0:T(128)} %bitcast.26.tile, bf16[5,1024,2048]{2,1,0:T(8,128)(2,1)S(1)} %copy-done.1, bf16[256,256]{1,0:T(8,128)(2,1)S(1)} %collective-permute-done.19.refs_0_, bf16[256,256]{1,0:T(8,128)(2,1)S(1)} %collective-permute-done.20.refs_1_, ...), custom_call_target="tpu_custom_call" | custom-call | tf_op jit(solution)/shard_map/pallas_call | solution.py:267
  138.2 2.3 %shard_map.102.refs_4_ = f32[1024,256]{1,0:T(8,128)S(1)} custom-call(s32[5]{0:T(128)S(1)} %bitcast.54, s32[1]{0:T(128)} %bitcast.28.tile, bf16[5,1024,2048]{2,1,0:T(8,128)(2,1)S(1)} %copy-done.1, bf16[256,256]{1,0:T(8,128)(2,1)S(1)} %get-tuple-element.200.refs_0_, bf16[256,256]{1,0:T(8,128)(2,1)S(1)} %collective-permute-done.51.refs_1_, ...), custom_call_target="tpu_custom_call" | custom-call | tf_op jit(solution)/shard_map/pallas_call | solution.py:267
  140.5 1.8 %collective-permute-done.50.refs_3_ = bf16[256,256]{1,0:T(8,128)(2,1)S(1)} collective-permute-done((bf16[256,256]{1,0:T(8,128)(2,1)S(1)}, bf16[256,256]{1,0:T(8,128)(2,1)S(1)}, u32[]{:S(2)}, u32[]{:S(2)}) %collective-permute-start.50) | collective-permute-done | bytes 131104 | tf_op jit(solution)/shard_map/ppermute | solution.py:292
  142.4 2.3 %shard_map.103 = (f32[2,256,256]{2,1,0:T(8,128)S(1)}, f32[2,256,256]{2,1,0:T(8,128)S(1)}) custom-call(s32[5]{0:T(128)S(1)} %bitcast.55, s32[1]{0:T(128)} %bitcast.29.tile, bf16[5,1024,2048]{2,1,0:T(8,128)(2,1)S(1)} %copy-done.1, bf16[256,256]{1,0:T(8,128)(2,1)S(1)} %collective-permute-done.47.refs_0_, bf16[256,256]{1,0:T(8,128)(2,1)S(1)} %collective-permute-done.48.refs_1_, ...), custom_call_target="tpu_custom_call" | custom-call | tf_op jit(solution)/shard_map/pallas_call | solution.py:267
  147.6 3.8 %collective-permute-done.46.got = s16[272,256]{1,0:T(8,128)(2,1)S(1)} collective-permute-done((s16[272,256]{1,0:T(8,128)(2,1)S(1)}, s16[272,256]{1,0:T(8,128)(2,1)S(1)}, u32[]{:S(2)}, u32[]{:S(2)}) %collective-permute-start.46) | collective-permute-done | bytes 139296 | tf_op jit(solution)/shard_map/ppermute | solution.py:292
  151.5 2.5 %collective-permute-done.55.got = s16[272,256]{1,0:T(8,128)(2,1)S(1)} collective-permute-done((s16[272,256]{1,0:T(8,128)(2,1)S(1)}, s16[272,256]{1,0:T(8,128)(2,1)S(1)}, u32[]{:S(2)}, u32[]{:S(2)}) %collective-permute-start.55) | collective-permute-done | bytes 139296 | tf_op jit(solution)/shard_map/ppermute | solution.py:292
  (96 shorter events, 20.9 us)
Async XLA Ops:
  0.0 6.4 %copy-start.3 = (f32[1024]{0:T(1024)S(1)}, f32[1024]{0:T(1024)}, u32[]{:S(2)}) copy-start(f32[1024]{0:T(1024)} %param.10) | copy-start | bytes 12292
  0.0 6.4 %copy-start.4 = (f32[1024]{0:T(1024)S(1)}, f32[1024]{0:T(1024)}, u32[]{:S(2)}) copy-start(f32[1024]{0:T(1024)} %param.11) | copy-start | bytes 12292
  1.3 12.5 %collective-permute-start = (bf16[4,128,256]{2,1,0:T(8,128)(2,1)S(1)}, bf16[4,128,256]{2,1,0:T(8,128)(2,1)S(1)}, u32[]{:S(2)}, u32[]{:S(2)}) collective-permute-start(bf16[4,128,256]{2,1,0:T(8,128)(2,1)S(1)} %get-tuple-element.212.front), channel_id=1, source_target_pairs={{0,8},{4,0},{8,16},{12,4},{16,24},{20,12},{24,28},{28,20},{1,9},{5... | collective-permute-start | bytes 786440 | tf_op jit(solution)/shard_map/ppermute | solution.py:303
  4.4 9.4 %collective-permute-start.1 = (bf16[4,128,256]{2,1,0:T(8,128)(2,1)S(1)}, bf16[4,128,256]{2,1,0:T(8,128)(2,1)S(1)}, u32[]{:S(2)}, u32[]{:S(2)}) collective-permute-start(bf16[4,128,256]{2,1,0:T(8,128)(2,1)S(1)} %get-tuple-element.211.back), channel_id=1, source_target_pairs={{0,4},{4,12},{8,0},{12,20},{16,8},{20,28},{24,16},{28,24},{1,5},{5... | collective-permute-start | bytes 786440 | tf_op jit(solution)/shard_map/ppermute | solution.py:303
  4.4 12.6 %collective-permute-start.23 = (bf16[4,128,256]{2,1,0:T(8,128)(2,1)S(1)}, bf16[4,128,256]{2,1,0:T(8,128)(2,1)S(1)}, u32[]{:S(2)}, u32[]{:S(2)}) collective-permute-start(bf16[4,128,256]{2,1,0:T(8,128)(2,1)S(1)} %get-tuple-element.214.front), channel_id=1, source_target_pairs={{0,8},{4,0},{8,16},{12,4},{16,24},{20,12},{24,28},{28,20},{1,9},{5... | collective-permute-start | bytes 786440 | tf_op jit(solution)/shard_map/ppermute | solution.py:303
  6.4 12.2 %collective-permute-start.24 = (bf16[4,128,256]{2,1,0:T(8,128)(2,1)S(1)}, bf16[4,128,256]{2,1,0:T(8,128)(2,1)S(1)}, u32[]{:S(2)}, u32[]{:S(2)}) collective-permute-start(bf16[4,128,256]{2,1,0:T(8,128)(2,1)S(1)} %get-tuple-element.213.back), channel_id=1, source_target_pairs={{0,4},{4,12},{8,0},{12,20},{16,8},{20,28},{24,16},{28,24},{1,5},{5... | collective-permute-start | bytes 786440 | tf_op jit(solution)/shard_map/ppermute | solution.py:303
  6.4 7.0 %copy-start = (bf16[5,1024,2048]{2,1,0:T(8,128)(2,1)S(1)}, bf16[5,1024,2048]{2,1,0:T(8,128)(2,1)}, u32[]{:S(2)}) copy-start(bf16[5,1024,2048]{2,1,0:T(8,128)(2,1)} %matrix.65) | copy-start | bytes 62914564
  13.4 7.9 %copy-start.1 = (bf16[5,1024,2048]{2,1,0:T(8,128)(2,1)S(1)}, bf16[5,1024,2048]{2,1,0:T(8,128)(2,1)}, u32[]{:S(2)}) copy-start(bf16[5,1024,2048]{2,1,0:T(8,128)(2,1)} %matrix.65) | copy-start | bytes 62914564
  13.4 7.9 %copy-start.2 = (s32[1,1,5]{2,1,0:T(1,128)S(1)}, s32[1,1,5]{2,1,0:T(1,128)}, u32[]{:S(2)}) copy-start(s32[1,1,5]{2,1,0:T(1,128)} %param.12) | copy-start | bytes 64
  13.8 9.9 %collective-permute-start.2 = (bf16[4,128,256]{2,1,0:T(8,128)(2,1)S(1)}, bf16[4,128,256]{2,1,0:T(8,128)(2,1)S(1)}, u32[]{:S(2)}, u32[]{:S(2)}) collective-permute-start(bf16[4,128,256]{2,1,0:T(8,128)(2,1)S(1)} %collective-permute-done.front), channel_id=1, source_target_pairs={{0,8},{4,0},{8,16},{12,4},{16,24},{20,12},{24,28},{28,20},{1,9},{5... | collective-permute-start | bytes 786440 | tf_op jit(solution)/shard_map/ppermute | solution.py:303
  15.9 9.2 %collective-permute-start.3 = (bf16[4,128,256]{2,1,0:T(8,128)(2,1)S(1)}, bf16[4,128,256]{2,1,0:T(8,128)(2,1)S(1)}, u32[]{:S(2)}, u32[]{:S(2)}) collective-permute-start(bf16[4,128,256]{2,1,0:T(8,128)(2,1)S(1)} %collective-permute-done.1.back), channel_id=1, source_target_pairs={{0,4},{4,12},{8,0},{12,20},{16,8},{20,28},{24,16},{28,24},{1,5},{5... | collective-permute-start | bytes 786440 | tf_op jit(solution)/shard_map/ppermute | solution.py:303
  18.6 10.9 %collective-permute-start.25 = (bf16[4,128,256]{2,1,0:T(8,128)(2,1)S(1)}, bf16[4,128,256]{2,1,0:T(8,128)(2,1)S(1)}, u32[]{:S(2)}, u32[]{:S(2)}) collective-permute-start(bf16[4,128,256]{2,1,0:T(8,128)(2,1)S(1)} %collective-permute-done.23.front), channel_id=1, source_target_pairs={{0,8},{4,0},{8,16},{12,4},{16,24},{20,12},{24,28},{28,20},{1,9},{5... | collective-permute-start | bytes 786440 | tf_op jit(solution)/shard_map/ppermute | solution.py:303
  20.2 10.6 %collective-permute-start.26 = (bf16[4,128,256]{2,1,0:T(8,128)(2,1)S(1)}, bf16[4,128,256]{2,1,0:T(8,128)(2,1)S(1)}, u32[]{:S(2)}, u32[]{:S(2)}) collective-permute-start(bf16[4,128,256]{2,1,0:T(8,128)(2,1)S(1)} %collective-permute-done.24.back), channel_id=1, source_target_pairs={{0,4},{4,12},{8,0},{12,20},{16,8},{20,28},{24,16},{28,24},{1,5},{5... | collective-permute-start | bytes 786440 | tf_op jit(solution)/shard_map/ppermute | solution.py:303
  25.1 12.5 %collective-permute-start.4 = (bf16[4,128,256]{2,1,0:T(8,128)(2,1)S(1)}, bf16[4,128,256]{2,1,0:T(8,128)(2,1)S(1)}, u32[]{:S(2)}, u32[]{:S(2)}) collective-permute-start(bf16[4,128,256]{2,1,0:T(8,128)(2,1)S(1)} %collective-permute-done.2.front), channel_id=1, source_target_pairs={{0,8},{4,0},{8,16},{12,4},{16,24},{20,12},{24,28},{28,20},{1,9},{5... | collective-permute-start | bytes 786440 | tf_op jit(solution)/shard_map/ppermute | solution.py:303
  26.7 10.9 %collective-permute-start.5 = (bf16[4,128,256]{2,1,0:T(8,128)(2,1)S(1)}, bf16[4,128,256]{2,1,0:T(8,128)(2,1)S(1)}, u32[]{:S(2)}, u32[]{:S(2)}) collective-permute-start(bf16[4,128,256]{2,1,0:T(8,128)(2,1)S(1)} %collective-permute-done.3.back), channel_id=1, source_target_pairs={{0,4},{4,12},{8,0},{12,20},{16,8},{20,28},{24,16},{28,24},{1,5},{5... | collective-permute-start | bytes 786440 | tf_op jit(solution)/shard_map/ppermute | solution.py:303
  30.7 13.8 %collective-permute-start.27 = (bf16[4,128,256]{2,1,0:T(8,128)(2,1)S(1)}, bf16[4,128,256]{2,1,0:T(8,128)(2,1)S(1)}, u32[]{:S(2)}, u32[]{:S(2)}) collective-permute-start(bf16[4,128,256]{2,1,0:T(8,128)(2,1)S(1)} %collective-permute-done.25.front), channel_id=1, source_target_pairs={{0,8},{4,0},{8,16},{12,4},{16,24},{20,12},{24,28},{28,20},{1,9},{5... | collective-permute-start | bytes 786440 | tf_op jit(solution)/shard_map/ppermute | solution.py:303
  32.3 12.2 %collective-permute-start.28 = (bf16[4,128,256]{2,1,0:T(8,128)(2,1)S(1)}, bf16[4,128,256]{2,1,0:T(8,128)(2,1)S(1)}, u32[]{:S(2)}, u32[]{:S(2)}) collective-permute-start(bf16[4,128,256]{2,1,0:T(8,128)(2,1)S(1)} %collective-permute-done.26.back), channel_id=1, source_target_pairs={{0,4},{4,12},{8,0},{12,20},{16,8},{20,28},{24,16},{28,24},{1,5},{5... | collective-permute-start | bytes 786440 | tf_op jit(solution)/shard_map/ppermute | solution.py:303
  37.6 11.4 %collective-permute-start.6 = (bf16[4,128,256]{2,1,0:T(8,128)(2,1)S(1)}, bf16[4,128,256]{2,1,0:T(8,128)(2,1)S(1)}, u32[]{:S(2)}, u32[]{:S(2)}) collective-permute-start(bf16[4,128,256]{2,1,0:T(8,128)(2,1)S(1)} %collective-permute-done.4.front), channel_id=1, source_target_pairs={{0,8},{4,0},{8,16},{12,4},{16,24},{20,12},{24,28},{28,20},{1,9},{5... | collective-permute-start | bytes 786440 | tf_op jit(solution)/shard_map/ppermute | solution.py:303
  39.2 9.8 %collective-permute-start.7 = (bf16[4,128,256]{2,1,0:T(8,128)(2,1)S(1)}, bf16[4,128,256]{2,1,0:T(8,128)(2,1)S(1)}, u32[]{:S(2)}, u32[]{:S(2)}) collective-permute-start(bf16[4,128,256]{2,1,0:T(8,128)(2,1)S(1)} %collective-permute-done.5.back), channel_id=1, source_target_pairs={{0,4},{4,12},{8,0},{12,20},{16,8},{20,28},{24,16},{28,24},{1,5},{5... | collective-permute-start | bytes 786440 | tf_op jit(solution)/shard_map/ppermute | solution.py:303
  44.5 9.3 %collective-permute-start.29 = (bf16[4,128,256]{2,1,0:T(8,128)(2,1)S(1)}, bf16[4,128,256]{2,1,0:T(8,128)(2,1)S(1)}, u32[]{:S(2)}, u32[]{:S(2)}) collective-permute-start(bf16[4,128,256]{2,1,0:T(8,128)(2,1)S(1)} %collective-permute-done.27.front), channel_id=1, source_target_pairs={{0,8},{4,0},{8,16},{12,4},{16,24},{20,12},{24,28},{28,20},{1,9},{5... | collective-permute-start | bytes 786440 | tf_op jit(solution)/shard_map/ppermute | solution.py:303
  46.1 9.2 %collective-permute-start.30 = (bf16[4,128,256]{2,1,0:T(8,128)(2,1)S(1)}, bf16[4,128,256]{2,1,0:T(8,128)(2,1)S(1)}, u32[]{:S(2)}, u32[]{:S(2)}) collective-permute-start(bf16[4,128,256]{2,1,0:T(8,128)(2,1)S(1)} %collective-permute-done.28.back), channel_id=1, source_target_pairs={{0,4},{4,12},{8,0},{12,20},{16,8},{20,28},{24,16},{28,24},{1,5},{5... | collective-permute-start | bytes 786440 | tf_op jit(solution)/shard_map/ppermute | solution.py:303
  49.0 10.8 %collective-permute-start.8 = (bf16[4,128,256]{2,1,0:T(8,128)(2,1)S(1)}, bf16[4,128,256]{2,1,0:T(8,128)(2,1)S(1)}, u32[]{:S(2)}, u32[]{:S(2)}) collective-permute-start(bf16[4,128,256]{2,1,0:T(8,128)(2,1)S(1)} %collective-permute-done.6.front), channel_id=1, source_target_pairs={{0,8},{4,0},{8,16},{12,4},{16,24},{20,12},{24,28},{28,20},{1,9},{5... | collective-permute-start | bytes 786440 | tf_op jit(solution)/shard_map/ppermute | solution.py:303
  50.7 10.4 %collective-permute-start.9 = (bf16[4,128,256]{2,1,0:T(8,128)(2,1)S(1)}, bf16[4,128,256]{2,1,0:T(8,128)(2,1)S(1)}, u32[]{:S(2)}, u32[]{:S(2)}) collective-permute-start(bf16[4,128,256]{2,1,0:T(8,128)(2,1)S(1)} %collective-permute-done.7.back), channel_id=1, source_target_pairs={{0,4},{4,12},{8,0},{12,20},{16,8},{20,28},{24,16},{28,24},{1,5},{5... | collective-permute-start | bytes 786440 | tf_op jit(solution)/shard_map/ppermute | solution.py:303
  55.4 10.1 %collective-permute-start.31 = (bf16[4,128,256]{2,1,0:T(8,128)(2,1)S(1)}, bf16[4,128,256]{2,1,0:T(8,128)(2,1)S(1)}, u32[]{:S(2)}, u32[]{:S(2)}) collective-permute-start(bf16[4,128,256]{2,1,0:T(8,128)(2,1)S(1)} %collective-permute-done.29.front), channel_id=1, source_target_pairs={{0,8},{4,0},{8,16},{12,4},{16,24},{20,12},{24,28},{28,20},{1,9},{5... | collective-permute-start | bytes 786440 | tf_op jit(solution)/shard_map/ppermute | solution.py:303
  56.9 9.8 %collective-permute-start.32 = (bf16[4,128,256]{2,1,0:T(8,128)(2,1)S(1)}, bf16[4,128,256]{2,1,0:T(8,128)(2,1)S(1)}, u32[]{:S(2)}, u32[]{:S(2)}) collective-permute-start(bf16[4,128,256]{2,1,0:T(8,128)(2,1)S(1)} %collective-permute-done.30.back), channel_id=1, source_target_pairs={{0,4},{4,12},{8,0},{12,20},{16,8},{20,28},{24,16},{28,24},{1,5},{5... | collective-permute-start | bytes 786440 | tf_op jit(solution)/shard_map/ppermute | solution.py:303
  61.0 10.0 %collective-permute-start.10 = (bf16[4,128,256]{2,1,0:T(8,128)(2,1)S(1)}, bf16[4,128,256]{2,1,0:T(8,128)(2,1)S(1)}, u32[]{:S(2)}, u32[]{:S(2)}) collective-permute-start(bf16[4,128,256]{2,1,0:T(8,128)(2,1)S(1)} %collective-permute-done.8.front), channel_id=1, source_target_pairs={{0,8},{4,0},{8,16},{12,4},{16,24},{20,12},{24,28},{28,20},{1,9},{5... | collective-permute-start | bytes 786440 | tf_op jit(solution)/shard_map/ppermute | solution.py:303
  62.5 9.8 %collective-permute-start.11 = (bf16[4,128,256]{2,1,0:T(8,128)(2,1)S(1)}, bf16[4,128,256]{2,1,0:T(8,128)(2,1)S(1)}, u32[]{:S(2)}, u32[]{:S(2)}) collective-permute-start(bf16[4,128,256]{2,1,0:T(8,128)(2,1)S(1)} %collective-permute-done.9.back), channel_id=1, source_target_pairs={{0,4},{4,12},{8,0},{12,20},{16,8},{20,28},{24,16},{28,24},{1,5},{5... | collective-permute-start | bytes 786440 | tf_op jit(solution)/shard_map/ppermute | solution.py:303
  66.6 10.1 %collective-permute-start.33 = (bf16[4,128,256]{2,1,0:T(8,128)(2,1)S(1)}, bf16[4,128,256]{2,1,0:T(8,128)(2,1)S(1)}, u32[]{:S(2)}, u32[]{:S(2)}) collective-permute-start(bf16[4,128,256]{2,1,0:T(8,128)(2,1)S(1)} %collective-permute-done.31.front), channel_id=1, source_target_pairs={{0,8},{4,0},{8,16},{12,4},{16,24},{20,12},{24,28},{28,20},{1,9},{5... | collective-permute-start | bytes 786440 | tf_op jit(solution)/shard_map/ppermute | solution.py:303
  68.1 9.8 %collective-permute-start.34 = (bf16[4,128,256]{2,1,0:T(8,128)(2,1)S(1)}, bf16[4,128,256]{2,1,0:T(8,128)(2,1)S(1)}, u32[]{:S(2)}, u32[]{:S(2)}) collective-permute-start(bf16[4,128,256]{2,1,0:T(8,128)(2,1)S(1)} %collective-permute-done.32.back), channel_id=1, source_target_pairs={{0,4},{4,12},{8,0},{12,20},{16,8},{20,28},{24,16},{28,24},{1,5},{5... | collective-permute-start | bytes 786440 | tf_op jit(solution)/shard_map/ppermute | solution.py:303
  68.7 5.6 %copy-start.5 = (f32[2,256,512]{2,1,0:T(8,128)S(1)}, f32[2,256,512]{2,1,0:T(8,128)}, u32[]{:S(2)}) copy-start(f32[2,256,512]{2,1,0:T(8,128)} %param.9) | copy-start | bytes 3145732
  72.2 10.1 %collective-permute-start.12 = (bf16[4,128,256]{2,1,0:T(8,128)(2,1)S(1)}, bf16[4,128,256]{2,1,0:T(8,128)(2,1)S(1)}, u32[]{:S(2)}, u32[]{:S(2)}) collective-permute-start(bf16[4,128,256]{2,1,0:T(8,128)(2,1)S(1)} %collective-permute-done.10.front), channel_id=1, source_target_pairs={{0,8},{4,0},{8,16},{12,4},{16,24},{20,12},{24,28},{28,20},{1,9},{5... | collective-permute-start | bytes 786440 | tf_op jit(solution)/shard_map/ppermute | solution.py:303
  73.7 8.7 %collective-permute-start.13 = (bf16[4,128,256]{2,1,0:T(8,128)(2,1)S(1)}, bf16[4,128,256]{2,1,0:T(8,128)(2,1)S(1)}, u32[]{:S(2)}, u32[]{:S(2)}) collective-permute-start(bf16[4,128,256]{2,1,0:T(8,128)(2,1)S(1)} %collective-permute-done.11.back), channel_id=1, source_target_pairs={{0,4},{4,12},{8,0},{12,20},{16,8},{20,28},{24,16},{28,24},{1,5},{5... | collective-permute-start | bytes 786440 | tf_op jit(solution)/shard_map/ppermute | solution.py:303
  77.9 8.8 %collective-permute-start.35 = (bf16[4,128,256]{2,1,0:T(8,128)(2,1)S(1)}, bf16[4,128,256]{2,1,0:T(8,128)(2,1)S(1)}, u32[]{:S(2)}, u32[]{:S(2)}) collective-permute-start(bf16[4,128,256]{2,1,0:T(8,128)(2,1)S(1)} %collective-permute-done.33.front), channel_id=1, source_target_pairs={{0,8},{4,0},{8,16},{12,4},{16,24},{20,12},{24,28},{28,20},{1,9},{5... | collective-permute-start | bytes 786440 | tf_op jit(solution)/shard_map/ppermute | solution.py:303
  79.3 7.3 %collective-permute-start.36 = (bf16[4,128,256]{2,1,0:T(8,128)(2,1)S(1)}, bf16[4,128,256]{2,1,0:T(8,128)(2,1)S(1)}, u32[]{:S(2)}, u32[]{:S(2)}) collective-permute-start(bf16[4,128,256]{2,1,0:T(8,128)(2,1)S(1)} %collective-permute-done.34.back), channel_id=1, source_target_pairs={{0,4},{4,12},{8,0},{12,20},{16,8},{20,28},{24,16},{28,24},{1,5},{5... | collective-permute-start | bytes 786440 | tf_op jit(solution)/shard_map/ppermute | solution.py:303
  84.1 4.8 %collective-permute-start.14 = (f32[2,256,256]{2,1,0:T(8,128)S(1)}, f32[2,256,256]{2,1,0:T(8,128)S(1)}, u32[]{:S(2)}, u32[]{:S(2)}) collective-permute-start(f32[2,256,256]{2,1,0:T(8,128)S(1)} %get-tuple-element.141), channel_id=1, source_target_pairs={{0,1},{1,0},{2,3},{3,2},{4,5},{5,4},{6,7},{7,6},{8,9},{9,8},{10,11... | collective-permute-start | bytes 1572872 | tf_op jit(solution)/shard_map/ppermute | solution.py:292
  88.4 2.2 %collective-permute-start.37 = (f32[2,256,256]{2,1,0:T(8,128)S(1)}, f32[2,256,256]{2,1,0:T(8,128)S(1)}, u32[]{:S(2)}, u32[]{:S(2)}) collective-permute-start(f32[2,256,256]{2,1,0:T(8,128)S(1)} %get-tuple-element.185), channel_id=1, source_target_pairs={{0,1},{1,0},{2,3},{3,2},{4,5},{5,4},{6,7},{7,6},{8,9},{9,8},{10,11... | collective-permute-start | bytes 1572872 | tf_op jit(solution)/shard_map/ppermute | solution.py:292
  89.1 6.6 %collective-permute-start.15 = (s16[272,256]{1,0:T(8,128)(2,1)S(1)}, s16[272,256]{1,0:T(8,128)(2,1)S(1)}, u32[]{:S(2)}, u32[]{:S(2)}) collective-permute-start(s16[272,256]{1,0:T(8,128)(2,1)S(1)} %get-tuple-element.143), channel_id=1, source_target_pairs={{0,2},{1,3},{2,0},{3,1},{4,6},{5,7},{6,4},{7,5},{8,10},{9,11},{10,... | collective-permute-start | bytes 417800 | tf_op jit(solution)/shard_map/ppermute | solution.py:292
  90.8 9.1 %collective-permute-start.38 = (s16[272,256]{1,0:T(8,128)(2,1)S(1)}, s16[272,256]{1,0:T(8,128)(2,1)S(1)}, u32[]{:S(2)}, u32[]{:S(2)}) collective-permute-start(s16[272,256]{1,0:T(8,128)(2,1)S(1)} %get-tuple-element.187), channel_id=1, source_target_pairs={{0,2},{1,3},{2,0},{3,1},{4,6},{5,7},{6,4},{7,5},{8,10},{9,11},{10,... | collective-permute-start | bytes 417800 | tf_op jit(solution)/shard_map/ppermute | solution.py:292
  95.8 9.7 %collective-permute-start.16 = (bf16[256,256]{1,0:T(8,128)(2,1)S(1)}, bf16[256,256]{1,0:T(8,128)(2,1)S(1)}, u32[]{:S(2)}, u32[]{:S(2)}) collective-permute-start(bf16[256,256]{1,0:T(8,128)(2,1)S(1)} %shard_map.83.refs_0_), channel_id=1, source_target_pairs={{0,16},{1,17},{2,18},{3,19},{4,20},{5,21},{6,22},{7,23},{8,24},{9,... | collective-permute-start | bytes 393224 | tf_op jit(solution)/shard_map/ppermute | solution.py:292
  98.4 9.3 %collective-permute-start.17 = (bf16[256,256]{1,0:T(8,128)(2,1)S(1)}, bf16[256,256]{1,0:T(8,128)(2,1)S(1)}, u32[]{:S(2)}, u32[]{:S(2)}) collective-permute-start(bf16[256,256]{1,0:T(8,128)(2,1)S(1)} %shard_map.83.refs_0_), channel_id=1, source_target_pairs={{0,8},{1,9},{2,10},{3,11},{4,12},{5,13},{6,14},{7,15},{8,0},{9,1},... | collective-permute-start | bytes 393224 | tf_op jit(solution)/shard_map/ppermute | solution.py:292
  100.0 8.1 %collective-permute-start.39 = (bf16[256,256]{1,0:T(8,128)(2,1)S(1)}, bf16[256,256]{1,0:T(8,128)(2,1)S(1)}, u32[]{:S(2)}, u32[]{:S(2)}) collective-permute-start(bf16[256,256]{1,0:T(8,128)(2,1)S(1)} %shard_map.94.refs_0_), channel_id=1, source_target_pairs={{0,16},{1,17},{2,18},{3,19},{4,20},{5,21},{6,22},{7,23},{8,24},{9,... | collective-permute-start | bytes 393224 | tf_op jit(solution)/shard_map/ppermute | solution.py:292
  100.5 10.2 %collective-permute-start.40 = (bf16[256,256]{1,0:T(8,128)(2,1)S(1)}, bf16[256,256]{1,0:T(8,128)(2,1)S(1)}, u32[]{:S(2)}, u32[]{:S(2)}) collective-permute-start(bf16[256,256]{1,0:T(8,128)(2,1)S(1)} %shard_map.94.refs_0_), channel_id=1, source_target_pairs={{0,8},{1,9},{2,10},{3,11},{4,12},{5,13},{6,14},{7,15},{8,0},{9,1},... | collective-permute-start | bytes 393224 | tf_op jit(solution)/shard_map/ppermute | solution.py:292
  107.7 5.8 %collective-permute-start.18 = (bf16[256,256]{1,0:T(8,128)(2,1)S(1)}, bf16[256,256]{1,0:T(8,128)(2,1)S(1)}, u32[]{:S(2)}, u32[]{:S(2)}) collective-permute-start(bf16[256,256]{1,0:T(8,128)(2,1)S(1)} %collective-permute-done.16.refs_2_), channel_id=1, source_target_pairs={{0,8},{1,9},{2,10},{3,11},{4,12},{5,13},{6,14},{7,15},{8,0},{9,1},... | collective-permute-start | bytes 393224 | tf_op jit(solution)/shard_map/ppermute | solution.py:292
  110.7 7.0 %collective-permute-start.41 = (bf16[256,256]{1,0:T(8,128)(2,1)S(1)}, bf16[256,256]{1,0:T(8,128)(2,1)S(1)}, u32[]{:S(2)}, u32[]{:S(2)}) collective-permute-start(bf16[256,256]{1,0:T(8,128)(2,1)S(1)} %collective-permute-done.39.refs_2_), channel_id=1, source_target_pairs={{0,8},{1,9},{2,10},{3,11},{4,12},{5,13},{6,14},{7,15},{8,0},{9,1},... | collective-permute-start | bytes 393224 | tf_op jit(solution)/shard_map/ppermute | solution.py:292
  113.6 5.7 %collective-permute-start.42 = (bf16[256,256]{1,0:T(8,128)(2,1)S(1)}, bf16[256,256]{1,0:T(8,128)(2,1)S(1)}, u32[]{:S(2)}, u32[]{:S(2)}) collective-permute-start(bf16[256,256]{1,0:T(8,128)(2,1)S(1)} %get-tuple-element.149), channel_id=1, source_target_pairs={{0,1},{1,0},{2,3},{3,2},{4,5},{5,4},{6,7},{7,6},{8,9},{9,8},{10,11... | collective-permute-start | bytes 393224 | tf_op jit(solution)/shard_map/ppermute | solution.py:292
  113.7 7.1 %collective-permute-start.43 = (bf16[256,256]{1,0:T(8,128)(2,1)S(1)}, bf16[256,256]{1,0:T(8,128)(2,1)S(1)}, u32[]{:S(2)}, u32[]{:S(2)}) collective-permute-start(bf16[256,256]{1,0:T(8,128)(2,1)S(1)} %get-tuple-element.150), channel_id=1, source_target_pairs={{0,2},{1,3},{2,0},{3,1},{4,6},{5,7},{6,4},{7,5},{8,10},{9,11},{10,... | collective-permute-start | bytes 393224 | tf_op jit(solution)/shard_map/ppermute | solution.py:292
  115.2 6.8 %collective-permute-start.44 = (bf16[256,256]{1,0:T(8,128)(2,1)S(1)}, bf16[256,256]{1,0:T(8,128)(2,1)S(1)}, u32[]{:S(2)}, u32[]{:S(2)}) collective-permute-start(bf16[256,256]{1,0:T(8,128)(2,1)S(1)} %get-tuple-element.151), channel_id=1, source_target_pairs={{0,3},{1,2},{2,1},{3,0},{4,7},{5,6},{6,5},{7,4},{8,11},{9,10},{10,... | collective-permute-start | bytes 393224 | tf_op jit(solution)/shard_map/ppermute | solution.py:292
  115.5 8.9 %collective-permute-start.19 = (bf16[256,256]{1,0:T(8,128)(2,1)S(1)}, bf16[256,256]{1,0:T(8,128)(2,1)S(1)}, u32[]{:S(2)}, u32[]{:S(2)}) collective-permute-start(bf16[256,256]{1,0:T(8,128)(2,1)S(1)} %get-tuple-element.148.refs_0_), channel_id=1, source_target_pairs={{0,4},{1,5},{2,6},{3,7},{4,0},{5,1},{6,2},{7,3},{8,12},{9,13},{10,... | collective-permute-start | bytes 393224 | tf_op jit(solution)/shard_map/ppermute | solution.py:292
  117.8 8.6 %collective-permute-start.20 = (bf16[256,256]{1,0:T(8,128)(2,1)S(1)}, bf16[256,256]{1,0:T(8,128)(2,1)S(1)}, u32[]{:S(2)}, u32[]{:S(2)}) collective-permute-start(bf16[256,256]{1,0:T(8,128)(2,1)S(1)} %get-tuple-element.149), channel_id=1, source_target_pairs={{0,5},{1,4},{2,7},{3,6},{4,1},{5,0},{6,3},{7,2},{8,13},{9,12},{10,... | collective-permute-start | bytes 393224 | tf_op jit(solution)/shard_map/ppermute | solution.py:292
  119.3 9.1 %collective-permute-start.21 = (bf16[256,256]{1,0:T(8,128)(2,1)S(1)}, bf16[256,256]{1,0:T(8,128)(2,1)S(1)}, u32[]{:S(2)}, u32[]{:S(2)}) collective-permute-start(bf16[256,256]{1,0:T(8,128)(2,1)S(1)} %get-tuple-element.150), channel_id=1, source_target_pairs={{0,6},{1,7},{2,4},{3,5},{4,2},{5,3},{6,0},{7,1},{8,14},{9,15},{10,... | collective-permute-start | bytes 393224 | tf_op jit(solution)/shard_map/ppermute | solution.py:292
  120.8 9.5 %collective-permute-start.22 = (bf16[256,256]{1,0:T(8,128)(2,1)S(1)}, bf16[256,256]{1,0:T(8,128)(2,1)S(1)}, u32[]{:S(2)}, u32[]{:S(2)}) collective-permute-start(bf16[256,256]{1,0:T(8,128)(2,1)S(1)} %get-tuple-element.151), channel_id=1, source_target_pairs={{0,7},{1,6},{2,5},{3,4},{4,3},{5,2},{6,1},{7,0},{8,15},{9,14},{10,... | collective-permute-start | bytes 393224 | tf_op jit(solution)/shard_map/ppermute | solution.py:292
  124.4 7.2 %collective-permute-start.51 = (bf16[256,256]{1,0:T(8,128)(2,1)S(1)}, bf16[256,256]{1,0:T(8,128)(2,1)S(1)}, u32[]{:S(2)}, u32[]{:S(2)}) collective-permute-start(bf16[256,256]{1,0:T(8,128)(2,1)S(1)} %get-tuple-element.201), channel_id=1, source_target_pairs={{0,1},{1,0},{2,3},{3,2},{4,5},{5,4},{6,7},{7,6},{8,9},{9,8},{10,11... | collective-permute-start | bytes 393224 | tf_op jit(solution)/shard_map/ppermute | solution.py:292
  124.5 9.0 %collective-permute-start.52 = (bf16[256,256]{1,0:T(8,128)(2,1)S(1)}, bf16[256,256]{1,0:T(8,128)(2,1)S(1)}, u32[]{:S(2)}, u32[]{:S(2)}) collective-permute-start(bf16[256,256]{1,0:T(8,128)(2,1)S(1)} %get-tuple-element.202), channel_id=1, source_target_pairs={{0,2},{1,3},{2,0},{3,1},{4,6},{5,7},{6,4},{7,5},{8,10},{9,11},{10,... | collective-permute-start | bytes 393224 | tf_op jit(solution)/shard_map/ppermute | solution.py:292
  126.4 11.8 %collective-permute-start.53 = (bf16[256,256]{1,0:T(8,128)(2,1)S(1)}, bf16[256,256]{1,0:T(8,128)(2,1)S(1)}, u32[]{:S(2)}, u32[]{:S(2)}) collective-permute-start(bf16[256,256]{1,0:T(8,128)(2,1)S(1)} %get-tuple-element.203), channel_id=1, source_target_pairs={{0,3},{1,2},{2,1},{3,0},{4,7},{5,6},{6,5},{7,4},{8,11},{9,10},{10,... | collective-permute-start | bytes 393224 | tf_op jit(solution)/shard_map/ppermute | solution.py:292
  128.4 12.2 %collective-permute-start.48 = (bf16[256,256]{1,0:T(8,128)(2,1)S(1)}, bf16[256,256]{1,0:T(8,128)(2,1)S(1)}, u32[]{:S(2)}, u32[]{:S(2)}) collective-permute-start(bf16[256,256]{1,0:T(8,128)(2,1)S(1)} %get-tuple-element.201), channel_id=1, source_target_pairs={{0,5},{1,4},{2,7},{3,6},{4,1},{5,0},{6,3},{7,2},{8,13},{9,12},{10,... | collective-permute-start | bytes 393224 | tf_op jit(solution)/shard_map/ppermute | solution.py:292
  130.3 10.2 %collective-permute-start.47 = (bf16[256,256]{1,0:T(8,128)(2,1)S(1)}, bf16[256,256]{1,0:T(8,128)(2,1)S(1)}, u32[]{:S(2)}, u32[]{:S(2)}) collective-permute-start(bf16[256,256]{1,0:T(8,128)(2,1)S(1)} %get-tuple-element.200.refs_0_), channel_id=1, source_target_pairs={{0,4},{1,5},{2,6},{3,7},{4,0},{5,1},{6,2},{7,3},{8,12},{9,13},{10,... | collective-permute-start | bytes 393224 | tf_op jit(solution)/shard_map/ppermute | solution.py:292
  131.6 9.0 %collective-permute-start.49 = (bf16[256,256]{1,0:T(8,128)(2,1)S(1)}, bf16[256,256]{1,0:T(8,128)(2,1)S(1)}, u32[]{:S(2)}, u32[]{:S(2)}) collective-permute-start(bf16[256,256]{1,0:T(8,128)(2,1)S(1)} %get-tuple-element.202), channel_id=1, source_target_pairs={{0,6},{1,7},{2,4},{3,5},{4,2},{5,3},{6,0},{7,1},{8,14},{9,15},{10,... | collective-permute-start | bytes 393224 | tf_op jit(solution)/shard_map/ppermute | solution.py:292
  133.5 8.9 %collective-permute-start.50 = (bf16[256,256]{1,0:T(8,128)(2,1)S(1)}, bf16[256,256]{1,0:T(8,128)(2,1)S(1)}, u32[]{:S(2)}, u32[]{:S(2)}) collective-permute-start(bf16[256,256]{1,0:T(8,128)(2,1)S(1)} %get-tuple-element.203), channel_id=1, source_target_pairs={{0,7},{1,6},{2,5},{3,4},{4,3},{5,2},{6,1},{7,0},{8,15},{9,14},{10,... | collective-permute-start | bytes 393224 | tf_op jit(solution)/shard_map/ppermute | solution.py:292
  138.1 6.6 %collective-permute-start.45 = (f32[2,256,256]{2,1,0:T(8,128)S(1)}, f32[2,256,256]{2,1,0:T(8,128)S(1)}, u32[]{:S(2)}, u32[]{:S(2)}) collective-permute-start(f32[2,256,256]{2,1,0:T(8,128)S(1)} %get-tuple-element.197), channel_id=1, source_target_pairs={{0,1},{1,0},{2,3},{3,2},{4,5},{5,4},{6,7},{7,6},{8,9},{9,8},{10,11... | collective-permute-start | bytes 1572872 | tf_op jit(solution)/shard_map/ppermute | solution.py:292
  144.6 2.0 %collective-permute-start.54 = (f32[2,256,256]{2,1,0:T(8,128)S(1)}, f32[2,256,256]{2,1,0:T(8,128)S(1)}, u32[]{:S(2)}, u32[]{:S(2)}) collective-permute-start(f32[2,256,256]{2,1,0:T(8,128)S(1)} %get-tuple-element.206), channel_id=1, source_target_pairs={{0,1},{1,0},{2,3},{3,2},{4,5},{5,4},{6,7},{7,6},{8,9},{9,8},{10,11... | collective-permute-start | bytes 1572872 | tf_op jit(solution)/shard_map/ppermute | solution.py:292
  144.8 6.5 %collective-permute-start.46 = (s16[272,256]{1,0:T(8,128)(2,1)S(1)}, s16[272,256]{1,0:T(8,128)(2,1)S(1)}, u32[]{:S(2)}, u32[]{:S(2)}) collective-permute-start(s16[272,256]{1,0:T(8,128)(2,1)S(1)} %get-tuple-element.199), channel_id=1, source_target_pairs={{0,2},{1,3},{2,0},{3,1},{4,6},{5,7},{6,4},{7,5},{8,10},{9,11},{10,... | collective-permute-start | bytes 417800 | tf_op jit(solution)/shard_map/ppermute | solution.py:292
  146.7 7.2 %collective-permute-start.55 = (s16[272,256]{1,0:T(8,128)(2,1)S(1)}, s16[272,256]{1,0:T(8,128)(2,1)S(1)}, u32[]{:S(2)}, u32[]{:S(2)}) collective-permute-start(s16[272,256]{1,0:T(8,128)(2,1)S(1)} %get-tuple-element.208), channel_id=1, source_target_pairs={{0,2},{1,3},{2,0},{3,1},{4,6},{5,7},{6,4},{7,5},{8,10},{9,11},{10,... | collective-permute-start | bytes 417800 | tf_op jit(solution)/shard_map/ppermute | solution.py:292

commit v2 on v1

--- a/solution.py
+++ b/solution.py
@@ -413,7 +413,8 @@
     for number in numbers:
         gots.append(last_hop(sents[number]))
         sents[number], marks[number] = lax.optimization_barrier((sents[number], marks[number]))
-        laters.append(end_past(number, 1)[0])
+        later, gots[number] = lax.optimization_barrier((end_past(number, 1)[0], gots[number]))
+        laters.append(later)
     by_layers = [to_layers(load_call(interaction, kepts[number], gots[number], gain, cubic)) for number in numbers]
     every, ends = [], []
     for number in numbers:

time: 154 us -> 154 us (level)
  Pallas kernels: 51 us -> 45.2 us
  waiting for transfers between devices: 38.5 us -> 41.4 us
  starting transfers between devices: 54.9 us -> 57 us
    pallas_call x4, Pallas kernels: 9.1 us -> 3.25 us  [recent_call(): pl.pallas_call(functools.partial(recent_kernel, fanout, beside, ending, l...]
    ppermute x28, waiting for transfers between devices: 26.5 us -> 29.5 us  [send(): return lax.ppermute(value, BOTH, pairs)]
    ppermute x28, starting transfers between devices: 25.3 us -> 27.4 us  [send(): return lax.ppermute(value, BOTH, pairs)]
  transfers between devices with their start and end apart: 56 -> 56, of which waited for: 24 -> 29; matrix products, arithmetic and copies ran while one was open for 0% -> 0% of each run, Pallas kernels for 33% -> 29%
where the time goes in v2:
time: 154 us
  starting transfers between devices  57 us (37%)
  Pallas kernels  45.2 us (29%)
  waiting for transfers between devices  41.4 us (27%)
  local copies, waits for them, and re-layouts  8.36 us (5%)
    pallas_call x18, Pallas kernels, past_call(): pl.pallas_call(functools.partial(past_kernel, number, carried is None, st...  40.5 us
    ppermute x28, starting transfers between devices, around(): return lax.ppermute(value, 'row', pairs)  29.6 us
    ppermute x28, waiting for transfers between devices, send(): return lax.ppermute(value, BOTH, pairs)  29.5 us
    ppermute x28, starting transfers between devices, send(): return lax.ppermute(value, BOTH, pairs)  27.4 us
    ppermute x28, waiting for transfers between devices, around(): return lax.ppermute(value, 'row', pairs)  12 us
    unnamed x12, local copies, waits for them, and re-layouts  6.98 us
    pallas_call x4, Pallas kernels, recent_call(): pl.pallas_call(functools.partial(recent_kernel, fanout, beside, ending, l...  3.25 us
  transfers between devices with their start and end apart: 56, of which 29 were waited for; matrix products, arithmetic and copies ran while one was open for 0% of the time, Pallas kernels for 29%

profile of v2, /device:TPU:0, one launch (start us, length us, event | category | flops | bytes accessed | tf_op | source)
XLA Modules:
  0.0 154.0 jit_solution(15275203089515456732)
XLA Ops:
  0.0 1.3 fusion.1
  1.3 3.1 %collective-permute-start = (bf16[4,128,256]{2,1,0:T(8,128)(2,1)S(1)}, bf16[4,128,256]{2,1,0:T(8,128)(2,1)S(1)}, u32[]{:S(2)}, u32[]{:S(2)}) collective-permute-start(bf16[4,128,256]{2,1,0:T(8,128)(2,1)S(1)} %get-tuple-element.220.front), channel_id=1, source_target_pairs={{0,8},{4,0},{8,16},{12,4},{16,24},{20,12},{24,28},{28,20},{1,9},{5... | collective-permute-start | bytes 786440 | tf_op jit(solution)/shard_map/ppermute | solution.py:303
  4.4 2.0 %collective-permute-start.23 = (bf16[4,128,256]{2,1,0:T(8,128)(2,1)S(1)}, bf16[4,128,256]{2,1,0:T(8,128)(2,1)S(1)}, u32[]{:S(2)}, u32[]{:S(2)}) collective-permute-start(bf16[4,128,256]{2,1,0:T(8,128)(2,1)S(1)} %get-tuple-element.222.front), channel_id=1, source_target_pairs={{0,8},{4,0},{8,16},{12,4},{16,24},{20,12},{24,28},{28,20},{1,9},{5... | collective-permute-start | bytes 786440 | tf_op jit(solution)/shard_map/ppermute | solution.py:303
  6.4 7.0 %copy-done = bf16[5,1024,2048]{2,1,0:T(8,128)(2,1)S(1)} copy-done((bf16[5,1024,2048]{2,1,0:T(8,128)(2,1)S(1)}, bf16[5,1024,2048]{2,1,0:T(8,128)(2,1)}, u32[]{:S(2)}) %copy-start) | copy-done | bytes 20971544
  13.8 2.1 %collective-permute-start.2 = (bf16[4,128,256]{2,1,0:T(8,128)(2,1)S(1)}, bf16[4,128,256]{2,1,0:T(8,128)(2,1)S(1)}, u32[]{:S(2)}, u32[]{:S(2)}) collective-permute-start(bf16[4,128,256]{2,1,0:T(8,128)(2,1)S(1)} %collective-permute-done.front), channel_id=1, source_target_pairs={{0,8},{4,0},{8,16},{12,4},{16,24},{20,12},{24,28},{28,20},{1,9},{5... | collective-permute-start | bytes 786440 | tf_op jit(solution)/shard_map/ppermute | solution.py:303
  16.9 1.6 %collective-permute-done.24.back = bf16[4,128,256]{2,1,0:T(8,128)(2,1)S(1)} collective-permute-done((bf16[4,128,256]{2,1,0:T(8,128)(2,1)S(1)}, bf16[4,128,256]{2,1,0:T(8,128)(2,1)S(1)}, u32[]{:S(2)}, u32[]{:S(2)}) %collective-permute-start.24) | collective-permute-done | bytes 262176 | tf_op jit(solution)/shard_map/ppermute | solution.py:303
  18.6 1.6 %collective-permute-start.25 = (bf16[4,128,256]{2,1,0:T(8,128)(2,1)S(1)}, bf16[4,128,256]{2,1,0:T(8,128)(2,1)S(1)}, u32[]{:S(2)}, u32[]{:S(2)}) collective-permute-start(bf16[4,128,256]{2,1,0:T(8,128)(2,1)S(1)} %collective-permute-done.23.front), channel_id=1, source_target_pairs={{0,8},{4,0},{8,16},{12,4},{16,24},{20,12},{24,28},{28,20},{1,9},{5... | collective-permute-start | bytes 786440 | tf_op jit(solution)/shard_map/ppermute | solution.py:303
  21.3 2.4 %shard_map.74 = (f32[1024,512]{1,0:T(8,128)S(1)}, f32[8,128]{1,0:T(8,128)S(1)}) custom-call(s32[5]{0:T(128)S(1)} %bitcast.34, s32[1]{0:T(128)} %bitcast.8.tile, bf16[5,1024,2048]{2,1,0:T(8,128)(2,1)S(1)} %copy-done.1, bf16[4,128,256]{2,1,0:T(8,128)(2,1)S(1)} %get-tuple-element.220.front, bf16[4,128,256]{2,1,0:T(8,128)(2,1)S(1)} %get-tuple-element.219.back, ...), custom_call_target="tpu_custom_call" | custom-call | flops 1342177280 | bytes 2621440 | tf_op jit(solution)/shard_map/pallas_call | solution.py:145
  23.7 1.4 collective-permute-done.3.back
  25.1 1.6 %collective-permute-start.4 = (bf16[4,128,256]{2,1,0:T(8,128)(2,1)S(1)}, bf16[4,128,256]{2,1,0:T(8,128)(2,1)S(1)}, u32[]{:S(2)}, u32[]{:S(2)}) collective-permute-start(bf16[4,128,256]{2,1,0:T(8,128)(2,1)S(1)} %collective-permute-done.2.front), channel_id=1, source_target_pairs={{0,8},{4,0},{8,16},{12,4},{16,24},{20,12},{24,28},{28,20},{1,9},{5... | collective-permute-start | bytes 786440 | tf_op jit(solution)/shard_map/ppermute | solution.py:303
  27.1 2.4 %shard_map.86 = (f32[1024,512]{1,0:T(8,128)S(1)}, f32[8,128]{1,0:T(8,128)S(1)}) custom-call(s32[5]{0:T(128)S(1)} %bitcast.35, s32[1]{0:T(128)} %bitcast.17.tile, bf16[5,1024,2048]{2,1,0:T(8,128)(2,1)S(1)} %copy-done.1, bf16[4,128,256]{2,1,0:T(8,128)(2,1)S(1)} %get-tuple-element.222.front, bf16[4,128,256]{2,1,0:T(8,128)(2,1)S(1)} %get-tuple-element.221.back, ...), custom_call_target="tpu_custom_call" | custom-call | flops 1342177280 | bytes 2621440 | tf_op jit(solution)/shard_map/pallas_call | solution.py:145
  29.5 1.2 collective-permute-done.26.back
  30.7 1.6 %collective-permute-start.27 = (bf16[4,128,256]{2,1,0:T(8,128)(2,1)S(1)}, bf16[4,128,256]{2,1,0:T(8,128)(2,1)S(1)}, u32[]{:S(2)}, u32[]{:S(2)}) collective-permute-start(bf16[4,128,256]{2,1,0:T(8,128)(2,1)S(1)} %collective-permute-done.25.front), channel_id=1, source_target_pairs={{0,8},{4,0},{8,16},{12,4},{16,24},{20,12},{24,28},{28,20},{1,9},{5... | collective-permute-start | bytes 786440 | tf_op jit(solution)/shard_map/ppermute | solution.py:303
  32.8 2.4 %shard_map.75 = (f32[1024,512]{1,0:T(8,128)S(1)}, f32[8,128]{1,0:T(8,128)S(1)}) custom-call(s32[5]{0:T(128)S(1)} %bitcast.36, s32[1]{0:T(128)} %bitcast.9.tile, bf16[5,1024,2048]{2,1,0:T(8,128)(2,1)S(1)} %copy-done.1, bf16[4,128,256]{2,1,0:T(8,128)(2,1)S(1)} %collective-permute-done.front, ...), custom_call_target="tpu_custom_call", output_to_operand_aliasing={{0}: (6, {})} | custom-call | flops 1342177280 | bytes 2621440 | tf_op jit(solution)/shard_map/pallas_call | solution.py:145
  35.1 2.4 %shard_map.76 = (f32[1024,512]{1,0:T(8,128)S(1)}, f32[8,128]{1,0:T(8,128)S(1)}) custom-call(s32[5]{0:T(128)S(1)} %bitcast.37, s32[1]{0:T(128)} %bitcast.10.tile, bf16[5,1024,2048]{2,1,0:T(8,128)(2,1)S(1)} %copy-done.1, bf16[4,128,256]{2,1,0:T(8,128)(2,1)S(1)} %collective-permute-done.2.front, ...), custom_call_target="tpu_custom_call", output_to_operand_aliasing={{0}: (6, {})} | custom-call | flops 1342177280 | bytes 2621440 | tf_op jit(solution)/shard_map/pallas_call | solution.py:145
  37.6 1.6 %collective-permute-start.6 = (bf16[4,128,256]{2,1,0:T(8,128)(2,1)S(1)}, bf16[4,128,256]{2,1,0:T(8,128)(2,1)S(1)}, u32[]{:S(2)}, u32[]{:S(2)}) collective-permute-start(bf16[4,128,256]{2,1,0:T(8,128)(2,1)S(1)} %collective-permute-done.4.front), channel_id=1, source_target_pairs={{0,8},{4,0},{8,16},{12,4},{16,24},{20,12},{24,28},{28,20},{1,9},{5... | collective-permute-start | bytes 786440 | tf_op jit(solution)/shard_map/ppermute | solution.py:303
  39.7 2.4 %shard_map.87 = (f32[1024,512]{1,0:T(8,128)S(1)}, f32[8,128]{1,0:T(8,128)S(1)}) custom-call(s32[5]{0:T(128)S(1)} %bitcast.38, s32[1]{0:T(128)} %bitcast.18.tile, bf16[5,1024,2048]{2,1,0:T(8,128)(2,1)S(1)} %copy-done.1, bf16[4,128,256]{2,1,0:T(8,128)(2,1)S(1)} %collective-permute-done.23.front, ...), custom_call_target="tpu_custom_call", output_to_operand_aliasing={{0}: (6, {})} | custom-call | flops 1342177280 | bytes 2621440 | tf_op jit(solution)/shard_map/pallas_call | solution.py:145
  42.1 2.4 %shard_map.88 = (f32[1024,512]{1,0:T(8,128)S(1)}, f32[8,128]{1,0:T(8,128)S(1)}) custom-call(s32[5]{0:T(128)S(1)} %bitcast.39, s32[1]{0:T(128)} %bitcast.19.tile, bf16[5,1024,2048]{2,1,0:T(8,128)(2,1)S(1)} %copy-done.1, bf16[4,128,256]{2,1,0:T(8,128)(2,1)S(1)} %collective-permute-done.25.front, ...), custom_call_target="tpu_custom_call", output_to_operand_aliasing={{0}: (6, {})} | custom-call | flops 1342177280 | bytes 2621440 | tf_op jit(solution)/shard_map/pallas_call | solution.py:145
  44.5 1.6 %collective-permute-start.29 = (bf16[4,128,256]{2,1,0:T(8,128)(2,1)S(1)}, bf16[4,128,256]{2,1,0:T(8,128)(2,1)S(1)}, u32[]{:S(2)}, u32[]{:S(2)}) collective-permute-start(bf16[4,128,256]{2,1,0:T(8,128)(2,1)S(1)} %collective-permute-done.27.front), channel_id=1, source_target_pairs={{0,8},{4,0},{8,16},{12,4},{16,24},{20,12},{24,28},{28,20},{1,9},{5... | collective-permute-start | bytes 786440 | tf_op jit(solution)/shard_map/ppermute | solution.py:303
  46.6 2.4 %shard_map.77 = (f32[1024,512]{1,0:T(8,128)S(1)}, f32[8,128]{1,0:T(8,128)S(1)}) custom-call(s32[5]{0:T(128)S(1)} %bitcast.40, s32[1]{0:T(128)} %bitcast.11.tile, bf16[5,1024,2048]{2,1,0:T(8,128)(2,1)S(1)} %copy-done.1, bf16[4,128,256]{2,1,0:T(8,128)(2,1)S(1)} %collective-permute-done.4.front, ...), custom_call_target="tpu_custom_call", output_to_operand_aliasing={{0}: (6, {})} | custom-call | flops 1342177280 | bytes 2621440 | tf_op jit(solution)/shard_map/pallas_call | solution.py:145
  49.0 1.7 %collective-permute-start.8 = (bf16[4,128,256]{2,1,0:T(8,128)(2,1)S(1)}, bf16[4,128,256]{2,1,0:T(8,128)(2,1)S(1)}, u32[]{:S(2)}, u32[]{:S(2)}) collective-permute-start(bf16[4,128,256]{2,1,0:T(8,128)(2,1)S(1)} %collective-permute-done.6.front), channel_id=1, source_target_pairs={{0,8},{4,0},{8,16},{12,4},{16,24},{20,12},{24,28},{28,20},{1,9},{5... | collective-permute-start | bytes 786440 | tf_op jit(solution)/shard_map/ppermute | solution.py:303
  51.1 2.4 %shard_map.89 = (f32[1024,512]{1,0:T(8,128)S(1)}, f32[8,128]{1,0:T(8,128)S(1)}) custom-call(s32[5]{0:T(128)S(1)} %bitcast.41, s32[1]{0:T(128)} %bitcast.20.tile, bf16[5,1024,2048]{2,1,0:T(8,128)(2,1)S(1)} %copy-done.1, bf16[4,128,256]{2,1,0:T(8,128)(2,1)S(1)} %collective-permute-done.27.front, ...), custom_call_target="tpu_custom_call", output_to_operand_aliasing={{0}: (6, {})} | custom-call | flops 1342177280 | bytes 2621440 | tf_op jit(solution)/shard_map/pallas_call | solution.py:145
  53.8 1.6 %collective-permute-done.30.back = bf16[4,128,256]{2,1,0:T(8,128)(2,1)S(1)} collective-permute-done((bf16[4,128,256]{2,1,0:T(8,128)(2,1)S(1)}, bf16[4,128,256]{2,1,0:T(8,128)(2,1)S(1)}, u32[]{:S(2)}, u32[]{:S(2)}) %collective-permute-start.30) | collective-permute-done | bytes 262176 | tf_op jit(solution)/shard_map/ppermute | solution.py:303
  55.4 1.5 collective-permute-start.31
  57.4 2.4 %shard_map.78 = (f32[1024,512]{1,0:T(8,128)S(1)}, f32[8,128]{1,0:T(8,128)S(1)}) custom-call(s32[5]{0:T(128)S(1)} %bitcast.42, s32[1]{0:T(128)} %bitcast.12.tile, bf16[5,1024,2048]{2,1,0:T(8,128)(2,1)S(1)} %copy-done.1, bf16[4,128,256]{2,1,0:T(8,128)(2,1)S(1)} %collective-permute-done.6.front, ...), custom_call_target="tpu_custom_call", output_to_operand_aliasing={{0}: (6, {})} | custom-call | flops 1342177280 | bytes 2621440 | tf_op jit(solution)/shard_map/pallas_call | solution.py:145
  61.0 1.5 collective-permute-start.10
  63.0 2.4 %shard_map.90 = (f32[1024,512]{1,0:T(8,128)S(1)}, f32[8,128]{1,0:T(8,128)S(1)}) custom-call(s32[5]{0:T(128)S(1)} %bitcast.43, s32[1]{0:T(128)} %bitcast.21.tile, bf16[5,1024,2048]{2,1,0:T(8,128)(2,1)S(1)} %copy-done.1, bf16[4,128,256]{2,1,0:T(8,128)(2,1)S(1)} %collective-permute-done.29.front, ...), custom_call_target="tpu_custom_call", output_to_operand_aliasing={{0}: (6, {})} | custom-call | flops 1342177280 | bytes 2621440 | tf_op jit(solution)/shard_map/pallas_call | solution.py:145
  66.6 1.5 collective-permute-start.33
  68.7 2.4 %shard_map.79 = (f32[1024,512]{1,0:T(8,128)S(1)}, f32[8,128]{1,0:T(8,128)S(1)}) custom-call(s32[5]{0:T(128)S(1)} %bitcast.44, s32[1]{0:T(128)} %bitcast.13.tile, bf16[5,1024,2048]{2,1,0:T(8,128)(2,1)S(1)} %copy-done.1, bf16[4,128,256]{2,1,0:T(8,128)(2,1)S(1)} %collective-permute-done.8.front, ...), custom_call_target="tpu_custom_call", output_to_operand_aliasing={{0}: (6, {})} | custom-call | flops 1342177280 | bytes 2621440 | tf_op jit(solution)/shard_map/pallas_call | solution.py:145
  72.2 1.5 collective-permute-start.12
  74.4 2.4 %shard_map.91 = (f32[1024,512]{1,0:T(8,128)S(1)}, f32[8,128]{1,0:T(8,128)S(1)}) custom-call(s32[5]{0:T(128)S(1)} %bitcast.45, s32[1]{0:T(128)} %bitcast.22.tile, bf16[5,1024,2048]{2,1,0:T(8,128)(2,1)S(1)} %copy-done.1, bf16[4,128,256]{2,1,0:T(8,128)(2,1)S(1)} %collective-permute-done.31.front, ...), custom_call_target="tpu_custom_call", output_to_operand_aliasing={{0}: (6, {})} | custom-call | flops 1342177280 | bytes 2621440 | tf_op jit(solution)/shard_map/pallas_call | solution.py:145
  77.9 1.5 collective-permute-start.35
  79.9 2.4 %shard_map.80 = (f32[1024,512]{1,0:T(8,128)S(1)}, f32[8,128]{1,0:T(8,128)S(1)}) custom-call(s32[5]{0:T(128)S(1)} %bitcast.46, s32[1]{0:T(128)} %bitcast.14.tile, bf16[5,1024,2048]{2,1,0:T(8,128)(2,1)S(1)} %copy-done.1, bf16[4,128,256]{2,1,0:T(8,128)(2,1)S(1)} %collective-permute-done.10.front, ...), custom_call_target="tpu_custom_call", output_to_operand_aliasing={{0}: (6, {})} | custom-call | flops 1342177280 | bytes 2621440 | tf_op jit(solution)/shard_map/pallas_call | solution.py:145
  82.4 1.8 %shard_map.81 = (f32[2,256,256]{2,1,0:T(8,128)S(1)}, f32[2,256,256]{2,1,0:T(8,128)S(1)}) custom-call(s32[5]{0:T(128)S(1)} %bitcast.47, s32[1]{0:T(128)} %bitcast.15.tile, bf16[5,1024,2048]{2,1,0:T(8,128)(2,1)S(1)} %copy-done.1, bf16[4,128,256]{2,1,0:T(8,128)(2,1)S(1)} %collective-permute-done.12.front, ...), custom_call_target="tpu_custom_call" | custom-call | flops 671088640 | bytes 2621440 | tf_op jit(solution)/shard_map/pallas_call | solution.py:145
  84.2 2.4 %shard_map.92 = (f32[1024,512]{1,0:T(8,128)S(1)}, f32[8,128]{1,0:T(8,128)S(1)}) custom-call(s32[5]{0:T(128)S(1)} %bitcast.48, s32[1]{0:T(128)} %bitcast.23.tile, bf16[5,1024,2048]{2,1,0:T(8,128)(2,1)S(1)} %copy-done.1, bf16[4,128,256]{2,1,0:T(8,128)(2,1)S(1)} %collective-permute-done.33.front, ...), custom_call_target="tpu_custom_call", output_to_operand_aliasing={{0}: (6, {})} | custom-call | flops 1342177280 | bytes 2621440 | tf_op jit(solution)/shard_map/pallas_call | solution.py:145
  86.7 1.8 %shard_map.93 = (f32[2,256,256]{2,1,0:T(8,128)S(1)}, f32[2,256,256]{2,1,0:T(8,128)S(1)}) custom-call(s32[5]{0:T(128)S(1)} %bitcast.49, s32[1]{0:T(128)} %bitcast.24.tile, bf16[5,1024,2048]{2,1,0:T(8,128)(2,1)S(1)} %copy-done.1, bf16[4,128,256]{2,1,0:T(8,128)(2,1)S(1)} %collective-permute-done.35.front, ...), custom_call_target="tpu_custom_call" | custom-call | flops 671088640 | bytes 2621440 | tf_op jit(solution)/shard_map/pallas_call | solution.py:145
  89.1 1.6 %collective-permute-start.15 = (s16[272,256]{1,0:T(8,128)(2,1)S(1)}, s16[272,256]{1,0:T(8,128)(2,1)S(1)}, u32[]{:S(2)}, u32[]{:S(2)}) collective-permute-start(s16[272,256]{1,0:T(8,128)(2,1)S(1)} %get-tuple-element.147), channel_id=1, source_target_pairs={{0,2},{1,3},{2,0},{3,1},{4,6},{5,7},{6,4},{7,5},{8,10},{9,11},{10,... | collective-permute-start | bytes 417800 | tf_op jit(solution)/shard_map/ppermute | solution.py:292
  90.8 1.4 collective-permute-start.38
  92.2 1.7 %shard_map.83.refs_4_ = f32[1024,256]{1,0:T(8,128)S(1)} custom-call(s32[5]{0:T(128)S(1)} %bitcast.50, s32[1]{0:T(128)} %bitcast.16.tile, bf16[5,1024,2048]{2,1,0:T(8,128)(2,1)S(1)} %copy-done.1, bf16[4,128,256]{2,1,0:T(8,128)(2,1)S(1)} %collective-permute-done.12.front, bf16[4,128,256]{2,1,0:T(8,128)(2,1)S(1)} %collective-permute-done.13.back, ...), custom_call_target="tpu_custom_call" | custom-call | flops 671088640 | bytes 2621440 | tf_op jit(solution)/shard_map/pallas_call | solution.py:145
  94.0 1.7 %collective-permute-done.15.got = s16[272,256]{1,0:T(8,128)(2,1)S(1)} collective-permute-done((s16[272,256]{1,0:T(8,128)(2,1)S(1)}, s16[272,256]{1,0:T(8,128)(2,1)S(1)}, u32[]{:S(2)}, u32[]{:S(2)}) %collective-permute-start.15) | collective-permute-done | bytes 139296 | tf_op jit(solution)/shard_map/ppermute | solution.py:292
  95.8 2.6 %collective-permute-start.16 = (bf16[256,256]{1,0:T(8,128)(2,1)S(1)}, bf16[256,256]{1,0:T(8,128)(2,1)S(1)}, u32[]{:S(2)}, u32[]{:S(2)}) collective-permute-start(bf16[256,256]{1,0:T(8,128)(2,1)S(1)} %shard_map.84.refs_0_), channel_id=1, source_target_pairs={{0,16},{1,17},{2,18},{3,19},{4,20},{5,21},{6,22},{7,23},{8,24},{9,... | collective-permute-start | bytes 393224 | tf_op jit(solution)/shard_map/ppermute | solution.py:292
  98.4 1.5 collective-permute-start.17
  99.9 1.7 %shard_map.95.refs_4_ = f32[1024,256]{1,0:T(8,128)S(1)} custom-call(s32[5]{0:T(128)S(1)} %bitcast.51, s32[1]{0:T(128)} %bitcast.25.tile, bf16[5,1024,2048]{2,1,0:T(8,128)(2,1)S(1)} %copy-done.1, bf16[4,128,256]{2,1,0:T(8,128)(2,1)S(1)} %collective-permute-done.35.front, bf16[4,128,256]{2,1,0:T(8,128)(2,1)S(1)} %collective-permute-done.36.back, ...), custom_call_target="tpu_custom_call" | custom-call | flops 671088640 | bytes 2621440 | tf_op jit(solution)/shard_map/pallas_call | solution.py:145
  102.7 1.4 collective-permute-done.16.refs_2_
  104.1 1.8 %collective-permute-done.17.refs_1_ = bf16[256,256]{1,0:T(8,128)(2,1)S(1)} collective-permute-done((bf16[256,256]{1,0:T(8,128)(2,1)S(1)}, bf16[256,256]{1,0:T(8,128)(2,1)S(1)}, u32[]{:S(2)}, u32[]{:S(2)}) %collective-permute-start.17) | collective-permute-done | bytes 131104 | tf_op jit(solution)/shard_map/ppermute | solution.py:292
  105.9 1.6 %collective-permute-start.18 = (bf16[256,256]{1,0:T(8,128)(2,1)S(1)}, bf16[256,256]{1,0:T(8,128)(2,1)S(1)}, u32[]{:S(2)}, u32[]{:S(2)}) collective-permute-start(bf16[256,256]{1,0:T(8,128)(2,1)S(1)} %collective-permute-done.16.refs_2_), channel_id=1, source_target_pairs={{0,8},{1,9},{2,10},{3,11},{4,12},{5,13},{6,14},{7,15},{8,0},{9,1},... | collective-permute-start | bytes 393224 | tf_op jit(solution)/shard_map/ppermute | solution.py:292
  107.5 1.4 collective-permute-done.39.refs_2_
  109.0 1.7 %collective-permute-done.40.refs_1_ = bf16[256,256]{1,0:T(8,128)(2,1)S(1)} collective-permute-done((bf16[256,256]{1,0:T(8,128)(2,1)S(1)}, bf16[256,256]{1,0:T(8,128)(2,1)S(1)}, u32[]{:S(2)}, u32[]{:S(2)}) %collective-permute-start.40) | collective-permute-done | bytes 131104 | tf_op jit(solution)/shard_map/ppermute | solution.py:292
  110.6 2.5 %collective-permute-start.41 = (bf16[256,256]{1,0:T(8,128)(2,1)S(1)}, bf16[256,256]{1,0:T(8,128)(2,1)S(1)}, u32[]{:S(2)}, u32[]{:S(2)}) collective-permute-start(bf16[256,256]{1,0:T(8,128)(2,1)S(1)} %collective-permute-done.39.refs_2_), channel_id=1, source_target_pairs={{0,8},{1,9},{2,10},{3,11},{4,12},{5,13},{6,14},{7,15},{8,0},{9,1},... | collective-permute-start | bytes 393224 | tf_op jit(solution)/shard_map/ppermute | solution.py:292
  113.3 1.6 %collective-permute-start.43 = (bf16[256,256]{1,0:T(8,128)(2,1)S(1)}, bf16[256,256]{1,0:T(8,128)(2,1)S(1)}, u32[]{:S(2)}, u32[]{:S(2)}) collective-permute-start(bf16[256,256]{1,0:T(8,128)(2,1)S(1)} %get-tuple-element.156), channel_id=1, source_target_pairs={{0,2},{1,3},{2,0},{3,1},{4,6},{5,7},{6,4},{7,5},{8,10},{9,11},{10,... | collective-permute-start | bytes 393224 | tf_op jit(solution)/shard_map/ppermute | solution.py:292
  117.2 1.5 collective-permute-start.21
  119.9 1.7 %collective-permute-done.44.refs_3_ = bf16[256,256]{1,0:T(8,128)(2,1)S(1)} collective-permute-done((bf16[256,256]{1,0:T(8,128)(2,1)S(1)}, bf16[256,256]{1,0:T(8,128)(2,1)S(1)}, u32[]{:S(2)}, u32[]{:S(2)}) %collective-permute-start.44) | collective-permute-done | bytes 131104 | tf_op jit(solution)/shard_map/ppermute | solution.py:292
  122.4 2.1 %collective-permute-start.51 = (bf16[256,256]{1,0:T(8,128)(2,1)S(1)}, bf16[256,256]{1,0:T(8,128)(2,1)S(1)}, u32[]{:S(2)}, u32[]{:S(2)}) collective-permute-start(bf16[256,256]{1,0:T(8,128)(2,1)S(1)} %get-tuple-element.209), channel_id=1, source_target_pairs={{0,1},{1,0},{2,3},{3,2},{4,5},{5,4},{6,7},{7,6},{8,9},{9,8},{10,11... | collective-permute-start | bytes 393224 | tf_op jit(solution)/shard_map/ppermute | solution.py:292
  124.5 1.6 %collective-permute-start.52 = (bf16[256,256]{1,0:T(8,128)(2,1)S(1)}, bf16[256,256]{1,0:T(8,128)(2,1)S(1)}, u32[]{:S(2)}, u32[]{:S(2)}) collective-permute-start(bf16[256,256]{1,0:T(8,128)(2,1)S(1)} %get-tuple-element.210), channel_id=1, source_target_pairs={{0,2},{1,3},{2,0},{3,1},{4,6},{5,7},{6,4},{7,5},{8,10},{9,11},{10,... | collective-permute-start | bytes 393224 | tf_op jit(solution)/shard_map/ppermute | solution.py:292
  126.1 2.1 %collective-permute-done.21.refs_2_ = bf16[256,256]{1,0:T(8,128)(2,1)S(1)} collective-permute-done((bf16[256,256]{1,0:T(8,128)(2,1)S(1)}, bf16[256,256]{1,0:T(8,128)(2,1)S(1)}, u32[]{:S(2)}, u32[]{:S(2)}) %collective-permute-start.21) | collective-permute-done | bytes 131104 | tf_op jit(solution)/shard_map/ppermute | solution.py:292
  128.2 1.7 %collective-permute-done.22.refs_3_ = bf16[256,256]{1,0:T(8,128)(2,1)S(1)} collective-permute-done((bf16[256,256]{1,0:T(8,128)(2,1)S(1)}, bf16[256,256]{1,0:T(8,128)(2,1)S(1)}, u32[]{:S(2)}, u32[]{:S(2)}) %collective-permute-start.22) | collective-permute-done | bytes 131104 | tf_op jit(solution)/shard_map/ppermute | solution.py:292
  130.3 1.5 collective-permute-start.49
  131.8 1.4 collective-permute-done.52.refs_2_
  134.2 1.7 %collective-permute-done.53.refs_3_ = bf16[256,256]{1,0:T(8,128)(2,1)S(1)} collective-permute-done((bf16[256,256]{1,0:T(8,128)(2,1)S(1)}, bf16[256,256]{1,0:T(8,128)(2,1)S(1)}, u32[]{:S(2)}, u32[]{:S(2)}) %collective-permute-start.53) | collective-permute-done | bytes 131104 | tf_op jit(solution)/shard_map/ppermute | solution.py:292
  137.1 1.9 %collective-permute-done.49.refs_2_ = bf16[256,256]{1,0:T(8,128)(2,1)S(1)} collective-permute-done((bf16[256,256]{1,0:T(8,128)(2,1)S(1)}, bf16[256,256]{1,0:T(8,128)(2,1)S(1)}, u32[]{:S(2)}, u32[]{:S(2)}) %collective-permute-start.49) | collective-permute-done | bytes 131104 | tf_op jit(solution)/shard_map/ppermute | solution.py:292
  139.0 3.0 %collective-permute-done.50.refs_3_ = bf16[256,256]{1,0:T(8,128)(2,1)S(1)} collective-permute-done((bf16[256,256]{1,0:T(8,128)(2,1)S(1)}, bf16[256,256]{1,0:T(8,128)(2,1)S(1)}, u32[]{:S(2)}, u32[]{:S(2)}) %collective-permute-start.50) | collective-permute-done | bytes 131104 | tf_op jit(solution)/shard_map/ppermute | solution.py:292
  142.9 1.4 collective-permute-start.54
  146.9 4.1 %collective-permute-done.46.got = s16[272,256]{1,0:T(8,128)(2,1)S(1)} collective-permute-done((s16[272,256]{1,0:T(8,128)(2,1)S(1)}, s16[272,256]{1,0:T(8,128)(2,1)S(1)}, u32[]{:S(2)}, u32[]{:S(2)}) %collective-permute-start.46) | collective-permute-done | bytes 139296 | tf_op jit(solution)/shard_map/ppermute | solution.py:292
  151.1 2.0 %collective-permute-done.55.got = s16[272,256]{1,0:T(8,128)(2,1)S(1)} collective-permute-done((s16[272,256]{1,0:T(8,128)(2,1)S(1)}, s16[272,256]{1,0:T(8,128)(2,1)S(1)}, u32[]{:S(2)}, u32[]{:S(2)}) %collective-permute-start.55) | collective-permute-done | bytes 139296 | tf_op jit(solution)/shard_map/ppermute | solution.py:292
  (96 shorter events, 25.6 us)
Async XLA Ops:
  0.0 6.4 %copy-start.3 = (f32[1024]{0:T(1024)S(1)}, f32[1024]{0:T(1024)}, u32[]{:S(2)}) copy-start(f32[1024]{0:T(1024)} %param.10) | copy-start | bytes 12292
  0.0 6.4 %copy-start.4 = (f32[1024]{0:T(1024)S(1)}, f32[1024]{0:T(1024)}, u32[]{:S(2)}) copy-start(f32[1024]{0:T(1024)} %param.11) | copy-start | bytes 12292
  1.3 12.5 %collective-permute-start = (bf16[4,128,256]{2,1,0:T(8,128)(2,1)S(1)}, bf16[4,128,256]{2,1,0:T(8,128)(2,1)S(1)}, u32[]{:S(2)}, u32[]{:S(2)}) collective-permute-start(bf16[4,128,256]{2,1,0:T(8,128)(2,1)S(1)} %get-tuple-element.220.front), channel_id=1, source_target_pairs={{0,8},{4,0},{8,16},{12,4},{16,24},{20,12},{24,28},{28,20},{1,9},{5... | collective-permute-start | bytes 786440 | tf_op jit(solution)/shard_map/ppermute | solution.py:303
  4.4 9.4 %collective-permute-start.1 = (bf16[4,128,256]{2,1,0:T(8,128)(2,1)S(1)}, bf16[4,128,256]{2,1,0:T(8,128)(2,1)S(1)}, u32[]{:S(2)}, u32[]{:S(2)}) collective-permute-start(bf16[4,128,256]{2,1,0:T(8,128)(2,1)S(1)} %get-tuple-element.219.back), channel_id=1, source_target_pairs={{0,4},{4,12},{8,0},{12,20},{16,8},{20,28},{24,16},{28,24},{1,5},{5... | collective-permute-start | bytes 786440 | tf_op jit(solution)/shard_map/ppermute | solution.py:303
  4.4 12.6 %collective-permute-start.23 = (bf16[4,128,256]{2,1,0:T(8,128)(2,1)S(1)}, bf16[4,128,256]{2,1,0:T(8,128)(2,1)S(1)}, u32[]{:S(2)}, u32[]{:S(2)}) collective-permute-start(bf16[4,128,256]{2,1,0:T(8,128)(2,1)S(1)} %get-tuple-element.222.front), channel_id=1, source_target_pairs={{0,8},{4,0},{8,16},{12,4},{16,24},{20,12},{24,28},{28,20},{1,9},{5... | collective-permute-start | bytes 786440 | tf_op jit(solution)/shard_map/ppermute | solution.py:303
  6.4 12.2 %collective-permute-start.24 = (bf16[4,128,256]{2,1,0:T(8,128)(2,1)S(1)}, bf16[4,128,256]{2,1,0:T(8,128)(2,1)S(1)}, u32[]{:S(2)}, u32[]{:S(2)}) collective-permute-start(bf16[4,128,256]{2,1,0:T(8,128)(2,1)S(1)} %get-tuple-element.221.back), channel_id=1, source_target_pairs={{0,4},{4,12},{8,0},{12,20},{16,8},{20,28},{24,16},{28,24},{1,5},{5... | collective-permute-start | bytes 786440 | tf_op jit(solution)/shard_map/ppermute | solution.py:303
  6.4 7.0 %copy-start = (bf16[5,1024,2048]{2,1,0:T(8,128)(2,1)S(1)}, bf16[5,1024,2048]{2,1,0:T(8,128)(2,1)}, u32[]{:S(2)}) copy-start(bf16[5,1024,2048]{2,1,0:T(8,128)(2,1)} %matrix.65) | copy-start | bytes 62914564
  13.4 7.9 %copy-start.1 = (bf16[5,1024,2048]{2,1,0:T(8,128)(2,1)S(1)}, bf16[5,1024,2048]{2,1,0:T(8,128)(2,1)}, u32[]{:S(2)}) copy-start(bf16[5,1024,2048]{2,1,0:T(8,128)(2,1)} %matrix.65) | copy-start | bytes 62914564
  13.4 7.9 %copy-start.2 = (s32[1,1,5]{2,1,0:T(1,128)S(1)}, s32[1,1,5]{2,1,0:T(1,128)}, u32[]{:S(2)}) copy-start(s32[1,1,5]{2,1,0:T(1,128)} %param.12) | copy-start | bytes 64
  13.8 9.9 %collective-permute-start.2 = (bf16[4,128,256]{2,1,0:T(8,128)(2,1)S(1)}, bf16[4,128,256]{2,1,0:T(8,128)(2,1)S(1)}, u32[]{:S(2)}, u32[]{:S(2)}) collective-permute-start(bf16[4,128,256]{2,1,0:T(8,128)(2,1)S(1)} %collective-permute-done.front), channel_id=1, source_target_pairs={{0,8},{4,0},{8,16},{12,4},{16,24},{20,12},{24,28},{28,20},{1,9},{5... | collective-permute-start | bytes 786440 | tf_op jit(solution)/shard_map/ppermute | solution.py:303
  15.9 9.2 %collective-permute-start.3 = (bf16[4,128,256]{2,1,0:T(8,128)(2,1)S(1)}, bf16[4,128,256]{2,1,0:T(8,128)(2,1)S(1)}, u32[]{:S(2)}, u32[]{:S(2)}) collective-permute-start(bf16[4,128,256]{2,1,0:T(8,128)(2,1)S(1)} %collective-permute-done.1.back), channel_id=1, source_target_pairs={{0,4},{4,12},{8,0},{12,20},{16,8},{20,28},{24,16},{28,24},{1,5},{5... | collective-permute-start | bytes 786440 | tf_op jit(solution)/shard_map/ppermute | solution.py:303
  18.6 10.9 %collective-permute-start.25 = (bf16[4,128,256]{2,1,0:T(8,128)(2,1)S(1)}, bf16[4,128,256]{2,1,0:T(8,128)(2,1)S(1)}, u32[]{:S(2)}, u32[]{:S(2)}) collective-permute-start(bf16[4,128,256]{2,1,0:T(8,128)(2,1)S(1)} %collective-permute-done.23.front), channel_id=1, source_target_pairs={{0,8},{4,0},{8,16},{12,4},{16,24},{20,12},{24,28},{28,20},{1,9},{5... | collective-permute-start | bytes 786440 | tf_op jit(solution)/shard_map/ppermute | solution.py:303
  20.2 10.6 %collective-permute-start.26 = (bf16[4,128,256]{2,1,0:T(8,128)(2,1)S(1)}, bf16[4,128,256]{2,1,0:T(8,128)(2,1)S(1)}, u32[]{:S(2)}, u32[]{:S(2)}) collective-permute-start(bf16[4,128,256]{2,1,0:T(8,128)(2,1)S(1)} %collective-permute-done.24.back), channel_id=1, source_target_pairs={{0,4},{4,12},{8,0},{12,20},{16,8},{20,28},{24,16},{28,24},{1,5},{5... | collective-permute-start | bytes 786440 | tf_op jit(solution)/shard_map/ppermute | solution.py:303
  25.1 12.5 %collective-permute-start.4 = (bf16[4,128,256]{2,1,0:T(8,128)(2,1)S(1)}, bf16[4,128,256]{2,1,0:T(8,128)(2,1)S(1)}, u32[]{:S(2)}, u32[]{:S(2)}) collective-permute-start(bf16[4,128,256]{2,1,0:T(8,128)(2,1)S(1)} %collective-permute-done.2.front), channel_id=1, source_target_pairs={{0,8},{4,0},{8,16},{12,4},{16,24},{20,12},{24,28},{28,20},{1,9},{5... | collective-permute-start | bytes 786440 | tf_op jit(solution)/shard_map/ppermute | solution.py:303
  26.7 10.9 %collective-permute-start.5 = (bf16[4,128,256]{2,1,0:T(8,128)(2,1)S(1)}, bf16[4,128,256]{2,1,0:T(8,128)(2,1)S(1)}, u32[]{:S(2)}, u32[]{:S(2)}) collective-permute-start(bf16[4,128,256]{2,1,0:T(8,128)(2,1)S(1)} %collective-permute-done.3.back), channel_id=1, source_target_pairs={{0,4},{4,12},{8,0},{12,20},{16,8},{20,28},{24,16},{28,24},{1,5},{5... | collective-permute-start | bytes 786440 | tf_op jit(solution)/shard_map/ppermute | solution.py:303
  30.7 13.8 %collective-permute-start.27 = (bf16[4,128,256]{2,1,0:T(8,128)(2,1)S(1)}, bf16[4,128,256]{2,1,0:T(8,128)(2,1)S(1)}, u32[]{:S(2)}, u32[]{:S(2)}) collective-permute-start(bf16[4,128,256]{2,1,0:T(8,128)(2,1)S(1)} %collective-permute-done.25.front), channel_id=1, source_target_pairs={{0,8},{4,0},{8,16},{12,4},{16,24},{20,12},{24,28},{28,20},{1,9},{5... | collective-permute-start | bytes 786440 | tf_op jit(solution)/shard_map/ppermute | solution.py:303
  32.3 12.2 %collective-permute-start.28 = (bf16[4,128,256]{2,1,0:T(8,128)(2,1)S(1)}, bf16[4,128,256]{2,1,0:T(8,128)(2,1)S(1)}, u32[]{:S(2)}, u32[]{:S(2)}) collective-permute-start(bf16[4,128,256]{2,1,0:T(8,128)(2,1)S(1)} %collective-permute-done.26.back), channel_id=1, source_target_pairs={{0,4},{4,12},{8,0},{12,20},{16,8},{20,28},{24,16},{28,24},{1,5},{5... | collective-permute-start | bytes 786440 | tf_op jit(solution)/shard_map/ppermute | solution.py:303
  37.6 11.4 %collective-permute-start.6 = (bf16[4,128,256]{2,1,0:T(8,128)(2,1)S(1)}, bf16[4,128,256]{2,1,0:T(8,128)(2,1)S(1)}, u32[]{:S(2)}, u32[]{:S(2)}) collective-permute-start(bf16[4,128,256]{2,1,0:T(8,128)(2,1)S(1)} %collective-permute-done.4.front), channel_id=1, source_target_pairs={{0,8},{4,0},{8,16},{12,4},{16,24},{20,12},{24,28},{28,20},{1,9},{5... | collective-permute-start | bytes 786440 | tf_op jit(solution)/shard_map/ppermute | solution.py:303
  39.2 9.8 %collective-permute-start.7 = (bf16[4,128,256]{2,1,0:T(8,128)(2,1)S(1)}, bf16[4,128,256]{2,1,0:T(8,128)(2,1)S(1)}, u32[]{:S(2)}, u32[]{:S(2)}) collective-permute-start(bf16[4,128,256]{2,1,0:T(8,128)(2,1)S(1)} %collective-permute-done.5.back), channel_id=1, source_target_pairs={{0,4},{4,12},{8,0},{12,20},{16,8},{20,28},{24,16},{28,24},{1,5},{5... | collective-permute-start | bytes 786440 | tf_op jit(solution)/shard_map/ppermute | solution.py:303
  44.5 9.3 %collective-permute-start.29 = (bf16[4,128,256]{2,1,0:T(8,128)(2,1)S(1)}, bf16[4,128,256]{2,1,0:T(8,128)(2,1)S(1)}, u32[]{:S(2)}, u32[]{:S(2)}) collective-permute-start(bf16[4,128,256]{2,1,0:T(8,128)(2,1)S(1)} %collective-permute-done.27.front), channel_id=1, source_target_pairs={{0,8},{4,0},{8,16},{12,4},{16,24},{20,12},{24,28},{28,20},{1,9},{5... | collective-permute-start | bytes 786440 | tf_op jit(solution)/shard_map/ppermute | solution.py:303
  46.1 9.2 %collective-permute-start.30 = (bf16[4,128,256]{2,1,0:T(8,128)(2,1)S(1)}, bf16[4,128,256]{2,1,0:T(8,128)(2,1)S(1)}, u32[]{:S(2)}, u32[]{:S(2)}) collective-permute-start(bf16[4,128,256]{2,1,0:T(8,128)(2,1)S(1)} %collective-permute-done.28.back), channel_id=1, source_target_pairs={{0,4},{4,12},{8,0},{12,20},{16,8},{20,28},{24,16},{28,24},{1,5},{5... | collective-permute-start | bytes 786440 | tf_op jit(solution)/shard_map/ppermute | solution.py:303
  49.0 10.8 %collective-permute-start.8 = (bf16[4,128,256]{2,1,0:T(8,128)(2,1)S(1)}, bf16[4,128,256]{2,1,0:T(8,128)(2,1)S(1)}, u32[]{:S(2)}, u32[]{:S(2)}) collective-permute-start(bf16[4,128,256]{2,1,0:T(8,128)(2,1)S(1)} %collective-permute-done.6.front), channel_id=1, source_target_pairs={{0,8},{4,0},{8,16},{12,4},{16,24},{20,12},{24,28},{28,20},{1,9},{5... | collective-permute-start | bytes 786440 | tf_op jit(solution)/shard_map/ppermute | solution.py:303
  50.7 10.4 %collective-permute-start.9 = (bf16[4,128,256]{2,1,0:T(8,128)(2,1)S(1)}, bf16[4,128,256]{2,1,0:T(8,128)(2,1)S(1)}, u32[]{:S(2)}, u32[]{:S(2)}) collective-permute-start(bf16[4,128,256]{2,1,0:T(8,128)(2,1)S(1)} %collective-permute-done.7.back), channel_id=1, source_target_pairs={{0,4},{4,12},{8,0},{12,20},{16,8},{20,28},{24,16},{28,24},{1,5},{5... | collective-permute-start | bytes 786440 | tf_op jit(solution)/shard_map/ppermute | solution.py:303
  55.4 10.1 %collective-permute-start.31 = (bf16[4,128,256]{2,1,0:T(8,128)(2,1)S(1)}, bf16[4,128,256]{2,1,0:T(8,128)(2,1)S(1)}, u32[]{:S(2)}, u32[]{:S(2)}) collective-permute-start(bf16[4,128,256]{2,1,0:T(8,128)(2,1)S(1)} %collective-permute-done.29.front), channel_id=1, source_target_pairs={{0,8},{4,0},{8,16},{12,4},{16,24},{20,12},{24,28},{28,20},{1,9},{5... | collective-permute-start | bytes 786440 | tf_op jit(solution)/shard_map/ppermute | solution.py:303
  56.9 9.8 %collective-permute-start.32 = (bf16[4,128,256]{2,1,0:T(8,128)(2,1)S(1)}, bf16[4,128,256]{2,1,0:T(8,128)(2,1)S(1)}, u32[]{:S(2)}, u32[]{:S(2)}) collective-permute-start(bf16[4,128,256]{2,1,0:T(8,128)(2,1)S(1)} %collective-permute-done.30.back), channel_id=1, source_target_pairs={{0,4},{4,12},{8,0},{12,20},{16,8},{20,28},{24,16},{28,24},{1,5},{5... | collective-permute-start | bytes 786440 | tf_op jit(solution)/shard_map/ppermute | solution.py:303
  61.0 10.0 %collective-permute-start.10 = (bf16[4,128,256]{2,1,0:T(8,128)(2,1)S(1)}, bf16[4,128,256]{2,1,0:T(8,128)(2,1)S(1)}, u32[]{:S(2)}, u32[]{:S(2)}) collective-permute-start(bf16[4,128,256]{2,1,0:T(8,128)(2,1)S(1)} %collective-permute-done.8.front), channel_id=1, source_target_pairs={{0,8},{4,0},{8,16},{12,4},{16,24},{20,12},{24,28},{28,20},{1,9},{5... | collective-permute-start | bytes 786440 | tf_op jit(solution)/shard_map/ppermute | solution.py:303
  62.5 9.8 %collective-permute-start.11 = (bf16[4,128,256]{2,1,0:T(8,128)(2,1)S(1)}, bf16[4,128,256]{2,1,0:T(8,128)(2,1)S(1)}, u32[]{:S(2)}, u32[]{:S(2)}) collective-permute-start(bf16[4,128,256]{2,1,0:T(8,128)(2,1)S(1)} %collective-permute-done.9.back), channel_id=1, source_target_pairs={{0,4},{4,12},{8,0},{12,20},{16,8},{20,28},{24,16},{28,24},{1,5},{5... | collective-permute-start | bytes 786440 | tf_op jit(solution)/shard_map/ppermute | solution.py:303
  66.6 10.1 %collective-permute-start.33 = (bf16[4,128,256]{2,1,0:T(8,128)(2,1)S(1)}, bf16[4,128,256]{2,1,0:T(8,128)(2,1)S(1)}, u32[]{:S(2)}, u32[]{:S(2)}) collective-permute-start(bf16[4,128,256]{2,1,0:T(8,128)(2,1)S(1)} %collective-permute-done.31.front), channel_id=1, source_target_pairs={{0,8},{4,0},{8,16},{12,4},{16,24},{20,12},{24,28},{28,20},{1,9},{5... | collective-permute-start | bytes 786440 | tf_op jit(solution)/shard_map/ppermute | solution.py:303
  68.1 9.8 %collective-permute-start.34 = (bf16[4,128,256]{2,1,0:T(8,128)(2,1)S(1)}, bf16[4,128,256]{2,1,0:T(8,128)(2,1)S(1)}, u32[]{:S(2)}, u32[]{:S(2)}) collective-permute-start(bf16[4,128,256]{2,1,0:T(8,128)(2,1)S(1)} %collective-permute-done.32.back), channel_id=1, source_target_pairs={{0,4},{4,12},{8,0},{12,20},{16,8},{20,28},{24,16},{28,24},{1,5},{5... | collective-permute-start | bytes 786440 | tf_op jit(solution)/shard_map/ppermute | solution.py:303
  68.7 5.6 %copy-start.5 = (f32[2,256,512]{2,1,0:T(8,128)S(1)}, f32[2,256,512]{2,1,0:T(8,128)}, u32[]{:S(2)}) copy-start(f32[2,256,512]{2,1,0:T(8,128)} %param.9) | copy-start | bytes 3145732
  72.2 10.1 %collective-permute-start.12 = (bf16[4,128,256]{2,1,0:T(8,128)(2,1)S(1)}, bf16[4,128,256]{2,1,0:T(8,128)(2,1)S(1)}, u32[]{:S(2)}, u32[]{:S(2)}) collective-permute-start(bf16[4,128,256]{2,1,0:T(8,128)(2,1)S(1)} %collective-permute-done.10.front), channel_id=1, source_target_pairs={{0,8},{4,0},{8,16},{12,4},{16,24},{20,12},{24,28},{28,20},{1,9},{5... | collective-permute-start | bytes 786440 | tf_op jit(solution)/shard_map/ppermute | solution.py:303
  73.7 8.7 %collective-permute-start.13 = (bf16[4,128,256]{2,1,0:T(8,128)(2,1)S(1)}, bf16[4,128,256]{2,1,0:T(8,128)(2,1)S(1)}, u32[]{:S(2)}, u32[]{:S(2)}) collective-permute-start(bf16[4,128,256]{2,1,0:T(8,128)(2,1)S(1)} %collective-permute-done.11.back), channel_id=1, source_target_pairs={{0,4},{4,12},{8,0},{12,20},{16,8},{20,28},{24,16},{28,24},{1,5},{5... | collective-permute-start | bytes 786440 | tf_op jit(solution)/shard_map/ppermute | solution.py:303
  77.9 8.8 %collective-permute-start.35 = (bf16[4,128,256]{2,1,0:T(8,128)(2,1)S(1)}, bf16[4,128,256]{2,1,0:T(8,128)(2,1)S(1)}, u32[]{:S(2)}, u32[]{:S(2)}) collective-permute-start(bf16[4,128,256]{2,1,0:T(8,128)(2,1)S(1)} %collective-permute-done.33.front), channel_id=1, source_target_pairs={{0,8},{4,0},{8,16},{12,4},{16,24},{20,12},{24,28},{28,20},{1,9},{5... | collective-permute-start | bytes 786440 | tf_op jit(solution)/shard_map/ppermute | solution.py:303
  79.3 7.3 %collective-permute-start.36 = (bf16[4,128,256]{2,1,0:T(8,128)(2,1)S(1)}, bf16[4,128,256]{2,1,0:T(8,128)(2,1)S(1)}, u32[]{:S(2)}, u32[]{:S(2)}) collective-permute-start(bf16[4,128,256]{2,1,0:T(8,128)(2,1)S(1)} %collective-permute-done.34.back), channel_id=1, source_target_pairs={{0,4},{4,12},{8,0},{12,20},{16,8},{20,28},{24,16},{28,24},{1,5},{5... | collective-permute-start | bytes 786440 | tf_op jit(solution)/shard_map/ppermute | solution.py:303
  84.1 4.8 %collective-permute-start.14 = (f32[2,256,256]{2,1,0:T(8,128)S(1)}, f32[2,256,256]{2,1,0:T(8,128)S(1)}, u32[]{:S(2)}, u32[]{:S(2)}) collective-permute-start(f32[2,256,256]{2,1,0:T(8,128)S(1)} %get-tuple-element.145), channel_id=1, source_target_pairs={{0,1},{1,0},{2,3},{3,2},{4,5},{5,4},{6,7},{7,6},{8,9},{9,8},{10,11... | collective-permute-start | bytes 1572872 | tf_op jit(solution)/shard_map/ppermute | solution.py:292
  88.4 2.2 %collective-permute-start.37 = (f32[2,256,256]{2,1,0:T(8,128)S(1)}, f32[2,256,256]{2,1,0:T(8,128)S(1)}, u32[]{:S(2)}, u32[]{:S(2)}) collective-permute-start(f32[2,256,256]{2,1,0:T(8,128)S(1)} %get-tuple-element.191), channel_id=1, source_target_pairs={{0,1},{1,0},{2,3},{3,2},{4,5},{5,4},{6,7},{7,6},{8,9},{9,8},{10,11... | collective-permute-start | bytes 1572872 | tf_op jit(solution)/shard_map/ppermute | solution.py:292
  89.1 6.6 %collective-permute-start.15 = (s16[272,256]{1,0:T(8,128)(2,1)S(1)}, s16[272,256]{1,0:T(8,128)(2,1)S(1)}, u32[]{:S(2)}, u32[]{:S(2)}) collective-permute-start(s16[272,256]{1,0:T(8,128)(2,1)S(1)} %get-tuple-element.147), channel_id=1, source_target_pairs={{0,2},{1,3},{2,0},{3,1},{4,6},{5,7},{6,4},{7,5},{8,10},{9,11},{10,... | collective-permute-start | bytes 417800 | tf_op jit(solution)/shard_map/ppermute | solution.py:292
  90.8 10.8 %collective-permute-start.38 = (s16[272,256]{1,0:T(8,128)(2,1)S(1)}, s16[272,256]{1,0:T(8,128)(2,1)S(1)}, u32[]{:S(2)}, u32[]{:S(2)}) collective-permute-start(s16[272,256]{1,0:T(8,128)(2,1)S(1)} %get-tuple-element.193), channel_id=1, source_target_pairs={{0,2},{1,3},{2,0},{3,1},{4,6},{5,7},{6,4},{7,5},{8,10},{9,11},{10,... | collective-permute-start | bytes 417800 | tf_op jit(solution)/shard_map/ppermute | solution.py:292
  95.8 8.3 %collective-permute-start.16 = (bf16[256,256]{1,0:T(8,128)(2,1)S(1)}, bf16[256,256]{1,0:T(8,128)(2,1)S(1)}, u32[]{:S(2)}, u32[]{:S(2)}) collective-permute-start(bf16[256,256]{1,0:T(8,128)(2,1)S(1)} %shard_map.84.refs_0_), channel_id=1, source_target_pairs={{0,16},{1,17},{2,18},{3,19},{4,20},{5,21},{6,22},{7,23},{8,24},{9,... | collective-permute-start | bytes 393224 | tf_op jit(solution)/shard_map/ppermute | solution.py:292
  98.4 7.5 %collective-permute-start.17 = (bf16[256,256]{1,0:T(8,128)(2,1)S(1)}, bf16[256,256]{1,0:T(8,128)(2,1)S(1)}, u32[]{:S(2)}, u32[]{:S(2)}) collective-permute-start(bf16[256,256]{1,0:T(8,128)(2,1)S(1)} %shard_map.84.refs_0_), channel_id=1, source_target_pairs={{0,8},{1,9},{2,10},{3,11},{4,12},{5,13},{6,14},{7,15},{8,0},{9,1},... | collective-permute-start | bytes 393224 | tf_op jit(solution)/shard_map/ppermute | solution.py:292
  101.7 7.3 %collective-permute-start.39 = (bf16[256,256]{1,0:T(8,128)(2,1)S(1)}, bf16[256,256]{1,0:T(8,128)(2,1)S(1)}, u32[]{:S(2)}, u32[]{:S(2)}) collective-permute-start(bf16[256,256]{1,0:T(8,128)(2,1)S(1)} %shard_map.96.refs_0_), channel_id=1, source_target_pairs={{0,16},{1,17},{2,18},{3,19},{4,20},{5,21},{6,22},{7,23},{8,24},{9,... | collective-permute-start | bytes 393224 | tf_op jit(solution)/shard_map/ppermute | solution.py:292
  102.2 8.4 %collective-permute-start.40 = (bf16[256,256]{1,0:T(8,128)(2,1)S(1)}, bf16[256,256]{1,0:T(8,128)(2,1)S(1)}, u32[]{:S(2)}, u32[]{:S(2)}) collective-permute-start(bf16[256,256]{1,0:T(8,128)(2,1)S(1)} %shard_map.96.refs_0_), channel_id=1, source_target_pairs={{0,8},{1,9},{2,10},{3,11},{4,12},{5,13},{6,14},{7,15},{8,0},{9,1},... | collective-permute-start | bytes 393224 | tf_op jit(solution)/shard_map/ppermute | solution.py:292
  105.9 7.3 %collective-permute-start.18 = (bf16[256,256]{1,0:T(8,128)(2,1)S(1)}, bf16[256,256]{1,0:T(8,128)(2,1)S(1)}, u32[]{:S(2)}, u32[]{:S(2)}) collective-permute-start(bf16[256,256]{1,0:T(8,128)(2,1)S(1)} %collective-permute-done.16.refs_2_), channel_id=1, source_target_pairs={{0,8},{1,9},{2,10},{3,11},{4,12},{5,13},{6,14},{7,15},{8,0},{9,1},... | collective-permute-start | bytes 393224 | tf_op jit(solution)/shard_map/ppermute | solution.py:292
  110.6 5.4 %collective-permute-start.41 = (bf16[256,256]{1,0:T(8,128)(2,1)S(1)}, bf16[256,256]{1,0:T(8,128)(2,1)S(1)}, u32[]{:S(2)}, u32[]{:S(2)}) collective-permute-start(bf16[256,256]{1,0:T(8,128)(2,1)S(1)} %collective-permute-done.39.refs_2_), channel_id=1, source_target_pairs={{0,8},{1,9},{2,10},{3,11},{4,12},{5,13},{6,14},{7,15},{8,0},{9,1},... | collective-permute-start | bytes 393224 | tf_op jit(solution)/shard_map/ppermute | solution.py:292
  113.3 3.9 %collective-permute-start.42 = (bf16[256,256]{1,0:T(8,128)(2,1)S(1)}, bf16[256,256]{1,0:T(8,128)(2,1)S(1)}, u32[]{:S(2)}, u32[]{:S(2)}) collective-permute-start(bf16[256,256]{1,0:T(8,128)(2,1)S(1)} %get-tuple-element.155), channel_id=1, source_target_pairs={{0,1},{1,0},{2,3},{3,2},{4,5},{5,4},{6,7},{7,6},{8,9},{9,8},{10,11... | collective-permute-start | bytes 393224 | tf_op jit(solution)/shard_map/ppermute | solution.py:292
  113.3 6.4 %collective-permute-start.43 = (bf16[256,256]{1,0:T(8,128)(2,1)S(1)}, bf16[256,256]{1,0:T(8,128)(2,1)S(1)}, u32[]{:S(2)}, u32[]{:S(2)}) collective-permute-start(bf16[256,256]{1,0:T(8,128)(2,1)S(1)} %get-tuple-element.156), channel_id=1, source_target_pairs={{0,2},{1,3},{2,0},{3,1},{4,6},{5,7},{6,4},{7,5},{8,10},{9,11},{10,... | collective-permute-start | bytes 393224 | tf_op jit(solution)/shard_map/ppermute | solution.py:292
  115.0 6.7 %collective-permute-start.44 = (bf16[256,256]{1,0:T(8,128)(2,1)S(1)}, bf16[256,256]{1,0:T(8,128)(2,1)S(1)}, u32[]{:S(2)}, u32[]{:S(2)}) collective-permute-start(bf16[256,256]{1,0:T(8,128)(2,1)S(1)} %get-tuple-element.157), channel_id=1, source_target_pairs={{0,3},{1,2},{2,1},{3,0},{4,7},{5,6},{6,5},{7,4},{8,11},{9,10},{10,... | collective-permute-start | bytes 393224 | tf_op jit(solution)/shard_map/ppermute | solution.py:292
  115.2 9.3 %collective-permute-start.19 = (bf16[256,256]{1,0:T(8,128)(2,1)S(1)}, bf16[256,256]{1,0:T(8,128)(2,1)S(1)}, u32[]{:S(2)}, u32[]{:S(2)}) collective-permute-start(bf16[256,256]{1,0:T(8,128)(2,1)S(1)} %get-tuple-element.154.refs_0_), channel_id=1, source_target_pairs={{0,4},{1,5},{2,6},{3,7},{4,0},{5,1},{6,2},{7,3},{8,12},{9,13},{10,... | collective-permute-start | bytes 393224 | tf_op jit(solution)/shard_map/ppermute | solution.py:292
  116.1 10.0 %collective-permute-start.20 = (bf16[256,256]{1,0:T(8,128)(2,1)S(1)}, bf16[256,256]{1,0:T(8,128)(2,1)S(1)}, u32[]{:S(2)}, u32[]{:S(2)}) collective-permute-start(bf16[256,256]{1,0:T(8,128)(2,1)S(1)} %get-tuple-element.155), channel_id=1, source_target_pairs={{0,5},{1,4},{2,7},{3,6},{4,1},{5,0},{6,3},{7,2},{8,13},{9,12},{10,... | collective-permute-start | bytes 393224 | tf_op jit(solution)/shard_map/ppermute | solution.py:292
  117.2 11.0 %collective-permute-start.21 = (bf16[256,256]{1,0:T(8,128)(2,1)S(1)}, bf16[256,256]{1,0:T(8,128)(2,1)S(1)}, u32[]{:S(2)}, u32[]{:S(2)}) collective-permute-start(bf16[256,256]{1,0:T(8,128)(2,1)S(1)} %get-tuple-element.156), channel_id=1, source_target_pairs={{0,6},{1,7},{2,4},{3,5},{4,2},{5,3},{6,0},{7,1},{8,14},{9,15},{10,... | collective-permute-start | bytes 393224 | tf_op jit(solution)/shard_map/ppermute | solution.py:292
  119.7 10.2 %collective-permute-start.22 = (bf16[256,256]{1,0:T(8,128)(2,1)S(1)}, bf16[256,256]{1,0:T(8,128)(2,1)S(1)}, u32[]{:S(2)}, u32[]{:S(2)}) collective-permute-start(bf16[256,256]{1,0:T(8,128)(2,1)S(1)} %get-tuple-element.157), channel_id=1, source_target_pairs={{0,7},{1,6},{2,5},{3,4},{4,3},{5,2},{6,1},{7,0},{8,15},{9,14},{10,... | collective-permute-start | bytes 393224 | tf_op jit(solution)/shard_map/ppermute | solution.py:292
  122.4 7.9 %collective-permute-start.51 = (bf16[256,256]{1,0:T(8,128)(2,1)S(1)}, bf16[256,256]{1,0:T(8,128)(2,1)S(1)}, u32[]{:S(2)}, u32[]{:S(2)}) collective-permute-start(bf16[256,256]{1,0:T(8,128)(2,1)S(1)} %get-tuple-element.209), channel_id=1, source_target_pairs={{0,1},{1,0},{2,3},{3,2},{4,5},{5,4},{6,7},{7,6},{8,9},{9,8},{10,11... | collective-permute-start | bytes 393224 | tf_op jit(solution)/shard_map/ppermute | solution.py:292
  124.5 8.7 %collective-permute-start.52 = (bf16[256,256]{1,0:T(8,128)(2,1)S(1)}, bf16[256,256]{1,0:T(8,128)(2,1)S(1)}, u32[]{:S(2)}, u32[]{:S(2)}) collective-permute-start(bf16[256,256]{1,0:T(8,128)(2,1)S(1)} %get-tuple-element.210), channel_id=1, source_target_pairs={{0,2},{1,3},{2,0},{3,1},{4,6},{5,7},{6,4},{7,5},{8,10},{9,11},{10,... | collective-permute-start | bytes 393224 | tf_op jit(solution)/shard_map/ppermute | solution.py:292
  126.1 9.8 %collective-permute-start.53 = (bf16[256,256]{1,0:T(8,128)(2,1)S(1)}, bf16[256,256]{1,0:T(8,128)(2,1)S(1)}, u32[]{:S(2)}, u32[]{:S(2)}) collective-permute-start(bf16[256,256]{1,0:T(8,128)(2,1)S(1)} %get-tuple-element.211), channel_id=1, source_target_pairs={{0,3},{1,2},{2,1},{3,0},{4,7},{5,6},{6,5},{7,4},{8,11},{9,10},{10,... | collective-permute-start | bytes 393224 | tf_op jit(solution)/shard_map/ppermute | solution.py:292
  128.2 8.9 %collective-permute-start.48 = (bf16[256,256]{1,0:T(8,128)(2,1)S(1)}, bf16[256,256]{1,0:T(8,128)(2,1)S(1)}, u32[]{:S(2)}, u32[]{:S(2)}) collective-permute-start(bf16[256,256]{1,0:T(8,128)(2,1)S(1)} %get-tuple-element.209), channel_id=1, source_target_pairs={{0,5},{1,4},{2,7},{3,6},{4,1},{5,0},{6,3},{7,2},{8,13},{9,12},{10,... | collective-permute-start | bytes 393224 | tf_op jit(solution)/shard_map/ppermute | solution.py:292
  129.9 7.2 %collective-permute-start.47 = (bf16[256,256]{1,0:T(8,128)(2,1)S(1)}, bf16[256,256]{1,0:T(8,128)(2,1)S(1)}, u32[]{:S(2)}, u32[]{:S(2)}) collective-permute-start(bf16[256,256]{1,0:T(8,128)(2,1)S(1)} %get-tuple-element.208.refs_0_), channel_id=1, source_target_pairs={{0,4},{1,5},{2,6},{3,7},{4,0},{5,1},{6,2},{7,3},{8,12},{9,13},{10,... | collective-permute-start | bytes 393224 | tf_op jit(solution)/shard_map/ppermute | solution.py:292
  130.3 8.7 %collective-permute-start.49 = (bf16[256,256]{1,0:T(8,128)(2,1)S(1)}, bf16[256,256]{1,0:T(8,128)(2,1)S(1)}, u32[]{:S(2)}, u32[]{:S(2)}) collective-permute-start(bf16[256,256]{1,0:T(8,128)(2,1)S(1)} %get-tuple-element.210), channel_id=1, source_target_pairs={{0,6},{1,7},{2,4},{3,5},{4,2},{5,3},{6,0},{7,1},{8,14},{9,15},{10,... | collective-permute-start | bytes 393224 | tf_op jit(solution)/shard_map/ppermute | solution.py:292
  133.3 8.8 %collective-permute-start.50 = (bf16[256,256]{1,0:T(8,128)(2,1)S(1)}, bf16[256,256]{1,0:T(8,128)(2,1)S(1)}, u32[]{:S(2)}, u32[]{:S(2)}) collective-permute-start(bf16[256,256]{1,0:T(8,128)(2,1)S(1)} %get-tuple-element.211), channel_id=1, source_target_pairs={{0,7},{1,6},{2,5},{3,4},{4,3},{5,2},{6,1},{7,0},{8,15},{9,14},{10,... | collective-permute-start | bytes 393224 | tf_op jit(solution)/shard_map/ppermute | solution.py:292
  135.9 8.4 %collective-permute-start.45 = (f32[2,256,256]{2,1,0:T(8,128)S(1)}, f32[2,256,256]{2,1,0:T(8,128)S(1)}, u32[]{:S(2)}, u32[]{:S(2)}) collective-permute-start(f32[2,256,256]{2,1,0:T(8,128)S(1)} %get-tuple-element.205), channel_id=1, source_target_pairs={{0,1},{1,0},{2,3},{3,2},{4,5},{5,4},{6,7},{7,6},{8,9},{9,8},{10,11... | collective-permute-start | bytes 1572872 | tf_op jit(solution)/shard_map/ppermute | solution.py:292
  142.9 3.0 %collective-permute-start.54 = (f32[2,256,256]{2,1,0:T(8,128)S(1)}, f32[2,256,256]{2,1,0:T(8,128)S(1)}, u32[]{:S(2)}, u32[]{:S(2)}) collective-permute-start(f32[2,256,256]{2,1,0:T(8,128)S(1)} %get-tuple-element.214), channel_id=1, source_target_pairs={{0,1},{1,0},{2,3},{3,2},{4,5},{5,4},{6,7},{7,6},{8,9},{9,8},{10,11... | collective-permute-start | bytes 1572872 | tf_op jit(solution)/shard_map/ppermute | solution.py:292
  144.4 6.6 %collective-permute-start.46 = (s16[272,256]{1,0:T(8,128)(2,1)S(1)}, s16[272,256]{1,0:T(8,128)(2,1)S(1)}, u32[]{:S(2)}, u32[]{:S(2)}) collective-permute-start(s16[272,256]{1,0:T(8,128)(2,1)S(1)} %get-tuple-element.207), channel_id=1, source_target_pairs={{0,2},{1,3},{2,0},{3,1},{4,6},{5,7},{6,4},{7,5},{8,10},{9,11},{10,... | collective-permute-start | bytes 417800 | tf_op jit(solution)/shard_map/ppermute | solution.py:292
  146.0 7.1 %collective-permute-start.55 = (s16[272,256]{1,0:T(8,128)(2,1)S(1)}, s16[272,256]{1,0:T(8,128)(2,1)S(1)}, u32[]{:S(2)}, u32[]{:S(2)}) collective-permute-start(s16[272,256]{1,0:T(8,128)(2,1)S(1)} %get-tuple-element.216), channel_id=1, source_target_pairs={{0,2},{1,3},{2,0},{3,1},{4,6},{5,7},{6,4},{7,5},{8,10},{9,11},{10,... | collective-permute-start | bytes 417800 | tf_op jit(solution)/shard_map/ppermute | solution.py:292

commit v3 on v2

--- a/solution.py
+++ b/solution.py
@@ -97,8 +97,10 @@
     total = refs[-1] if steps == (0,) else refs[0]
     weight = 1.0 if len(steps) == 2 else -tile[0].astype(jnp.float32)
 
+    height = matrix.shape[1] if 1 < count <= number + 2 else ROWS
+
     def some_rows(turn, _):
-        rows = pl.ds(pl.multiple_of(turn * ROWS, ROWS), ROWS)
+        rows = pl.ds(pl.multiple_of(turn * height, height), height)
         left = jnp.concatenate([matrix[slot, rows, line] for line in columns for slot in range(slots)], axis=1)
         added = jnp.dot(left, right, preferred_element_type=jnp.float32)
         if not opening:
@@ -106,7 +108,7 @@
         total[rows, :] = added if len(steps) == 2 else weight * added
         return 0
 
-    lax.fori_loop(0, matrix.shape[1] // ROWS, some_rows, 0)
+    lax.fori_loop(0, matrix.shape[1] // height, some_rows, 0)
     if len(steps) == 2:
         refs[1][...] = jnp.zeros_like(refs[1])
         return

time: 154 us -> 154 us (level)
  transfers between devices with their start and end apart: 56 -> 56, of which waited for: 29 -> 28; matrix products, arithmetic and copies ran while one was open for 0% -> 0% of each run, Pallas kernels for 29% -> 29%
where the time goes in v3:
time: 154 us; the launch traced here: 153 us
  starting transfers between devices  56.5 us (37%)
  Pallas kernels  44.3 us (29%)
  waiting for transfers between devices  41.5 us (27%)
  local copies, waits for them, and re-layouts  8.36 us (5%)
    pallas_call x18, Pallas kernels, past_call(): pl.pallas_call(functools.partial(past_kernel, number, carried is None, st...  39.6 us
    ppermute x28, starting transfers between devices, around(): return lax.ppermute(value, 'row', pairs)  29.6 us
    ppermute x28, waiting for transfers between devices, send(): return lax.ppermute(value, BOTH, pairs)  29.2 us
    ppermute x28, starting transfers between devices, send(): return lax.ppermute(value, BOTH, pairs)  26.9 us
    ppermute x28, waiting for transfers between devices, around(): return lax.ppermute(value, 'row', pairs)  12.2 us
    unnamed x12, local copies, waits for them, and re-layouts  6.98 us
    pallas_call x4, Pallas kernels, recent_call(): pl.pallas_call(functools.partial(recent_kernel, fanout, beside, ending, l...  3.25 us
  transfers between devices with their start and end apart: 56, of which 28 were waited for; matrix products, arithmetic and copies ran while one was open for 0% of the time, Pallas kernels for 29%

profile of v3, /device:TPU:0, one launch (start us, length us, event | category | flops | bytes accessed | tf_op | source)
XLA Modules:
  0.0 152.7 jit_solution(7581150013850343730)
XLA Ops:
  0.0 1.3 fusion.1
  1.3 3.1 %collective-permute-start = (bf16[4,128,256]{2,1,0:T(8,128)(2,1)S(1)}, bf16[4,128,256]{2,1,0:T(8,128)(2,1)S(1)}, u32[]{:S(2)}, u32[]{:S(2)}) collective-permute-start(bf16[4,128,256]{2,1,0:T(8,128)(2,1)S(1)} %get-tuple-element.220.front), channel_id=1, source_target_pairs={{0,8},{4,0},{8,16},{12,4},{16,24},{20,12},{24,28},{28,20},{1,9},{5... | collective-permute-start | bytes 786440 | tf_op jit(solution)/shard_map/ppermute | solution.py:305
  4.4 2.0 %collective-permute-start.23 = (bf16[4,128,256]{2,1,0:T(8,128)(2,1)S(1)}, bf16[4,128,256]{2,1,0:T(8,128)(2,1)S(1)}, u32[]{:S(2)}, u32[]{:S(2)}) collective-permute-start(bf16[4,128,256]{2,1,0:T(8,128)(2,1)S(1)} %get-tuple-element.222.front), channel_id=1, source_target_pairs={{0,8},{4,0},{8,16},{12,4},{16,24},{20,12},{24,28},{28,20},{1,9},{5... | collective-permute-start | bytes 786440 | tf_op jit(solution)/shard_map/ppermute | solution.py:305
  6.4 7.0 %copy-done = bf16[5,1024,2048]{2,1,0:T(8,128)(2,1)S(1)} copy-done((bf16[5,1024,2048]{2,1,0:T(8,128)(2,1)S(1)}, bf16[5,1024,2048]{2,1,0:T(8,128)(2,1)}, u32[]{:S(2)}) %copy-start) | copy-done | bytes 20971544
  13.8 2.1 %collective-permute-start.2 = (bf16[4,128,256]{2,1,0:T(8,128)(2,1)S(1)}, bf16[4,128,256]{2,1,0:T(8,128)(2,1)S(1)}, u32[]{:S(2)}, u32[]{:S(2)}) collective-permute-start(bf16[4,128,256]{2,1,0:T(8,128)(2,1)S(1)} %collective-permute-done.front), channel_id=1, source_target_pairs={{0,8},{4,0},{8,16},{12,4},{16,24},{20,12},{24,28},{28,20},{1,9},{5... | collective-permute-start | bytes 786440 | tf_op jit(solution)/shard_map/ppermute | solution.py:305
  16.9 1.6 %collective-permute-done.24.back = bf16[4,128,256]{2,1,0:T(8,128)(2,1)S(1)} collective-permute-done((bf16[4,128,256]{2,1,0:T(8,128)(2,1)S(1)}, bf16[4,128,256]{2,1,0:T(8,128)(2,1)S(1)}, u32[]{:S(2)}, u32[]{:S(2)}) %collective-permute-start.24) | collective-permute-done | bytes 262176 | tf_op jit(solution)/shard_map/ppermute | solution.py:305
  18.6 1.6 %collective-permute-start.25 = (bf16[4,128,256]{2,1,0:T(8,128)(2,1)S(1)}, bf16[4,128,256]{2,1,0:T(8,128)(2,1)S(1)}, u32[]{:S(2)}, u32[]{:S(2)}) collective-permute-start(bf16[4,128,256]{2,1,0:T(8,128)(2,1)S(1)} %collective-permute-done.23.front), channel_id=1, source_target_pairs={{0,8},{4,0},{8,16},{12,4},{16,24},{20,12},{24,28},{28,20},{1,9},{5... | collective-permute-start | bytes 786440 | tf_op jit(solution)/shard_map/ppermute | solution.py:305
  21.3 2.4 %shard_map.74 = (f32[1024,512]{1,0:T(8,128)S(1)}, f32[8,128]{1,0:T(8,128)S(1)}) custom-call(s32[5]{0:T(128)S(1)} %bitcast.34, s32[1]{0:T(128)} %bitcast.8.tile, bf16[5,1024,2048]{2,1,0:T(8,128)(2,1)S(1)} %copy-done.1, bf16[4,128,256]{2,1,0:T(8,128)(2,1)S(1)} %get-tuple-element.220.front, bf16[4,128,256]{2,1,0:T(8,128)(2,1)S(1)} %get-tuple-element.219.back, ...), custom_call_target="tpu_custom_call" | custom-call | flops 1342177280 | bytes 2621440 | tf_op jit(solution)/shard_map/pallas_call | solution.py:147
  23.7 1.4 collective-permute-done.3.back
  25.1 1.6 %collective-permute-start.4 = (bf16[4,128,256]{2,1,0:T(8,128)(2,1)S(1)}, bf16[4,128,256]{2,1,0:T(8,128)(2,1)S(1)}, u32[]{:S(2)}, u32[]{:S(2)}) collective-permute-start(bf16[4,128,256]{2,1,0:T(8,128)(2,1)S(1)} %collective-permute-done.2.front), channel_id=1, source_target_pairs={{0,8},{4,0},{8,16},{12,4},{16,24},{20,12},{24,28},{28,20},{1,9},{5... | collective-permute-start | bytes 786440 | tf_op jit(solution)/shard_map/ppermute | solution.py:305
  27.1 2.4 %shard_map.86 = (f32[1024,512]{1,0:T(8,128)S(1)}, f32[8,128]{1,0:T(8,128)S(1)}) custom-call(s32[5]{0:T(128)S(1)} %bitcast.35, s32[1]{0:T(128)} %bitcast.17.tile, bf16[5,1024,2048]{2,1,0:T(8,128)(2,1)S(1)} %copy-done.1, bf16[4,128,256]{2,1,0:T(8,128)(2,1)S(1)} %get-tuple-element.222.front, bf16[4,128,256]{2,1,0:T(8,128)(2,1)S(1)} %get-tuple-element.221.back, ...), custom_call_target="tpu_custom_call" | custom-call | flops 1342177280 | bytes 2621440 | tf_op jit(solution)/shard_map/pallas_call | solution.py:147
  29.5 1.2 collective-permute-done.26.back
  30.7 1.6 %collective-permute-start.27 = (bf16[4,128,256]{2,1,0:T(8,128)(2,1)S(1)}, bf16[4,128,256]{2,1,0:T(8,128)(2,1)S(1)}, u32[]{:S(2)}, u32[]{:S(2)}) collective-permute-start(bf16[4,128,256]{2,1,0:T(8,128)(2,1)S(1)} %collective-permute-done.25.front), channel_id=1, source_target_pairs={{0,8},{4,0},{8,16},{12,4},{16,24},{20,12},{24,28},{28,20},{1,9},{5... | collective-permute-start | bytes 786440 | tf_op jit(solution)/shard_map/ppermute | solution.py:305
  32.8 2.4 %shard_map.75 = (f32[1024,512]{1,0:T(8,128)S(1)}, f32[8,128]{1,0:T(8,128)S(1)}) custom-call(s32[5]{0:T(128)S(1)} %bitcast.36, s32[1]{0:T(128)} %bitcast.9.tile, bf16[5,1024,2048]{2,1,0:T(8,128)(2,1)S(1)} %copy-done.1, bf16[4,128,256]{2,1,0:T(8,128)(2,1)S(1)} %collective-permute-done.front, ...), custom_call_target="tpu_custom_call", output_to_operand_aliasing={{0}: (6, {})} | custom-call | flops 1342177280 | bytes 2621440 | tf_op jit(solution)/shard_map/pallas_call | solution.py:147
  35.1 2.4 %shard_map.76 = (f32[1024,512]{1,0:T(8,128)S(1)}, f32[8,128]{1,0:T(8,128)S(1)}) custom-call(s32[5]{0:T(128)S(1)} %bitcast.37, s32[1]{0:T(128)} %bitcast.10.tile, bf16[5,1024,2048]{2,1,0:T(8,128)(2,1)S(1)} %copy-done.1, bf16[4,128,256]{2,1,0:T(8,128)(2,1)S(1)} %collective-permute-done.2.front, ...), custom_call_target="tpu_custom_call", output_to_operand_aliasing={{0}: (6, {})} | custom-call | flops 1342177280 | bytes 2621440 | tf_op jit(solution)/shard_map/pallas_call | solution.py:147
  37.6 1.6 %collective-permute-start.6 = (bf16[4,128,256]{2,1,0:T(8,128)(2,1)S(1)}, bf16[4,128,256]{2,1,0:T(8,128)(2,1)S(1)}, u32[]{:S(2)}, u32[]{:S(2)}) collective-permute-start(bf16[4,128,256]{2,1,0:T(8,128)(2,1)S(1)} %collective-permute-done.4.front), channel_id=1, source_target_pairs={{0,8},{4,0},{8,16},{12,4},{16,24},{20,12},{24,28},{28,20},{1,9},{5... | collective-permute-start | bytes 786440 | tf_op jit(solution)/shard_map/ppermute | solution.py:305
  39.7 2.4 %shard_map.87 = (f32[1024,512]{1,0:T(8,128)S(1)}, f32[8,128]{1,0:T(8,128)S(1)}) custom-call(s32[5]{0:T(128)S(1)} %bitcast.38, s32[1]{0:T(128)} %bitcast.18.tile, bf16[5,1024,2048]{2,1,0:T(8,128)(2,1)S(1)} %copy-done.1, bf16[4,128,256]{2,1,0:T(8,128)(2,1)S(1)} %collective-permute-done.23.front, ...), custom_call_target="tpu_custom_call", output_to_operand_aliasing={{0}: (6, {})} | custom-call | flops 1342177280 | bytes 2621440 | tf_op jit(solution)/shard_map/pallas_call | solution.py:147
  42.1 2.4 %shard_map.88 = (f32[1024,512]{1,0:T(8,128)S(1)}, f32[8,128]{1,0:T(8,128)S(1)}) custom-call(s32[5]{0:T(128)S(1)} %bitcast.39, s32[1]{0:T(128)} %bitcast.19.tile, bf16[5,1024,2048]{2,1,0:T(8,128)(2,1)S(1)} %copy-done.1, bf16[4,128,256]{2,1,0:T(8,128)(2,1)S(1)} %collective-permute-done.25.front, ...), custom_call_target="tpu_custom_call", output_to_operand_aliasing={{0}: (6, {})} | custom-call | flops 1342177280 | bytes 2621440 | tf_op jit(solution)/shard_map/pallas_call | solution.py:147
  44.5 1.6 %collective-permute-start.29 = (bf16[4,128,256]{2,1,0:T(8,128)(2,1)S(1)}, bf16[4,128,256]{2,1,0:T(8,128)(2,1)S(1)}, u32[]{:S(2)}, u32[]{:S(2)}) collective-permute-start(bf16[4,128,256]{2,1,0:T(8,128)(2,1)S(1)} %collective-permute-done.27.front), channel_id=1, source_target_pairs={{0,8},{4,0},{8,16},{12,4},{16,24},{20,12},{24,28},{28,20},{1,9},{5... | collective-permute-start | bytes 786440 | tf_op jit(solution)/shard_map/ppermute | solution.py:305
  46.6 2.4 %shard_map.77 = (f32[1024,512]{1,0:T(8,128)S(1)}, f32[8,128]{1,0:T(8,128)S(1)}) custom-call(s32[5]{0:T(128)S(1)} %bitcast.40, s32[1]{0:T(128)} %bitcast.11.tile, bf16[5,1024,2048]{2,1,0:T(8,128)(2,1)S(1)} %copy-done.1, bf16[4,128,256]{2,1,0:T(8,128)(2,1)S(1)} %collective-permute-done.4.front, ...), custom_call_target="tpu_custom_call", output_to_operand_aliasing={{0}: (6, {})} | custom-call | flops 1342177280 | bytes 2621440 | tf_op jit(solution)/shard_map/pallas_call | solution.py:147
  49.0 1.7 %collective-permute-start.8 = (bf16[4,128,256]{2,1,0:T(8,128)(2,1)S(1)}, bf16[4,128,256]{2,1,0:T(8,128)(2,1)S(1)}, u32[]{:S(2)}, u32[]{:S(2)}) collective-permute-start(bf16[4,128,256]{2,1,0:T(8,128)(2,1)S(1)} %collective-permute-done.6.front), channel_id=1, source_target_pairs={{0,8},{4,0},{8,16},{12,4},{16,24},{20,12},{24,28},{28,20},{1,9},{5... | collective-permute-start | bytes 786440 | tf_op jit(solution)/shard_map/ppermute | solution.py:305
  51.1 2.4 %shard_map.89 = (f32[1024,512]{1,0:T(8,128)S(1)}, f32[8,128]{1,0:T(8,128)S(1)}) custom-call(s32[5]{0:T(128)S(1)} %bitcast.41, s32[1]{0:T(128)} %bitcast.20.tile, bf16[5,1024,2048]{2,1,0:T(8,128)(2,1)S(1)} %copy-done.1, bf16[4,128,256]{2,1,0:T(8,128)(2,1)S(1)} %collective-permute-done.27.front, ...), custom_call_target="tpu_custom_call", output_to_operand_aliasing={{0}: (6, {})} | custom-call | flops 1342177280 | bytes 2621440 | tf_op jit(solution)/shard_map/pallas_call | solution.py:147
  53.8 1.6 %collective-permute-done.30.back = bf16[4,128,256]{2,1,0:T(8,128)(2,1)S(1)} collective-permute-done((bf16[4,128,256]{2,1,0:T(8,128)(2,1)S(1)}, bf16[4,128,256]{2,1,0:T(8,128)(2,1)S(1)}, u32[]{:S(2)}, u32[]{:S(2)}) %collective-permute-start.30) | collective-permute-done | bytes 262176 | tf_op jit(solution)/shard_map/ppermute | solution.py:305
  55.4 1.5 collective-permute-start.31
  57.4 2.4 %shard_map.78 = (f32[1024,512]{1,0:T(8,128)S(1)}, f32[8,128]{1,0:T(8,128)S(1)}) custom-call(s32[5]{0:T(128)S(1)} %bitcast.42, s32[1]{0:T(128)} %bitcast.12.tile, bf16[5,1024,2048]{2,1,0:T(8,128)(2,1)S(1)} %copy-done.1, bf16[4,128,256]{2,1,0:T(8,128)(2,1)S(1)} %collective-permute-done.6.front, ...), custom_call_target="tpu_custom_call", output_to_operand_aliasing={{0}: (6, {})} | custom-call | flops 1342177280 | bytes 2621440 | tf_op jit(solution)/shard_map/pallas_call | solution.py:147
  61.0 1.5 collective-permute-start.10
  63.0 2.4 %shard_map.90 = (f32[1024,512]{1,0:T(8,128)S(1)}, f32[8,128]{1,0:T(8,128)S(1)}) custom-call(s32[5]{0:T(128)S(1)} %bitcast.43, s32[1]{0:T(128)} %bitcast.21.tile, bf16[5,1024,2048]{2,1,0:T(8,128)(2,1)S(1)} %copy-done.1, bf16[4,128,256]{2,1,0:T(8,128)(2,1)S(1)} %collective-permute-done.29.front, ...), custom_call_target="tpu_custom_call", output_to_operand_aliasing={{0}: (6, {})} | custom-call | flops 1342177280 | bytes 2621440 | tf_op jit(solution)/shard_map/pallas_call | solution.py:147
  66.6 1.5 collective-permute-start.33
  68.7 2.4 %shard_map.79 = (f32[1024,512]{1,0:T(8,128)S(1)}, f32[8,128]{1,0:T(8,128)S(1)}) custom-call(s32[5]{0:T(128)S(1)} %bitcast.44, s32[1]{0:T(128)} %bitcast.13.tile, bf16[5,1024,2048]{2,1,0:T(8,128)(2,1)S(1)} %copy-done.1, bf16[4,128,256]{2,1,0:T(8,128)(2,1)S(1)} %collective-permute-done.8.front, ...), custom_call_target="tpu_custom_call", output_to_operand_aliasing={{0}: (6, {})} | custom-call | flops 1342177280 | bytes 2621440 | tf_op jit(solution)/shard_map/pallas_call | solution.py:147
  72.2 1.5 collective-permute-start.12
  74.4 2.4 %shard_map.91 = (f32[1024,512]{1,0:T(8,128)S(1)}, f32[8,128]{1,0:T(8,128)S(1)}) custom-call(s32[5]{0:T(128)S(1)} %bitcast.45, s32[1]{0:T(128)} %bitcast.22.tile, bf16[5,1024,2048]{2,1,0:T(8,128)(2,1)S(1)} %copy-done.1, bf16[4,128,256]{2,1,0:T(8,128)(2,1)S(1)} %collective-permute-done.31.front, ...), custom_call_target="tpu_custom_call", output_to_operand_aliasing={{0}: (6, {})} | custom-call | flops 1342177280 | bytes 2621440 | tf_op jit(solution)/shard_map/pallas_call | solution.py:147
  77.9 1.5 collective-permute-start.35
  79.9 2.1 %shard_map.80 = (f32[1024,512]{1,0:T(8,128)S(1)}, f32[8,128]{1,0:T(8,128)S(1)}) custom-call(s32[5]{0:T(128)S(1)} %bitcast.46, s32[1]{0:T(128)} %bitcast.14.tile, bf16[5,1024,2048]{2,1,0:T(8,128)(2,1)S(1)} %copy-done.1, bf16[4,128,256]{2,1,0:T(8,128)(2,1)S(1)} %collective-permute-done.10.front, ...), custom_call_target="tpu_custom_call", output_to_operand_aliasing={{0}: (6, {})} | custom-call | flops 1342177280 | bytes 2621440 | tf_op jit(solution)/shard_map/pallas_call | solution.py:147
  82.4 1.7 %shard_map.81 = (f32[2,256,256]{2,1,0:T(8,128)S(1)}, f32[2,256,256]{2,1,0:T(8,128)S(1)}) custom-call(s32[5]{0:T(128)S(1)} %bitcast.47, s32[1]{0:T(128)} %bitcast.15.tile, bf16[5,1024,2048]{2,1,0:T(8,128)(2,1)S(1)} %copy-done.1, bf16[4,128,256]{2,1,0:T(8,128)(2,1)S(1)} %collective-permute-done.12.front, ...), custom_call_target="tpu_custom_call" | custom-call | flops 671088640 | bytes 2621440 | tf_op jit(solution)/shard_map/pallas_call | solution.py:147
  84.2 2.1 %shard_map.92 = (f32[1024,512]{1,0:T(8,128)S(1)}, f32[8,128]{1,0:T(8,128)S(1)}) custom-call(s32[5]{0:T(128)S(1)} %bitcast.48, s32[1]{0:T(128)} %bitcast.23.tile, bf16[5,1024,2048]{2,1,0:T(8,128)(2,1)S(1)} %copy-done.1, bf16[4,128,256]{2,1,0:T(8,128)(2,1)S(1)} %collective-permute-done.33.front, ...), custom_call_target="tpu_custom_call", output_to_operand_aliasing={{0}: (6, {})} | custom-call | flops 1342177280 | bytes 2621440 | tf_op jit(solution)/shard_map/pallas_call | solution.py:147
  86.4 1.7 %shard_map.93 = (f32[2,256,256]{2,1,0:T(8,128)S(1)}, f32[2,256,256]{2,1,0:T(8,128)S(1)}) custom-call(s32[5]{0:T(128)S(1)} %bitcast.49, s32[1]{0:T(128)} %bitcast.24.tile, bf16[5,1024,2048]{2,1,0:T(8,128)(2,1)S(1)} %copy-done.1, bf16[4,128,256]{2,1,0:T(8,128)(2,1)S(1)} %collective-permute-done.35.front, ...), custom_call_target="tpu_custom_call" | custom-call | flops 671088640 | bytes 2621440 | tf_op jit(solution)/shard_map/pallas_call | solution.py:147
  88.8 1.6 %collective-permute-start.15 = (s16[272,256]{1,0:T(8,128)(2,1)S(1)}, s16[272,256]{1,0:T(8,128)(2,1)S(1)}, u32[]{:S(2)}, u32[]{:S(2)}) collective-permute-start(s16[272,256]{1,0:T(8,128)(2,1)S(1)} %get-tuple-element.147), channel_id=1, source_target_pairs={{0,2},{1,3},{2,0},{3,1},{4,6},{5,7},{6,4},{7,5},{8,10},{9,11},{10,... | collective-permute-start | bytes 417800 | tf_op jit(solution)/shard_map/ppermute | solution.py:294
  90.5 1.4 collective-permute-start.38
  92.0 1.5 %shard_map.83.refs_4_ = f32[1024,256]{1,0:T(8,128)S(1)} custom-call(s32[5]{0:T(128)S(1)} %bitcast.50, s32[1]{0:T(128)} %bitcast.16.tile, bf16[5,1024,2048]{2,1,0:T(8,128)(2,1)S(1)} %copy-done.1, bf16[4,128,256]{2,1,0:T(8,128)(2,1)S(1)} %collective-permute-done.12.front, bf16[4,128,256]{2,1,0:T(8,128)(2,1)S(1)} %collective-permute-done.13.back, ...), custom_call_target="tpu_custom_call" | custom-call | flops 671088640 | bytes 2621440 | tf_op jit(solution)/shard_map/pallas_call | solution.py:147
  93.5 1.9 %collective-permute-done.15.got = s16[272,256]{1,0:T(8,128)(2,1)S(1)} collective-permute-done((s16[272,256]{1,0:T(8,128)(2,1)S(1)}, s16[272,256]{1,0:T(8,128)(2,1)S(1)}, u32[]{:S(2)}, u32[]{:S(2)}) %collective-permute-start.15) | collective-permute-done | bytes 139296 | tf_op jit(solution)/shard_map/ppermute | solution.py:294
  95.5 2.6 %collective-permute-start.16 = (bf16[256,256]{1,0:T(8,128)(2,1)S(1)}, bf16[256,256]{1,0:T(8,128)(2,1)S(1)}, u32[]{:S(2)}, u32[]{:S(2)}) collective-permute-start(bf16[256,256]{1,0:T(8,128)(2,1)S(1)} %shard_map.84.refs_0_), channel_id=1, source_target_pairs={{0,16},{1,17},{2,18},{3,19},{4,20},{5,21},{6,22},{7,23},{8,24},{9,... | collective-permute-start | bytes 393224 | tf_op jit(solution)/shard_map/ppermute | solution.py:294
  98.1 1.5 collective-permute-start.17
  99.6 1.6 %shard_map.95.refs_4_ = f32[1024,256]{1,0:T(8,128)S(1)} custom-call(s32[5]{0:T(128)S(1)} %bitcast.51, s32[1]{0:T(128)} %bitcast.25.tile, bf16[5,1024,2048]{2,1,0:T(8,128)(2,1)S(1)} %copy-done.1, bf16[4,128,256]{2,1,0:T(8,128)(2,1)S(1)} %collective-permute-done.35.front, bf16[4,128,256]{2,1,0:T(8,128)(2,1)S(1)} %collective-permute-done.36.back, ...), custom_call_target="tpu_custom_call" | custom-call | flops 671088640 | bytes 2621440 | tf_op jit(solution)/shard_map/pallas_call | solution.py:147
  102.2 1.6 %collective-permute-done.16.refs_2_ = bf16[256,256]{1,0:T(8,128)(2,1)S(1)} collective-permute-done((bf16[256,256]{1,0:T(8,128)(2,1)S(1)}, bf16[256,256]{1,0:T(8,128)(2,1)S(1)}, u32[]{:S(2)}, u32[]{:S(2)}) %collective-permute-start.16) | collective-permute-done | bytes 131104 | tf_op jit(solution)/shard_map/ppermute | solution.py:294
  103.8 2.6 %collective-permute-done.17.refs_1_ = bf16[256,256]{1,0:T(8,128)(2,1)S(1)} collective-permute-done((bf16[256,256]{1,0:T(8,128)(2,1)S(1)}, bf16[256,256]{1,0:T(8,128)(2,1)S(1)}, u32[]{:S(2)}, u32[]{:S(2)}) %collective-permute-start.17) | collective-permute-done | bytes 131104 | tf_op jit(solution)/shard_map/ppermute | solution.py:294
  107.2 1.4 collective-permute-done.39.refs_2_
  108.6 1.7 %collective-permute-done.40.refs_1_ = bf16[256,256]{1,0:T(8,128)(2,1)S(1)} collective-permute-done((bf16[256,256]{1,0:T(8,128)(2,1)S(1)}, bf16[256,256]{1,0:T(8,128)(2,1)S(1)}, u32[]{:S(2)}, u32[]{:S(2)}) %collective-permute-start.40) | collective-permute-done | bytes 131104 | tf_op jit(solution)/shard_map/ppermute | solution.py:294
  110.3 2.5 %collective-permute-start.41 = (bf16[256,256]{1,0:T(8,128)(2,1)S(1)}, bf16[256,256]{1,0:T(8,128)(2,1)S(1)}, u32[]{:S(2)}, u32[]{:S(2)}) collective-permute-start(bf16[256,256]{1,0:T(8,128)(2,1)S(1)} %collective-permute-done.39.refs_2_), channel_id=1, source_target_pairs={{0,8},{1,9},{2,10},{3,11},{4,12},{5,13},{6,14},{7,15},{8,0},{9,1},... | collective-permute-start | bytes 393224 | tf_op jit(solution)/shard_map/ppermute | solution.py:294
  113.3 1.6 %collective-permute-start.43 = (bf16[256,256]{1,0:T(8,128)(2,1)S(1)}, bf16[256,256]{1,0:T(8,128)(2,1)S(1)}, u32[]{:S(2)}, u32[]{:S(2)}) collective-permute-start(bf16[256,256]{1,0:T(8,128)(2,1)S(1)} %get-tuple-element.156), channel_id=1, source_target_pairs={{0,2},{1,3},{2,0},{3,1},{4,6},{5,7},{6,4},{7,5},{8,10},{9,11},{10,... | collective-permute-start | bytes 393224 | tf_op jit(solution)/shard_map/ppermute | solution.py:294
  117.1 1.6 %collective-permute-start.21 = (bf16[256,256]{1,0:T(8,128)(2,1)S(1)}, bf16[256,256]{1,0:T(8,128)(2,1)S(1)}, u32[]{:S(2)}, u32[]{:S(2)}) collective-permute-start(bf16[256,256]{1,0:T(8,128)(2,1)S(1)} %get-tuple-element.156), channel_id=1, source_target_pairs={{0,6},{1,7},{2,4},{3,5},{4,2},{5,3},{6,0},{7,1},{8,14},{9,15},{10,... | collective-permute-start | bytes 393224 | tf_op jit(solution)/shard_map/ppermute | solution.py:294
  120.0 1.5 %collective-permute-done.44.refs_3_ = bf16[256,256]{1,0:T(8,128)(2,1)S(1)} collective-permute-done((bf16[256,256]{1,0:T(8,128)(2,1)S(1)}, bf16[256,256]{1,0:T(8,128)(2,1)S(1)}, u32[]{:S(2)}, u32[]{:S(2)}) %collective-permute-start.44) | collective-permute-done | bytes 131104 | tf_op jit(solution)/shard_map/ppermute | solution.py:294
  122.4 1.4 collective-permute-start.51
  123.7 1.5 collective-permute-start.52
  125.5 2.6 %collective-permute-done.21.refs_2_ = bf16[256,256]{1,0:T(8,128)(2,1)S(1)} collective-permute-done((bf16[256,256]{1,0:T(8,128)(2,1)S(1)}, bf16[256,256]{1,0:T(8,128)(2,1)S(1)}, u32[]{:S(2)}, u32[]{:S(2)}) %collective-permute-start.21) | collective-permute-done | bytes 131104 | tf_op jit(solution)/shard_map/ppermute | solution.py:294
  128.1 1.7 %collective-permute-done.22.refs_3_ = bf16[256,256]{1,0:T(8,128)(2,1)S(1)} collective-permute-done((bf16[256,256]{1,0:T(8,128)(2,1)S(1)}, bf16[256,256]{1,0:T(8,128)(2,1)S(1)}, u32[]{:S(2)}, u32[]{:S(2)}) %collective-permute-start.22) | collective-permute-done | bytes 131104 | tf_op jit(solution)/shard_map/ppermute | solution.py:294
  130.4 1.4 collective-permute-start.49
  131.8 1.4 collective-permute-done.52.refs_2_
  134.2 1.7 %collective-permute-done.53.refs_3_ = bf16[256,256]{1,0:T(8,128)(2,1)S(1)} collective-permute-done((bf16[256,256]{1,0:T(8,128)(2,1)S(1)}, bf16[256,256]{1,0:T(8,128)(2,1)S(1)}, u32[]{:S(2)}, u32[]{:S(2)}) %collective-permute-start.53) | collective-permute-done | bytes 131104 | tf_op jit(solution)/shard_map/ppermute | solution.py:294
  137.0 1.9 %collective-permute-done.49.refs_2_ = bf16[256,256]{1,0:T(8,128)(2,1)S(1)} collective-permute-done((bf16[256,256]{1,0:T(8,128)(2,1)S(1)}, bf16[256,256]{1,0:T(8,128)(2,1)S(1)}, u32[]{:S(2)}, u32[]{:S(2)}) %collective-permute-start.49) | collective-permute-done | bytes 131104 | tf_op jit(solution)/shard_map/ppermute | solution.py:294
  139.0 2.3 %collective-permute-done.50.refs_3_ = bf16[256,256]{1,0:T(8,128)(2,1)S(1)} collective-permute-done((bf16[256,256]{1,0:T(8,128)(2,1)S(1)}, bf16[256,256]{1,0:T(8,128)(2,1)S(1)}, u32[]{:S(2)}, u32[]{:S(2)}) %collective-permute-start.50) | collective-permute-done | bytes 131104 | tf_op jit(solution)/shard_map/ppermute | solution.py:294
  143.1 1.4 collective-permute-start.46
  144.6 1.5 collective-permute-start.55
  146.1 3.6 %collective-permute-done.46.got = s16[272,256]{1,0:T(8,128)(2,1)S(1)} collective-permute-done((s16[272,256]{1,0:T(8,128)(2,1)S(1)}, s16[272,256]{1,0:T(8,128)(2,1)S(1)}, u32[]{:S(2)}, u32[]{:S(2)}) %collective-permute-start.46) | collective-permute-done | bytes 139296 | tf_op jit(solution)/shard_map/ppermute | solution.py:294
  149.8 2.0 %collective-permute-done.55.got = s16[272,256]{1,0:T(8,128)(2,1)S(1)} collective-permute-done((s16[272,256]{1,0:T(8,128)(2,1)S(1)}, s16[272,256]{1,0:T(8,128)(2,1)S(1)}, u32[]{:S(2)}, u32[]{:S(2)}) %collective-permute-start.55) | collective-permute-done | bytes 139296 | tf_op jit(solution)/shard_map/ppermute | solution.py:294
  (96 shorter events, 25.8 us)
Async XLA Ops:
  0.0 6.4 %copy-start.3 = (f32[1024]{0:T(1024)S(1)}, f32[1024]{0:T(1024)}, u32[]{:S(2)}) copy-start(f32[1024]{0:T(1024)} %param.10) | copy-start | bytes 12292
  0.0 6.4 %copy-start.4 = (f32[1024]{0:T(1024)S(1)}, f32[1024]{0:T(1024)}, u32[]{:S(2)}) copy-start(f32[1024]{0:T(1024)} %param.11) | copy-start | bytes 12292
  1.3 12.5 %collective-permute-start = (bf16[4,128,256]{2,1,0:T(8,128)(2,1)S(1)}, bf16[4,128,256]{2,1,0:T(8,128)(2,1)S(1)}, u32[]{:S(2)}, u32[]{:S(2)}) collective-permute-start(bf16[4,128,256]{2,1,0:T(8,128)(2,1)S(1)} %get-tuple-element.220.front), channel_id=1, source_target_pairs={{0,8},{4,0},{8,16},{12,4},{16,24},{20,12},{24,28},{28,20},{1,9},{5... | collective-permute-start | bytes 786440 | tf_op jit(solution)/shard_map/ppermute | solution.py:305
  4.4 9.4 %collective-permute-start.1 = (bf16[4,128,256]{2,1,0:T(8,128)(2,1)S(1)}, bf16[4,128,256]{2,1,0:T(8,128)(2,1)S(1)}, u32[]{:S(2)}, u32[]{:S(2)}) collective-permute-start(bf16[4,128,256]{2,1,0:T(8,128)(2,1)S(1)} %get-tuple-element.219.back), channel_id=1, source_target_pairs={{0,4},{4,12},{8,0},{12,20},{16,8},{20,28},{24,16},{28,24},{1,5},{5... | collective-permute-start | bytes 786440 | tf_op jit(solution)/shard_map/ppermute | solution.py:305
  4.4 12.6 %collective-permute-start.23 = (bf16[4,128,256]{2,1,0:T(8,128)(2,1)S(1)}, bf16[4,128,256]{2,1,0:T(8,128)(2,1)S(1)}, u32[]{:S(2)}, u32[]{:S(2)}) collective-permute-start(bf16[4,128,256]{2,1,0:T(8,128)(2,1)S(1)} %get-tuple-element.222.front), channel_id=1, source_target_pairs={{0,8},{4,0},{8,16},{12,4},{16,24},{20,12},{24,28},{28,20},{1,9},{5... | collective-permute-start | bytes 786440 | tf_op jit(solution)/shard_map/ppermute | solution.py:305
  6.4 12.2 %collective-permute-start.24 = (bf16[4,128,256]{2,1,0:T(8,128)(2,1)S(1)}, bf16[4,128,256]{2,1,0:T(8,128)(2,1)S(1)}, u32[]{:S(2)}, u32[]{:S(2)}) collective-permute-start(bf16[4,128,256]{2,1,0:T(8,128)(2,1)S(1)} %get-tuple-element.221.back), channel_id=1, source_target_pairs={{0,4},{4,12},{8,0},{12,20},{16,8},{20,28},{24,16},{28,24},{1,5},{5... | collective-permute-start | bytes 786440 | tf_op jit(solution)/shard_map/ppermute | solution.py:305
  6.4 7.0 %copy-start = (bf16[5,1024,2048]{2,1,0:T(8,128)(2,1)S(1)}, bf16[5,1024,2048]{2,1,0:T(8,128)(2,1)}, u32[]{:S(2)}) copy-start(bf16[5,1024,2048]{2,1,0:T(8,128)(2,1)} %matrix.65) | copy-start | bytes 62914564
  13.4 7.9 %copy-start.1 = (bf16[5,1024,2048]{2,1,0:T(8,128)(2,1)S(1)}, bf16[5,1024,2048]{2,1,0:T(8,128)(2,1)}, u32[]{:S(2)}) copy-start(bf16[5,1024,2048]{2,1,0:T(8,128)(2,1)} %matrix.65) | copy-start | bytes 62914564
  13.4 7.9 %copy-start.2 = (s32[1,1,5]{2,1,0:T(1,128)S(1)}, s32[1,1,5]{2,1,0:T(1,128)}, u32[]{:S(2)}) copy-start(s32[1,1,5]{2,1,0:T(1,128)} %param.12) | copy-start | bytes 64
  13.8 9.9 %collective-permute-start.2 = (bf16[4,128,256]{2,1,0:T(8,128)(2,1)S(1)}, bf16[4,128,256]{2,1,0:T(8,128)(2,1)S(1)}, u32[]{:S(2)}, u32[]{:S(2)}) collective-permute-start(bf16[4,128,256]{2,1,0:T(8,128)(2,1)S(1)} %collective-permute-done.front), channel_id=1, source_target_pairs={{0,8},{4,0},{8,16},{12,4},{16,24},{20,12},{24,28},{28,20},{1,9},{5... | collective-permute-start | bytes 786440 | tf_op jit(solution)/shard_map/ppermute | solution.py:305
  15.9 9.2 %collective-permute-start.3 = (bf16[4,128,256]{2,1,0:T(8,128)(2,1)S(1)}, bf16[4,128,256]{2,1,0:T(8,128)(2,1)S(1)}, u32[]{:S(2)}, u32[]{:S(2)}) collective-permute-start(bf16[4,128,256]{2,1,0:T(8,128)(2,1)S(1)} %collective-permute-done.1.back), channel_id=1, source_target_pairs={{0,4},{4,12},{8,0},{12,20},{16,8},{20,28},{24,16},{28,24},{1,5},{5... | collective-permute-start | bytes 786440 | tf_op jit(solution)/shard_map/ppermute | solution.py:305
  18.6 10.9 %collective-permute-start.25 = (bf16[4,128,256]{2,1,0:T(8,128)(2,1)S(1)}, bf16[4,128,256]{2,1,0:T(8,128)(2,1)S(1)}, u32[]{:S(2)}, u32[]{:S(2)}) collective-permute-start(bf16[4,128,256]{2,1,0:T(8,128)(2,1)S(1)} %collective-permute-done.23.front), channel_id=1, source_target_pairs={{0,8},{4,0},{8,16},{12,4},{16,24},{20,12},{24,28},{28,20},{1,9},{5... | collective-permute-start | bytes 786440 | tf_op jit(solution)/shard_map/ppermute | solution.py:305
  20.2 10.6 %collective-permute-start.26 = (bf16[4,128,256]{2,1,0:T(8,128)(2,1)S(1)}, bf16[4,128,256]{2,1,0:T(8,128)(2,1)S(1)}, u32[]{:S(2)}, u32[]{:S(2)}) collective-permute-start(bf16[4,128,256]{2,1,0:T(8,128)(2,1)S(1)} %collective-permute-done.24.back), channel_id=1, source_target_pairs={{0,4},{4,12},{8,0},{12,20},{16,8},{20,28},{24,16},{28,24},{1,5},{5... | collective-permute-start | bytes 786440 | tf_op jit(solution)/shard_map/ppermute | solution.py:305
  25.1 12.5 %collective-permute-start.4 = (bf16[4,128,256]{2,1,0:T(8,128)(2,1)S(1)}, bf16[4,128,256]{2,1,0:T(8,128)(2,1)S(1)}, u32[]{:S(2)}, u32[]{:S(2)}) collective-permute-start(bf16[4,128,256]{2,1,0:T(8,128)(2,1)S(1)} %collective-permute-done.2.front), channel_id=1, source_target_pairs={{0,8},{4,0},{8,16},{12,4},{16,24},{20,12},{24,28},{28,20},{1,9},{5... | collective-permute-start | bytes 786440 | tf_op jit(solution)/shard_map/ppermute | solution.py:305
  26.7 10.9 %collective-permute-start.5 = (bf16[4,128,256]{2,1,0:T(8,128)(2,1)S(1)}, bf16[4,128,256]{2,1,0:T(8,128)(2,1)S(1)}, u32[]{:S(2)}, u32[]{:S(2)}) collective-permute-start(bf16[4,128,256]{2,1,0:T(8,128)(2,1)S(1)} %collective-permute-done.3.back), channel_id=1, source_target_pairs={{0,4},{4,12},{8,0},{12,20},{16,8},{20,28},{24,16},{28,24},{1,5},{5... | collective-permute-start | bytes 786440 | tf_op jit(solution)/shard_map/ppermute | solution.py:305
  30.7 13.8 %collective-permute-start.27 = (bf16[4,128,256]{2,1,0:T(8,128)(2,1)S(1)}, bf16[4,128,256]{2,1,0:T(8,128)(2,1)S(1)}, u32[]{:S(2)}, u32[]{:S(2)}) collective-permute-start(bf16[4,128,256]{2,1,0:T(8,128)(2,1)S(1)} %collective-permute-done.25.front), channel_id=1, source_target_pairs={{0,8},{4,0},{8,16},{12,4},{16,24},{20,12},{24,28},{28,20},{1,9},{5... | collective-permute-start | bytes 786440 | tf_op jit(solution)/shard_map/ppermute | solution.py:305
  32.3 12.2 %collective-permute-start.28 = (bf16[4,128,256]{2,1,0:T(8,128)(2,1)S(1)}, bf16[4,128,256]{2,1,0:T(8,128)(2,1)S(1)}, u32[]{:S(2)}, u32[]{:S(2)}) collective-permute-start(bf16[4,128,256]{2,1,0:T(8,128)(2,1)S(1)} %collective-permute-done.26.back), channel_id=1, source_target_pairs={{0,4},{4,12},{8,0},{12,20},{16,8},{20,28},{24,16},{28,24},{1,5},{5... | collective-permute-start | bytes 786440 | tf_op jit(solution)/shard_map/ppermute | solution.py:305
  37.6 11.4 %collective-permute-start.6 = (bf16[4,128,256]{2,1,0:T(8,128)(2,1)S(1)}, bf16[4,128,256]{2,1,0:T(8,128)(2,1)S(1)}, u32[]{:S(2)}, u32[]{:S(2)}) collective-permute-start(bf16[4,128,256]{2,1,0:T(8,128)(2,1)S(1)} %collective-permute-done.4.front), channel_id=1, source_target_pairs={{0,8},{4,0},{8,16},{12,4},{16,24},{20,12},{24,28},{28,20},{1,9},{5... | collective-permute-start | bytes 786440 | tf_op jit(solution)/shard_map/ppermute | solution.py:305
  39.2 9.8 %collective-permute-start.7 = (bf16[4,128,256]{2,1,0:T(8,128)(2,1)S(1)}, bf16[4,128,256]{2,1,0:T(8,128)(2,1)S(1)}, u32[]{:S(2)}, u32[]{:S(2)}) collective-permute-start(bf16[4,128,256]{2,1,0:T(8,128)(2,1)S(1)} %collective-permute-done.5.back), channel_id=1, source_target_pairs={{0,4},{4,12},{8,0},{12,20},{16,8},{20,28},{24,16},{28,24},{1,5},{5... | collective-permute-start | bytes 786440 | tf_op jit(solution)/shard_map/ppermute | solution.py:305
  44.5 9.3 %collective-permute-start.29 = (bf16[4,128,256]{2,1,0:T(8,128)(2,1)S(1)}, bf16[4,128,256]{2,1,0:T(8,128)(2,1)S(1)}, u32[]{:S(2)}, u32[]{:S(2)}) collective-permute-start(bf16[4,128,256]{2,1,0:T(8,128)(2,1)S(1)} %collective-permute-done.27.front), channel_id=1, source_target_pairs={{0,8},{4,0},{8,16},{12,4},{16,24},{20,12},{24,28},{28,20},{1,9},{5... | collective-permute-start | bytes 786440 | tf_op jit(solution)/shard_map/ppermute | solution.py:305
  46.1 9.2 %collective-permute-start.30 = (bf16[4,128,256]{2,1,0:T(8,128)(2,1)S(1)}, bf16[4,128,256]{2,1,0:T(8,128)(2,1)S(1)}, u32[]{:S(2)}, u32[]{:S(2)}) collective-permute-start(bf16[4,128,256]{2,1,0:T(8,128)(2,1)S(1)} %collective-permute-done.28.back), channel_id=1, source_target_pairs={{0,4},{4,12},{8,0},{12,20},{16,8},{20,28},{24,16},{28,24},{1,5},{5... | collective-permute-start | bytes 786440 | tf_op jit(solution)/shard_map/ppermute | solution.py:305
  49.0 10.8 %collective-permute-start.8 = (bf16[4,128,256]{2,1,0:T(8,128)(2,1)S(1)}, bf16[4,128,256]{2,1,0:T(8,128)(2,1)S(1)}, u32[]{:S(2)}, u32[]{:S(2)}) collective-permute-start(bf16[4,128,256]{2,1,0:T(8,128)(2,1)S(1)} %collective-permute-done.6.front), channel_id=1, source_target_pairs={{0,8},{4,0},{8,16},{12,4},{16,24},{20,12},{24,28},{28,20},{1,9},{5... | collective-permute-start | bytes 786440 | tf_op jit(solution)/shard_map/ppermute | solution.py:305
  50.7 10.4 %collective-permute-start.9 = (bf16[4,128,256]{2,1,0:T(8,128)(2,1)S(1)}, bf16[4,128,256]{2,1,0:T(8,128)(2,1)S(1)}, u32[]{:S(2)}, u32[]{:S(2)}) collective-permute-start(bf16[4,128,256]{2,1,0:T(8,128)(2,1)S(1)} %collective-permute-done.7.back), channel_id=1, source_target_pairs={{0,4},{4,12},{8,0},{12,20},{16,8},{20,28},{24,16},{28,24},{1,5},{5... | collective-permute-start | bytes 786440 | tf_op jit(solution)/shard_map/ppermute | solution.py:305
  55.4 10.1 %collective-permute-start.31 = (bf16[4,128,256]{2,1,0:T(8,128)(2,1)S(1)}, bf16[4,128,256]{2,1,0:T(8,128)(2,1)S(1)}, u32[]{:S(2)}, u32[]{:S(2)}) collective-permute-start(bf16[4,128,256]{2,1,0:T(8,128)(2,1)S(1)} %collective-permute-done.29.front), channel_id=1, source_target_pairs={{0,8},{4,0},{8,16},{12,4},{16,24},{20,12},{24,28},{28,20},{1,9},{5... | collective-permute-start | bytes 786440 | tf_op jit(solution)/shard_map/ppermute | solution.py:305
  56.9 9.8 %collective-permute-start.32 = (bf16[4,128,256]{2,1,0:T(8,128)(2,1)S(1)}, bf16[4,128,256]{2,1,0:T(8,128)(2,1)S(1)}, u32[]{:S(2)}, u32[]{:S(2)}) collective-permute-start(bf16[4,128,256]{2,1,0:T(8,128)(2,1)S(1)} %collective-permute-done.30.back), channel_id=1, source_target_pairs={{0,4},{4,12},{8,0},{12,20},{16,8},{20,28},{24,16},{28,24},{1,5},{5... | collective-permute-start | bytes 786440 | tf_op jit(solution)/shard_map/ppermute | solution.py:305
  61.0 10.0 %collective-permute-start.10 = (bf16[4,128,256]{2,1,0:T(8,128)(2,1)S(1)}, bf16[4,128,256]{2,1,0:T(8,128)(2,1)S(1)}, u32[]{:S(2)}, u32[]{:S(2)}) collective-permute-start(bf16[4,128,256]{2,1,0:T(8,128)(2,1)S(1)} %collective-permute-done.8.front), channel_id=1, source_target_pairs={{0,8},{4,0},{8,16},{12,4},{16,24},{20,12},{24,28},{28,20},{1,9},{5... | collective-permute-start | bytes 786440 | tf_op jit(solution)/shard_map/ppermute | solution.py:305
  62.5 9.8 %collective-permute-start.11 = (bf16[4,128,256]{2,1,0:T(8,128)(2,1)S(1)}, bf16[4,128,256]{2,1,0:T(8,128)(2,1)S(1)}, u32[]{:S(2)}, u32[]{:S(2)}) collective-permute-start(bf16[4,128,256]{2,1,0:T(8,128)(2,1)S(1)} %collective-permute-done.9.back), channel_id=1, source_target_pairs={{0,4},{4,12},{8,0},{12,20},{16,8},{20,28},{24,16},{28,24},{1,5},{5... | collective-permute-start | bytes 786440 | tf_op jit(solution)/shard_map/ppermute | solution.py:305
  66.6 10.1 %collective-permute-start.33 = (bf16[4,128,256]{2,1,0:T(8,128)(2,1)S(1)}, bf16[4,128,256]{2,1,0:T(8,128)(2,1)S(1)}, u32[]{:S(2)}, u32[]{:S(2)}) collective-permute-start(bf16[4,128,256]{2,1,0:T(8,128)(2,1)S(1)} %collective-permute-done.31.front), channel_id=1, source_target_pairs={{0,8},{4,0},{8,16},{12,4},{16,24},{20,12},{24,28},{28,20},{1,9},{5... | collective-permute-start | bytes 786440 | tf_op jit(solution)/shard_map/ppermute | solution.py:305
  68.1 9.8 %collective-permute-start.34 = (bf16[4,128,256]{2,1,0:T(8,128)(2,1)S(1)}, bf16[4,128,256]{2,1,0:T(8,128)(2,1)S(1)}, u32[]{:S(2)}, u32[]{:S(2)}) collective-permute-start(bf16[4,128,256]{2,1,0:T(8,128)(2,1)S(1)} %collective-permute-done.32.back), channel_id=1, source_target_pairs={{0,4},{4,12},{8,0},{12,20},{16,8},{20,28},{24,16},{28,24},{1,5},{5... | collective-permute-start | bytes 786440 | tf_op jit(solution)/shard_map/ppermute | solution.py:305
  68.7 5.6 %copy-start.5 = (f32[2,256,512]{2,1,0:T(8,128)S(1)}, f32[2,256,512]{2,1,0:T(8,128)}, u32[]{:S(2)}) copy-start(f32[2,256,512]{2,1,0:T(8,128)} %param.9) | copy-start | bytes 3145732
  72.2 9.8 %collective-permute-start.12 = (bf16[4,128,256]{2,1,0:T(8,128)(2,1)S(1)}, bf16[4,128,256]{2,1,0:T(8,128)(2,1)S(1)}, u32[]{:S(2)}, u32[]{:S(2)}) collective-permute-start(bf16[4,128,256]{2,1,0:T(8,128)(2,1)S(1)} %collective-permute-done.10.front), channel_id=1, source_target_pairs={{0,8},{4,0},{8,16},{12,4},{16,24},{20,12},{24,28},{28,20},{1,9},{5... | collective-permute-start | bytes 786440 | tf_op jit(solution)/shard_map/ppermute | solution.py:305
  73.7 8.7 %collective-permute-start.13 = (bf16[4,128,256]{2,1,0:T(8,128)(2,1)S(1)}, bf16[4,128,256]{2,1,0:T(8,128)(2,1)S(1)}, u32[]{:S(2)}, u32[]{:S(2)}) collective-permute-start(bf16[4,128,256]{2,1,0:T(8,128)(2,1)S(1)} %collective-permute-done.11.back), channel_id=1, source_target_pairs={{0,4},{4,12},{8,0},{12,20},{16,8},{20,28},{24,16},{28,24},{1,5},{5... | collective-permute-start | bytes 786440 | tf_op jit(solution)/shard_map/ppermute | solution.py:305
  77.9 8.5 %collective-permute-start.35 = (bf16[4,128,256]{2,1,0:T(8,128)(2,1)S(1)}, bf16[4,128,256]{2,1,0:T(8,128)(2,1)S(1)}, u32[]{:S(2)}, u32[]{:S(2)}) collective-permute-start(bf16[4,128,256]{2,1,0:T(8,128)(2,1)S(1)} %collective-permute-done.33.front), channel_id=1, source_target_pairs={{0,8},{4,0},{8,16},{12,4},{16,24},{20,12},{24,28},{28,20},{1,9},{5... | collective-permute-start | bytes 786440 | tf_op jit(solution)/shard_map/ppermute | solution.py:305
  79.3 7.0 %collective-permute-start.36 = (bf16[4,128,256]{2,1,0:T(8,128)(2,1)S(1)}, bf16[4,128,256]{2,1,0:T(8,128)(2,1)S(1)}, u32[]{:S(2)}, u32[]{:S(2)}) collective-permute-start(bf16[4,128,256]{2,1,0:T(8,128)(2,1)S(1)} %collective-permute-done.34.back), channel_id=1, source_target_pairs={{0,4},{4,12},{8,0},{12,20},{16,8},{20,28},{24,16},{28,24},{1,5},{5... | collective-permute-start | bytes 786440 | tf_op jit(solution)/shard_map/ppermute | solution.py:305
  84.1 4.6 %collective-permute-start.14 = (f32[2,256,256]{2,1,0:T(8,128)S(1)}, f32[2,256,256]{2,1,0:T(8,128)S(1)}, u32[]{:S(2)}, u32[]{:S(2)}) collective-permute-start(f32[2,256,256]{2,1,0:T(8,128)S(1)} %get-tuple-element.145), channel_id=1, source_target_pairs={{0,1},{1,0},{2,3},{3,2},{4,5},{5,4},{6,7},{7,6},{8,9},{9,8},{10,11... | collective-permute-start | bytes 1572872 | tf_op jit(solution)/shard_map/ppermute | solution.py:294
  88.1 2.3 %collective-permute-start.37 = (f32[2,256,256]{2,1,0:T(8,128)S(1)}, f32[2,256,256]{2,1,0:T(8,128)S(1)}, u32[]{:S(2)}, u32[]{:S(2)}) collective-permute-start(f32[2,256,256]{2,1,0:T(8,128)S(1)} %get-tuple-element.191), channel_id=1, source_target_pairs={{0,1},{1,0},{2,3},{3,2},{4,5},{5,4},{6,7},{7,6},{8,9},{9,8},{10,11... | collective-permute-start | bytes 1572872 | tf_op jit(solution)/shard_map/ppermute | solution.py:294
  88.8 6.6 %collective-permute-start.15 = (s16[272,256]{1,0:T(8,128)(2,1)S(1)}, s16[272,256]{1,0:T(8,128)(2,1)S(1)}, u32[]{:S(2)}, u32[]{:S(2)}) collective-permute-start(s16[272,256]{1,0:T(8,128)(2,1)S(1)} %get-tuple-element.147), channel_id=1, source_target_pairs={{0,2},{1,3},{2,0},{3,1},{4,6},{5,7},{6,4},{7,5},{8,10},{9,11},{10,... | collective-permute-start | bytes 417800 | tf_op jit(solution)/shard_map/ppermute | solution.py:294
  90.5 10.7 %collective-permute-start.38 = (s16[272,256]{1,0:T(8,128)(2,1)S(1)}, s16[272,256]{1,0:T(8,128)(2,1)S(1)}, u32[]{:S(2)}, u32[]{:S(2)}) collective-permute-start(s16[272,256]{1,0:T(8,128)(2,1)S(1)} %get-tuple-element.193), channel_id=1, source_target_pairs={{0,2},{1,3},{2,0},{3,1},{4,6},{5,7},{6,4},{7,5},{8,10},{9,11},{10,... | collective-permute-start | bytes 417800 | tf_op jit(solution)/shard_map/ppermute | solution.py:294
  95.5 8.3 %collective-permute-start.16 = (bf16[256,256]{1,0:T(8,128)(2,1)S(1)}, bf16[256,256]{1,0:T(8,128)(2,1)S(1)}, u32[]{:S(2)}, u32[]{:S(2)}) collective-permute-start(bf16[256,256]{1,0:T(8,128)(2,1)S(1)} %shard_map.84.refs_0_), channel_id=1, source_target_pairs={{0,16},{1,17},{2,18},{3,19},{4,20},{5,21},{6,22},{7,23},{8,24},{9,... | collective-permute-start | bytes 393224 | tf_op jit(solution)/shard_map/ppermute | solution.py:294
  98.1 8.3 %collective-permute-start.17 = (bf16[256,256]{1,0:T(8,128)(2,1)S(1)}, bf16[256,256]{1,0:T(8,128)(2,1)S(1)}, u32[]{:S(2)}, u32[]{:S(2)}) collective-permute-start(bf16[256,256]{1,0:T(8,128)(2,1)S(1)} %shard_map.84.refs_0_), channel_id=1, source_target_pairs={{0,8},{1,9},{2,10},{3,11},{4,12},{5,13},{6,14},{7,15},{8,0},{9,1},... | collective-permute-start | bytes 393224 | tf_op jit(solution)/shard_map/ppermute | solution.py:294
  101.3 7.3 %collective-permute-start.39 = (bf16[256,256]{1,0:T(8,128)(2,1)S(1)}, bf16[256,256]{1,0:T(8,128)(2,1)S(1)}, u32[]{:S(2)}, u32[]{:S(2)}) collective-permute-start(bf16[256,256]{1,0:T(8,128)(2,1)S(1)} %shard_map.96.refs_0_), channel_id=1, source_target_pairs={{0,16},{1,17},{2,18},{3,19},{4,20},{5,21},{6,22},{7,23},{8,24},{9,... | collective-permute-start | bytes 393224 | tf_op jit(solution)/shard_map/ppermute | solution.py:294
  101.7 8.6 %collective-permute-start.40 = (bf16[256,256]{1,0:T(8,128)(2,1)S(1)}, bf16[256,256]{1,0:T(8,128)(2,1)S(1)}, u32[]{:S(2)}, u32[]{:S(2)}) collective-permute-start(bf16[256,256]{1,0:T(8,128)(2,1)S(1)} %shard_map.96.refs_0_), channel_id=1, source_target_pairs={{0,8},{1,9},{2,10},{3,11},{4,12},{5,13},{6,14},{7,15},{8,0},{9,1},... | collective-permute-start | bytes 393224 | tf_op jit(solution)/shard_map/ppermute | solution.py:294
  106.4 6.7 %collective-permute-start.18 = (bf16[256,256]{1,0:T(8,128)(2,1)S(1)}, bf16[256,256]{1,0:T(8,128)(2,1)S(1)}, u32[]{:S(2)}, u32[]{:S(2)}) collective-permute-start(bf16[256,256]{1,0:T(8,128)(2,1)S(1)} %collective-permute-done.16.refs_2_), channel_id=1, source_target_pairs={{0,8},{1,9},{2,10},{3,11},{4,12},{5,13},{6,14},{7,15},{8,0},{9,1},... | collective-permute-start | bytes 393224 | tf_op jit(solution)/shard_map/ppermute | solution.py:294
  110.3 5.5 %collective-permute-start.41 = (bf16[256,256]{1,0:T(8,128)(2,1)S(1)}, bf16[256,256]{1,0:T(8,128)(2,1)S(1)}, u32[]{:S(2)}, u32[]{:S(2)}) collective-permute-start(bf16[256,256]{1,0:T(8,128)(2,1)S(1)} %collective-permute-done.39.refs_2_), channel_id=1, source_target_pairs={{0,8},{1,9},{2,10},{3,11},{4,12},{5,13},{6,14},{7,15},{8,0},{9,1},... | collective-permute-start | bytes 393224 | tf_op jit(solution)/shard_map/ppermute | solution.py:294
  113.2 3.9 %collective-permute-start.42 = (bf16[256,256]{1,0:T(8,128)(2,1)S(1)}, bf16[256,256]{1,0:T(8,128)(2,1)S(1)}, u32[]{:S(2)}, u32[]{:S(2)}) collective-permute-start(bf16[256,256]{1,0:T(8,128)(2,1)S(1)} %get-tuple-element.155), channel_id=1, source_target_pairs={{0,1},{1,0},{2,3},{3,2},{4,5},{5,4},{6,7},{7,6},{8,9},{9,8},{10,11... | collective-permute-start | bytes 393224 | tf_op jit(solution)/shard_map/ppermute | solution.py:294
  113.3 6.4 %collective-permute-start.43 = (bf16[256,256]{1,0:T(8,128)(2,1)S(1)}, bf16[256,256]{1,0:T(8,128)(2,1)S(1)}, u32[]{:S(2)}, u32[]{:S(2)}) collective-permute-start(bf16[256,256]{1,0:T(8,128)(2,1)S(1)} %get-tuple-element.156), channel_id=1, source_target_pairs={{0,2},{1,3},{2,0},{3,1},{4,6},{5,7},{6,4},{7,5},{8,10},{9,11},{10,... | collective-permute-start | bytes 393224 | tf_op jit(solution)/shard_map/ppermute | solution.py:294
  114.8 6.7 %collective-permute-start.44 = (bf16[256,256]{1,0:T(8,128)(2,1)S(1)}, bf16[256,256]{1,0:T(8,128)(2,1)S(1)}, u32[]{:S(2)}, u32[]{:S(2)}) collective-permute-start(bf16[256,256]{1,0:T(8,128)(2,1)S(1)} %get-tuple-element.157), channel_id=1, source_target_pairs={{0,3},{1,2},{2,1},{3,0},{4,7},{5,6},{6,5},{7,4},{8,11},{9,10},{10,... | collective-permute-start | bytes 393224 | tf_op jit(solution)/shard_map/ppermute | solution.py:294
  115.1 8.6 %collective-permute-start.19 = (bf16[256,256]{1,0:T(8,128)(2,1)S(1)}, bf16[256,256]{1,0:T(8,128)(2,1)S(1)}, u32[]{:S(2)}, u32[]{:S(2)}) collective-permute-start(bf16[256,256]{1,0:T(8,128)(2,1)S(1)} %get-tuple-element.154.refs_0_), channel_id=1, source_target_pairs={{0,4},{1,5},{2,6},{3,7},{4,0},{5,1},{6,2},{7,3},{8,12},{9,13},{10,... | collective-permute-start | bytes 393224 | tf_op jit(solution)/shard_map/ppermute | solution.py:294
  115.8 9.4 %collective-permute-start.20 = (bf16[256,256]{1,0:T(8,128)(2,1)S(1)}, bf16[256,256]{1,0:T(8,128)(2,1)S(1)}, u32[]{:S(2)}, u32[]{:S(2)}) collective-permute-start(bf16[256,256]{1,0:T(8,128)(2,1)S(1)} %get-tuple-element.155), channel_id=1, source_target_pairs={{0,5},{1,4},{2,7},{3,6},{4,1},{5,0},{6,3},{7,2},{8,13},{9,12},{10,... | collective-permute-start | bytes 393224 | tf_op jit(solution)/shard_map/ppermute | solution.py:294
  117.1 11.0 %collective-permute-start.21 = (bf16[256,256]{1,0:T(8,128)(2,1)S(1)}, bf16[256,256]{1,0:T(8,128)(2,1)S(1)}, u32[]{:S(2)}, u32[]{:S(2)}) collective-permute-start(bf16[256,256]{1,0:T(8,128)(2,1)S(1)} %get-tuple-element.156), channel_id=1, source_target_pairs={{0,6},{1,7},{2,4},{3,5},{4,2},{5,3},{6,0},{7,1},{8,14},{9,15},{10,... | collective-permute-start | bytes 393224 | tf_op jit(solution)/shard_map/ppermute | solution.py:294
  119.6 10.1 %collective-permute-start.22 = (bf16[256,256]{1,0:T(8,128)(2,1)S(1)}, bf16[256,256]{1,0:T(8,128)(2,1)S(1)}, u32[]{:S(2)}, u32[]{:S(2)}) collective-permute-start(bf16[256,256]{1,0:T(8,128)(2,1)S(1)} %get-tuple-element.157), channel_id=1, source_target_pairs={{0,7},{1,6},{2,5},{3,4},{4,3},{5,2},{6,1},{7,0},{8,15},{9,14},{10,... | collective-permute-start | bytes 393224 | tf_op jit(solution)/shard_map/ppermute | solution.py:294
  122.4 8.0 %collective-permute-start.51 = (bf16[256,256]{1,0:T(8,128)(2,1)S(1)}, bf16[256,256]{1,0:T(8,128)(2,1)S(1)}, u32[]{:S(2)}, u32[]{:S(2)}) collective-permute-start(bf16[256,256]{1,0:T(8,128)(2,1)S(1)} %get-tuple-element.209), channel_id=1, source_target_pairs={{0,1},{1,0},{2,3},{3,2},{4,5},{5,4},{6,7},{7,6},{8,9},{9,8},{10,11... | collective-permute-start | bytes 393224 | tf_op jit(solution)/shard_map/ppermute | solution.py:294
  123.7 9.4 %collective-permute-start.52 = (bf16[256,256]{1,0:T(8,128)(2,1)S(1)}, bf16[256,256]{1,0:T(8,128)(2,1)S(1)}, u32[]{:S(2)}, u32[]{:S(2)}) collective-permute-start(bf16[256,256]{1,0:T(8,128)(2,1)S(1)} %get-tuple-element.210), channel_id=1, source_target_pairs={{0,2},{1,3},{2,0},{3,1},{4,6},{5,7},{6,4},{7,5},{8,10},{9,11},{10,... | collective-permute-start | bytes 393224 | tf_op jit(solution)/shard_map/ppermute | solution.py:294
  125.2 10.7 %collective-permute-start.53 = (bf16[256,256]{1,0:T(8,128)(2,1)S(1)}, bf16[256,256]{1,0:T(8,128)(2,1)S(1)}, u32[]{:S(2)}, u32[]{:S(2)}) collective-permute-start(bf16[256,256]{1,0:T(8,128)(2,1)S(1)} %get-tuple-element.211), channel_id=1, source_target_pairs={{0,3},{1,2},{2,1},{3,0},{4,7},{5,6},{6,5},{7,4},{8,11},{9,10},{10,... | collective-permute-start | bytes 393224 | tf_op jit(solution)/shard_map/ppermute | solution.py:294
  128.1 8.9 %collective-permute-start.48 = (bf16[256,256]{1,0:T(8,128)(2,1)S(1)}, bf16[256,256]{1,0:T(8,128)(2,1)S(1)}, u32[]{:S(2)}, u32[]{:S(2)}) collective-permute-start(bf16[256,256]{1,0:T(8,128)(2,1)S(1)} %get-tuple-element.209), channel_id=1, source_target_pairs={{0,5},{1,4},{2,7},{3,6},{4,1},{5,0},{6,3},{7,2},{8,13},{9,12},{10,... | collective-permute-start | bytes 393224 | tf_op jit(solution)/shard_map/ppermute | solution.py:294
  129.8 7.3 %collective-permute-start.47 = (bf16[256,256]{1,0:T(8,128)(2,1)S(1)}, bf16[256,256]{1,0:T(8,128)(2,1)S(1)}, u32[]{:S(2)}, u32[]{:S(2)}) collective-permute-start(bf16[256,256]{1,0:T(8,128)(2,1)S(1)} %get-tuple-element.208.refs_0_), channel_id=1, source_target_pairs={{0,4},{1,5},{2,6},{3,7},{4,0},{5,1},{6,2},{7,3},{8,12},{9,13},{10,... | collective-permute-start | bytes 393224 | tf_op jit(solution)/shard_map/ppermute | solution.py:294
  130.4 8.6 %collective-permute-start.49 = (bf16[256,256]{1,0:T(8,128)(2,1)S(1)}, bf16[256,256]{1,0:T(8,128)(2,1)S(1)}, u32[]{:S(2)}, u32[]{:S(2)}) collective-permute-start(bf16[256,256]{1,0:T(8,128)(2,1)S(1)} %get-tuple-element.210), channel_id=1, source_target_pairs={{0,6},{1,7},{2,4},{3,5},{4,2},{5,3},{6,0},{7,1},{8,14},{9,15},{10,... | collective-permute-start | bytes 393224 | tf_op jit(solution)/shard_map/ppermute | solution.py:294
  133.1 8.1 %collective-permute-start.50 = (bf16[256,256]{1,0:T(8,128)(2,1)S(1)}, bf16[256,256]{1,0:T(8,128)(2,1)S(1)}, u32[]{:S(2)}, u32[]{:S(2)}) collective-permute-start(bf16[256,256]{1,0:T(8,128)(2,1)S(1)} %get-tuple-element.211), channel_id=1, source_target_pairs={{0,7},{1,6},{2,5},{3,4},{4,3},{5,2},{6,1},{7,0},{8,15},{9,14},{10,... | collective-permute-start | bytes 393224 | tf_op jit(solution)/shard_map/ppermute | solution.py:294
  135.9 7.1 %collective-permute-start.45 = (f32[2,256,256]{2,1,0:T(8,128)S(1)}, f32[2,256,256]{2,1,0:T(8,128)S(1)}, u32[]{:S(2)}, u32[]{:S(2)}) collective-permute-start(f32[2,256,256]{2,1,0:T(8,128)S(1)} %get-tuple-element.205), channel_id=1, source_target_pairs={{0,1},{1,0},{2,3},{3,2},{4,5},{5,4},{6,7},{7,6},{8,9},{9,8},{10,11... | collective-permute-start | bytes 1572872 | tf_op jit(solution)/shard_map/ppermute | solution.py:294
  142.1 2.4 %collective-permute-start.54 = (f32[2,256,256]{2,1,0:T(8,128)S(1)}, f32[2,256,256]{2,1,0:T(8,128)S(1)}, u32[]{:S(2)}, u32[]{:S(2)}) collective-permute-start(f32[2,256,256]{2,1,0:T(8,128)S(1)} %get-tuple-element.214), channel_id=1, source_target_pairs={{0,1},{1,0},{2,3},{3,2},{4,5},{5,4},{6,7},{7,6},{8,9},{9,8},{10,11... | collective-permute-start | bytes 1572872 | tf_op jit(solution)/shard_map/ppermute | solution.py:294
  143.1 6.6 %collective-permute-start.46 = (s16[272,256]{1,0:T(8,128)(2,1)S(1)}, s16[272,256]{1,0:T(8,128)(2,1)S(1)}, u32[]{:S(2)}, u32[]{:S(2)}) collective-permute-start(s16[272,256]{1,0:T(8,128)(2,1)S(1)} %get-tuple-element.207), channel_id=1, source_target_pairs={{0,2},{1,3},{2,0},{3,1},{4,6},{5,7},{6,4},{7,5},{8,10},{9,11},{10,... | collective-permute-start | bytes 417800 | tf_op jit(solution)/shard_map/ppermute | solution.py:294
  144.6 7.1 %collective-permute-start.55 = (s16[272,256]{1,0:T(8,128)(2,1)S(1)}, s16[272,256]{1,0:T(8,128)(2,1)S(1)}, u32[]{:S(2)}, u32[]{:S(2)}) collective-permute-start(s16[272,256]{1,0:T(8,128)(2,1)S(1)} %get-tuple-element.216), channel_id=1, source_target_pairs={{0,2},{1,3},{2,0},{3,1},{4,6},{5,7},{6,4},{7,5},{8,10},{9,11},{10,... | collective-permute-start | bytes 417800 | tf_op jit(solution)/shard_map/ppermute | solution.py:294
